TPU v7x, 256 devices: a whole 4x4x8 slice. The times are simulated.
256 devices in a mesh: section: 8 (over z), expert: 32 (over y, x, core).
Axes of the slice: x: 4, y: 4, z: 8, core: 2. Of those that a mesh axis runs over, the one named last changes fastest.
Arguments:
- x_saved: bfloat16 [8, 8, 512, 2560], P('section', None, 'expert'), may hold values from -6 to 6
- routes: int32 [8, 8, 512, 2], P('section', None, 'expert'), may hold values from 0 to 15, all different within a row; in each aligned block of 16 rows (0 to 15, 16 to 31, ..., all dimensions but the last counted through in order) at most 3 rows name the same one
- gates: float32 [8, 8, 512, 2], P('section', None, 'expert'), may hold values from 0.1 to 0.6
- cotangent: bfloat16 [8, 512, 2560], P(None, 'expert', 'section'), may hold values from -6 to 6
- w_gate: bfloat16 [8, 12288, 2560], P('section', 'expert'), may hold values from -0.125 to 0.125
- w_up: bfloat16 [8, 12288, 2560], P('section', 'expert'), may hold values from -0.125 to 0.125
- w_down: bfloat16 [8, 12288, 2560], P('section', 'expert'), may hold values from -0.21875 to 0.21875
Outputs:
- grad_inputs: bfloat16 [8, 8, 512, 2560], P('section', None, 'expert')
- grad_gate: bfloat16 [8, 12288, 2560], P('section', 'expert')
- grad_up: bfloat16 [8, 12288, 2560], P('section', 'expert')
- grad_down: bfloat16 [8, 12288, 2560], P('section', 'expert')
Inputs may be any that keep to these rules, and one draw needn't show every extreme that they name: `routes`: each token names 2 different experts. In each aligned block of 16 tokens (one device's tokens of one section and micro-batch), no expert is named by more than 3 tokens, and in some blocks one is named by exactly 3.
All inputs are finite; a program needn't handle non-finite values.
Results may differ from a plain program's by a relative error of at most 0.025.
Values may be sent and summed in bfloat16 or wider, within the bound.
No kernel may reach another device: no remote copies, remote signals or barrier semaphores. Data moves between devices by JAX's collectives and lax.ppermute only.
A program may use at most 128 MiB of HBM per device.

v0:
```python
from functools import partial

import jax
import jax.numpy as jnp
from jax import lax
from jax.sharding import PartitionSpec as P

SPLIT = 2


CONTRACT_ROWS = (((0,), (0,)), ((), ()))
CONTRACT_COLS = (((1,), (1,)), ((), ()))


def passed_along(value, axis, steps):
    count = lax.axis_size(axis)
    first, last = (max(0, -steps), min(count, count - steps))
    return lax.ppermute(value, axis, [(source, source + steps) for source in range(first, last)])


def swish_parts(pre_gate):
    sigmoid = jax.nn.sigmoid(pre_gate)
    return (pre_gate * sigmoid, sigmoid * (1.0 + pre_gate * (1.0 - sigmoid)))


def slot_index(route_rows, experts, capacity):
    route_hot = (route_rows[:, None] == jnp.arange(experts, dtype=jnp.int32)[None, :]).astype(
        jnp.int32
    )
    earlier = jnp.cumsum(route_hot, axis=0) - route_hot
    return route_rows * capacity + jnp.sum(earlier * route_hot, axis=1)


def spread(slot_rows, experts, capacity):
    leading = slot_rows.shape[:-2]
    features = slot_rows.shape[-1]
    shaped = slot_rows.reshape(leading + (experts, 1, capacity, features))
    widened = jnp.broadcast_to(shaped, leading + (experts, SPLIT, capacity, features))
    return widened.reshape(leading + (experts * SPLIT, capacity, features))


def forward_parts(rows_in, gate_rows, up_rows):
    pre_gate = lax.dot_general(
        rows_in, gate_rows, CONTRACT_COLS, preferred_element_type=jnp.float32
    )
    pre_up = lax.dot_general(rows_in, up_rows, CONTRACT_COLS, preferred_element_type=jnp.float32)
    return (pre_gate, pre_up)


def backward_rows(rows_grad, pre_gate, pre_up, gate_rows, up_rows, down_rows):
    swished, slope_act = swish_parts(pre_gate)
    hidden_act = (swished * pre_up).astype(jnp.bfloat16)
    d_hidden = lax.dot_general(
        rows_grad, down_rows, CONTRACT_COLS, preferred_element_type=jnp.float32
    )
    d_gate = (d_hidden * pre_up * slope_act).astype(jnp.bfloat16)
    d_up = (d_hidden * swished).astype(jnp.bfloat16)
    slice_part = jnp.dot(d_gate, gate_rows, preferred_element_type=jnp.float32)
    slice_part = slice_part + jnp.dot(d_up, up_rows, preferred_element_type=jnp.float32)
    return (slice_part.astype(jnp.bfloat16), hidden_act, d_gate, d_up)


def weight_terms(rows_in, rows_grad, hidden_act, d_gate, d_up):
    return (
        lax.dot_general(d_gate, rows_in, CONTRACT_ROWS, preferred_element_type=jnp.float32),
        lax.dot_general(d_up, rows_in, CONTRACT_ROWS, preferred_element_type=jnp.float32),
        lax.dot_general(hidden_act, rows_grad, CONTRACT_ROWS, preferred_element_type=jnp.float32),
    )


def on_device(x_saved, routes, gates, cotangent, w_gate, w_up, w_down):
    sections = lax.axis_size("section")
    devices_wide = lax.axis_size("expert")
    section_index = lax.axis_index("section")
    experts = devices_wide // SPLIT
    batches = x_saved.shape[1]
    tokens_dev = x_saved.shape[2]
    model_width = x_saved.shape[3]
    top_count = routes.shape[3]
    capacity = max(2, 3 * tokens_dev * top_count // (2 * experts))
    slot_count = experts * capacity
    rows_total = devices_wide * capacity
    gate_rows = w_gate[0]
    up_rows = w_up[0]
    down_rows = w_down[0]
    hidden_dev = gate_rows.shape[0]
    route_flat = routes[0].reshape(batches, tokens_dev * top_count)
    slot_table = jax.vmap(partial(slot_index, experts=experts, capacity=capacity))(route_flat)
    placing = (
        jnp.arange(slot_count, dtype=jnp.int32)[None, :, None] == slot_table[:, None, :]
    ).astype(jnp.bfloat16)
    input_repeat = jnp.repeat(x_saved[0], top_count, axis=1)
    input_slots = jnp.einsum(
        "bsr,brd->bsd", placing, input_repeat, preferred_element_type=jnp.float32
    ).astype(jnp.bfloat16)
    top_grads = lax.all_gather(cotangent, "section", axis=2, tiled=True)
    saved_state = tuple((jnp.zeros((hidden_dev, model_width), jnp.float32) for unused in range(3)))

    def clock_tick(tick_index, carried):
        arriving, results, saved_state = carried
        micro_batch = tick_index - (sections - 1 - section_index)
        active = jnp.logical_and(micro_batch >= 0, micro_batch < batches)
        chosen = jnp.clip(micro_batch, 0, batches - 1)
        upstream = jnp.where(section_index == sections - 1, top_grads[chosen], arriving)
        scaled = jnp.repeat(upstream, top_count, axis=0).astype(jnp.float32) * gates[
            0, chosen
        ].reshape(-1, 1)
        grad_slots = jnp.dot(
            placing[chosen], scaled.astype(jnp.bfloat16), preferred_element_type=jnp.float32
        ).astype(jnp.bfloat16)
        rows_in, rows_grad = (
            lax.all_to_all(
                spread(input_slots[chosen], experts, capacity),
                "expert",
                split_axis=0,
                concat_axis=0,
                tiled=True,
            ),
            lax.all_to_all(
                spread(grad_slots, experts, capacity),
                "expert",
                split_axis=0,
                concat_axis=0,
                tiled=True,
            ),
        )
        rows_in = rows_in.reshape(rows_total, model_width)
        rows_grad = rows_grad.reshape(rows_total, model_width)

        def section_work(saved_state):
            pre_gate, pre_up = forward_parts(rows_in, gate_rows, up_rows)
            slice_part, hidden_act, d_gate, d_up = backward_rows(
                rows_grad, pre_gate, pre_up, gate_rows, up_rows, down_rows
            )
            saved_state = jax.tree.map(
                jnp.add, saved_state, weight_terms(rows_in, rows_grad, hidden_act, d_gate, d_up)
            )
            return (slice_part, saved_state)

        def skipped(saved_state):
            return (jnp.zeros((rows_total, model_width), jnp.bfloat16), saved_state)

        slice_part, saved_state = lax.cond(active, section_work, skipped, saved_state)
        returned = lax.all_to_all(
            slice_part.reshape(devices_wide, capacity, model_width),
            "expert",
            split_axis=0,
            concat_axis=0,
            tiled=True,
        )
        summed = jnp.sum(
            returned.reshape(experts, SPLIT, capacity, model_width).astype(jnp.float32), axis=1
        )
        picked = jnp.take(summed.reshape(slot_count, model_width), slot_table[chosen], axis=0)
        outgoing = (
            upstream.astype(jnp.float32)
            + jnp.sum(picked.reshape(tokens_dev, top_count, model_width), axis=1)
        ).astype(jnp.bfloat16)
        written = jnp.where(active, outgoing, results[chosen])
        results = lax.dynamic_update_index_in_dim(results, written, chosen, 0)
        arriving = passed_along(outgoing, "section", -1)
        return (arriving, results, saved_state)

    initial = (
        jnp.zeros((tokens_dev, model_width), jnp.bfloat16),
        jnp.zeros((batches, tokens_dev, model_width), jnp.bfloat16),
        saved_state,
    )
    arriving, results, saved_state = lax.fori_loop(0, sections + batches - 1, clock_tick, initial)
    grad_gate, grad_up, grad_down = [
        (running_sum / batches).astype(jnp.bfloat16)[None] for running_sum in saved_state
    ]
    return (results[None], grad_gate, grad_up, grad_down)


def solution(mesh):
    in_specs = (
        P("section", None, "expert", None),
        P("section", None, "expert", None),
        P("section", None, "expert", None),
        P(None, "expert", "section"),
        P("section", "expert", None),
        P("section", "expert", None),
        P("section", "expert", None),
    )
    out_specs = (
        P("section", None, "expert", None),
        P("section", "expert", None),
        P("section", "expert", None),
        P("section", "expert", None),
    )
    return jax.shard_map(
        on_device, mesh=mesh, in_specs=in_specs, out_specs=out_specs, check_vma=False
    )
```

profile of v0, /device:TPU:1, one launch (start us, length us, event | category | flops | bytes accessed | tf_op | source)
XLA Modules:
  0.0 1393.8 jit_solution(9695624659455525608)
XLA Ops:
  7.8 57.3 %all_gather.3 = bf16[8,16,2560]{1,0,2:T(8,128)(2,1)} all-gather(bf16[8,16,320]{1,0,2:T(8,128)(2,1)S(1)} %copy.21), channel_id=1, replica_groups=mesh['section'=8,'expert'=32] {'section'}, dimensions={2}, use_global_device_ids=true | all-gather | bytes 737280 | tf_op jit(solution)/shard_map/all_gather | solution.py:96
  78.7 1307.4 %while.23 = (s32[]{:T(128)}, bf16[16,2560]{1,0:T(8,128)(2,1)S(1)}, bf16[8,16,2560]{2,1,0:T(8,128)(2,1)}, f32[384,2560]{1,0:T(8,128)}, f32[384,2560]{1,0:T(8,128)...) while((s32[]{:T(128)}, bf16[16,2560]{1,0:T(8,128)(2,1)S(1)}, ...), condition=%wide.region_7.8_spmd, body=%wide.region_2.7_spmd.sunk | while | flops 1522939136 | bytes 161909296 | solution.py:169
  109.5 12.9 all-to-all-done.1
  177.9 12.9 all-to-all-done.1
  246.3 12.9 all-to-all-done.1
  314.7 12.9 all-to-all-done.1
  383.1 12.9 all-to-all-done.1
  451.5 12.9 all-to-all-done.1
  521.0 12.9 all-to-all-done.1
  558.0 126.3 %collective-permute-done = bf16[16,2560]{1,0:T(8,128)(2,1)S(1)} collective-permute-done((bf16[16,2560]{1,0:T(8,128)(2,1)S(1)}, bf16[16,2560]{1,0:T(8,128)(2,1)S(1)}, u32[]{:S(2)}, u32[]{:S(2)}) %collective-permute-start) | collective-permute-done | bytes 81952 | tf_op jit(solution)/shard_map/while/body/eval_jaxpr/ppermute | solution.py:18
  711.2 12.9 all-to-all-done.1
  724.1 19.1 %conditional.2 = (bf16[96,2560]{1,0:T(8,128)(2,1)}, f32[384,2560]{1,0:T(8,128)}, f32[384,2560]{1,0:T(8,128)}, f32[384,2560]{1,0:T(8,128)}) conditional(s32[]{:T(128)} %convert_element_type.144, (f32[384,2560]{1,0:T(8,128)}, f32[384,2560]{1,0:T(8,128)}, f32[384,2560]{1,0:T(8,128)}) %tuple.56, (bf16[32,3,2560]{2,1,0:T(4,128)(2,1)S(1)}, ...), branch_computations={%region_3.3_spmd, %region_4.4_spmd} | conditional | flops 1514090496 | bytes 146325760 | solution.py:143
  799.2 12.9 all-to-all-done.1
  812.1 19.1 %conditional.2 = (bf16[96,2560]{1,0:T(8,128)(2,1)}, f32[384,2560]{1,0:T(8,128)}, f32[384,2560]{1,0:T(8,128)}, f32[384,2560]{1,0:T(8,128)}) conditional(s32[]{:T(128)} %convert_element_type.144, (f32[384,2560]{1,0:T(8,128)}, f32[384,2560]{1,0:T(8,128)}, f32[384,2560]{1,0:T(8,128)}) %tuple.56, (bf16[32,3,2560]{2,1,0:T(4,128)(2,1)S(1)}, ...), branch_computations={%region_3.3_spmd, %region_4.4_spmd} | conditional | flops 1514090496 | bytes 146325760 | solution.py:143
  887.1 12.9 all-to-all-done.1
  900.0 19.1 %conditional.2 = (bf16[96,2560]{1,0:T(8,128)(2,1)}, f32[384,2560]{1,0:T(8,128)}, f32[384,2560]{1,0:T(8,128)}, f32[384,2560]{1,0:T(8,128)}) conditional(s32[]{:T(128)} %convert_element_type.144, (f32[384,2560]{1,0:T(8,128)}, f32[384,2560]{1,0:T(8,128)}, f32[384,2560]{1,0:T(8,128)}) %tuple.56, (bf16[32,3,2560]{2,1,0:T(4,128)(2,1)S(1)}, ...), branch_computations={%region_3.3_spmd, %region_4.4_spmd} | conditional | flops 1514090496 | bytes 146325760 | solution.py:143
  988.0 19.1 %conditional.2 = (bf16[96,2560]{1,0:T(8,128)(2,1)}, f32[384,2560]{1,0:T(8,128)}, f32[384,2560]{1,0:T(8,128)}, f32[384,2560]{1,0:T(8,128)}) conditional(s32[]{:T(128)} %convert_element_type.144, (f32[384,2560]{1,0:T(8,128)}, f32[384,2560]{1,0:T(8,128)}, f32[384,2560]{1,0:T(8,128)}) %tuple.56, (bf16[32,3,2560]{2,1,0:T(4,128)(2,1)S(1)}, ...), branch_computations={%region_3.3_spmd, %region_4.4_spmd} | conditional | flops 1514090496 | bytes 146325760 | solution.py:143
  1063.0 12.9 all-to-all-done.1
  1075.9 19.1 %conditional.2 = (bf16[96,2560]{1,0:T(8,128)(2,1)}, f32[384,2560]{1,0:T(8,128)}, f32[384,2560]{1,0:T(8,128)}, f32[384,2560]{1,0:T(8,128)}) conditional(s32[]{:T(128)} %convert_element_type.144, (f32[384,2560]{1,0:T(8,128)}, f32[384,2560]{1,0:T(8,128)}, f32[384,2560]{1,0:T(8,128)}) %tuple.56, (bf16[32,3,2560]{2,1,0:T(4,128)(2,1)S(1)}, ...), branch_computations={%region_3.3_spmd, %region_4.4_spmd} | conditional | flops 1514090496 | bytes 146325760 | solution.py:143
  1151.0 12.9 all-to-all-done.1
  1163.9 19.1 %conditional.2 = (bf16[96,2560]{1,0:T(8,128)(2,1)}, f32[384,2560]{1,0:T(8,128)}, f32[384,2560]{1,0:T(8,128)}, f32[384,2560]{1,0:T(8,128)}) conditional(s32[]{:T(128)} %convert_element_type.144, (f32[384,2560]{1,0:T(8,128)}, f32[384,2560]{1,0:T(8,128)}, f32[384,2560]{1,0:T(8,128)}) %tuple.56, (bf16[32,3,2560]{2,1,0:T(4,128)(2,1)S(1)}, ...), branch_computations={%region_3.3_spmd, %region_4.4_spmd} | conditional | flops 1514090496 | bytes 146325760 | solution.py:143
  1238.9 12.9 all-to-all-done.1
  1251.8 19.1 %conditional.2 = (bf16[96,2560]{1,0:T(8,128)(2,1)}, f32[384,2560]{1,0:T(8,128)}, f32[384,2560]{1,0:T(8,128)}, f32[384,2560]{1,0:T(8,128)}) conditional(s32[]{:T(128)} %convert_element_type.144, (f32[384,2560]{1,0:T(8,128)}, f32[384,2560]{1,0:T(8,128)}, f32[384,2560]{1,0:T(8,128)}) %tuple.56, (bf16[32,3,2560]{2,1,0:T(4,128)(2,1)S(1)}, ...), branch_computations={%region_3.3_spmd, %region_4.4_spmd} | conditional | flops 1514090496 | bytes 146325760 | solution.py:143
  1339.8 19.1 %conditional.2 = (bf16[96,2560]{1,0:T(8,128)(2,1)}, f32[384,2560]{1,0:T(8,128)}, f32[384,2560]{1,0:T(8,128)}, f32[384,2560]{1,0:T(8,128)}) conditional(s32[]{:T(128)} %convert_element_type.144, (f32[384,2560]{1,0:T(8,128)}, f32[384,2560]{1,0:T(8,128)}, f32[384,2560]{1,0:T(8,128)}) %tuple.56, (bf16[32,3,2560]{2,1,0:T(4,128)(2,1)S(1)}, ...), branch_computations={%region_3.3_spmd, %region_4.4_spmd} | conditional | flops 1514090496 | bytes 146325760 | solution.py:143
  (711 shorter events, 1044.5 us)
Async XLA Ops:
  82.7 21.6 %all-to-all-start = ((bf16[32,3,2560]{2,1,0:T(4,128)(2,1)}), bf16[32,3,2560]{2,1,0:T(4,128)(2,1)S(1)}, u32[]{:S(2)}, u32[]{:S(2)}) async-start(bf16[32,3,2560]{2,1,0:T(4,128)(2,1)} %bitcast.73), calls=%async_computation | async-start | bytes 1310720 | tf_op jit(solution)/shard_map/while/body/eval_jaxpr/all_to_all | solution.py:119
  105.2 17.1 %all-to-all-start.1 = ((bf16[32,3,2560]{2,1,0:T(4,128)(2,1)}), bf16[32,3,2560]{2,1,0:T(4,128)(2,1)S(1)}, u32[]{:S(2)}, u32[]{:S(2)}) async-start(bf16[32,3,2560]{2,1,0:T(4,128)(2,1)} %bitcast.77), calls=%async_computation.1 | async-start | bytes 1310720 | tf_op jit(solution)/shard_map/while/body/eval_jaxpr/all_to_all | solution.py:112
  154.4 18.3 %all-to-all-start = ((bf16[32,3,2560]{2,1,0:T(4,128)(2,1)}), bf16[32,3,2560]{2,1,0:T(4,128)(2,1)S(1)}, u32[]{:S(2)}, u32[]{:S(2)}) async-start(bf16[32,3,2560]{2,1,0:T(4,128)(2,1)} %bitcast.73), calls=%async_computation | async-start | bytes 1310720 | tf_op jit(solution)/shard_map/while/body/eval_jaxpr/all_to_all | solution.py:119
  173.6 17.1 %all-to-all-start.1 = ((bf16[32,3,2560]{2,1,0:T(4,128)(2,1)}), bf16[32,3,2560]{2,1,0:T(4,128)(2,1)S(1)}, u32[]{:S(2)}, u32[]{:S(2)}) async-start(bf16[32,3,2560]{2,1,0:T(4,128)(2,1)} %bitcast.77), calls=%async_computation.1 | async-start | bytes 1310720 | tf_op jit(solution)/shard_map/while/body/eval_jaxpr/all_to_all | solution.py:112
  222.8 18.3 %all-to-all-start = ((bf16[32,3,2560]{2,1,0:T(4,128)(2,1)}), bf16[32,3,2560]{2,1,0:T(4,128)(2,1)S(1)}, u32[]{:S(2)}, u32[]{:S(2)}) async-start(bf16[32,3,2560]{2,1,0:T(4,128)(2,1)} %bitcast.73), calls=%async_computation | async-start | bytes 1310720 | tf_op jit(solution)/shard_map/while/body/eval_jaxpr/all_to_all | solution.py:119
  242.1 17.1 %all-to-all-start.1 = ((bf16[32,3,2560]{2,1,0:T(4,128)(2,1)}), bf16[32,3,2560]{2,1,0:T(4,128)(2,1)S(1)}, u32[]{:S(2)}, u32[]{:S(2)}) async-start(bf16[32,3,2560]{2,1,0:T(4,128)(2,1)} %bitcast.77), calls=%async_computation.1 | async-start | bytes 1310720 | tf_op jit(solution)/shard_map/while/body/eval_jaxpr/all_to_all | solution.py:112
  291.2 18.3 %all-to-all-start = ((bf16[32,3,2560]{2,1,0:T(4,128)(2,1)}), bf16[32,3,2560]{2,1,0:T(4,128)(2,1)S(1)}, u32[]{:S(2)}, u32[]{:S(2)}) async-start(bf16[32,3,2560]{2,1,0:T(4,128)(2,1)} %bitcast.73), calls=%async_computation | async-start | bytes 1310720 | tf_op jit(solution)/shard_map/while/body/eval_jaxpr/all_to_all | solution.py:119
  310.5 17.1 %all-to-all-start.1 = ((bf16[32,3,2560]{2,1,0:T(4,128)(2,1)}), bf16[32,3,2560]{2,1,0:T(4,128)(2,1)S(1)}, u32[]{:S(2)}, u32[]{:S(2)}) async-start(bf16[32,3,2560]{2,1,0:T(4,128)(2,1)} %bitcast.77), calls=%async_computation.1 | async-start | bytes 1310720 | tf_op jit(solution)/shard_map/while/body/eval_jaxpr/all_to_all | solution.py:112
  359.6 18.3 %all-to-all-start = ((bf16[32,3,2560]{2,1,0:T(4,128)(2,1)}), bf16[32,3,2560]{2,1,0:T(4,128)(2,1)S(1)}, u32[]{:S(2)}, u32[]{:S(2)}) async-start(bf16[32,3,2560]{2,1,0:T(4,128)(2,1)} %bitcast.73), calls=%async_computation | async-start | bytes 1310720 | tf_op jit(solution)/shard_map/while/body/eval_jaxpr/all_to_all | solution.py:119
  378.9 17.1 %all-to-all-start.1 = ((bf16[32,3,2560]{2,1,0:T(4,128)(2,1)}), bf16[32,3,2560]{2,1,0:T(4,128)(2,1)S(1)}, u32[]{:S(2)}, u32[]{:S(2)}) async-start(bf16[32,3,2560]{2,1,0:T(4,128)(2,1)} %bitcast.77), calls=%async_computation.1 | async-start | bytes 1310720 | tf_op jit(solution)/shard_map/while/body/eval_jaxpr/all_to_all | solution.py:112
  428.0 18.3 %all-to-all-start = ((bf16[32,3,2560]{2,1,0:T(4,128)(2,1)}), bf16[32,3,2560]{2,1,0:T(4,128)(2,1)S(1)}, u32[]{:S(2)}, u32[]{:S(2)}) async-start(bf16[32,3,2560]{2,1,0:T(4,128)(2,1)} %bitcast.73), calls=%async_computation | async-start | bytes 1310720 | tf_op jit(solution)/shard_map/while/body/eval_jaxpr/all_to_all | solution.py:119
  447.3 17.1 %all-to-all-start.1 = ((bf16[32,3,2560]{2,1,0:T(4,128)(2,1)}), bf16[32,3,2560]{2,1,0:T(4,128)(2,1)S(1)}, u32[]{:S(2)}, u32[]{:S(2)}) async-start(bf16[32,3,2560]{2,1,0:T(4,128)(2,1)} %bitcast.77), calls=%async_computation.1 | async-start | bytes 1310720 | tf_op jit(solution)/shard_map/while/body/eval_jaxpr/all_to_all | solution.py:112
  498.1 17.7 %all-to-all-start = ((bf16[32,3,2560]{2,1,0:T(4,128)(2,1)}), bf16[32,3,2560]{2,1,0:T(4,128)(2,1)S(1)}, u32[]{:S(2)}, u32[]{:S(2)}) async-start(bf16[32,3,2560]{2,1,0:T(4,128)(2,1)} %bitcast.73), calls=%async_computation | async-start | bytes 1310720 | tf_op jit(solution)/shard_map/while/body/eval_jaxpr/all_to_all | solution.py:119
  556.7 127.6 %collective-permute-start = (bf16[16,2560]{1,0:T(8,128)(2,1)S(1)}, bf16[16,2560]{1,0:T(8,128)(2,1)S(1)}, u32[]{:S(2)}, u32[]{:S(2)}) collective-permute-start(bf16[16,2560]{1,0:T(8,128)(2,1)S(1)} %get-tuple-element.579), channel_id=1, source_target_pairs={{32,0},{64,32},{96,64},{128,96},{160,128},{192,160},{224,192},{33,... | collective-permute-start | bytes 245768 | tf_op jit(solution)/shard_map/while/body/eval_jaxpr/ppermute | solution.py:18
  688.3 17.7 %all-to-all-start = ((bf16[32,3,2560]{2,1,0:T(4,128)(2,1)}), bf16[32,3,2560]{2,1,0:T(4,128)(2,1)S(1)}, u32[]{:S(2)}, u32[]{:S(2)}) async-start(bf16[32,3,2560]{2,1,0:T(4,128)(2,1)} %bitcast.73), calls=%async_computation | async-start | bytes 1310720 | tf_op jit(solution)/shard_map/while/body/eval_jaxpr/all_to_all | solution.py:119
  745.5 17.1 %all-to-all-start.2 = ((bf16[32,3,2560]{2,1,0:T(4,128)(2,1)}), bf16[32,3,2560]{2,1,0:T(4,128)(2,1)S(1)}, u32[]{:S(2)}, u32[]{:S(2)}) async-start(bf16[32,3,2560]{2,1,0:T(4,128)(2,1)} %reshape.216), calls=%async_computation.2 | async-start | bytes 1310720 | tf_op jit(solution)/shard_map/while/body/eval_jaxpr/all_to_all | solution.py:144
  776.3 17.7 %all-to-all-start = ((bf16[32,3,2560]{2,1,0:T(4,128)(2,1)}), bf16[32,3,2560]{2,1,0:T(4,128)(2,1)S(1)}, u32[]{:S(2)}, u32[]{:S(2)}) async-start(bf16[32,3,2560]{2,1,0:T(4,128)(2,1)} %bitcast.73), calls=%async_computation | async-start | bytes 1310720 | tf_op jit(solution)/shard_map/while/body/eval_jaxpr/all_to_all | solution.py:119
  864.2 17.7 %all-to-all-start = ((bf16[32,3,2560]{2,1,0:T(4,128)(2,1)}), bf16[32,3,2560]{2,1,0:T(4,128)(2,1)S(1)}, u32[]{:S(2)}, u32[]{:S(2)}) async-start(bf16[32,3,2560]{2,1,0:T(4,128)(2,1)} %bitcast.73), calls=%async_computation | async-start | bytes 1310720 | tf_op jit(solution)/shard_map/while/body/eval_jaxpr/all_to_all | solution.py:119
  952.2 17.7 %all-to-all-start = ((bf16[32,3,2560]{2,1,0:T(4,128)(2,1)}), bf16[32,3,2560]{2,1,0:T(4,128)(2,1)S(1)}, u32[]{:S(2)}, u32[]{:S(2)}) async-start(bf16[32,3,2560]{2,1,0:T(4,128)(2,1)} %bitcast.73), calls=%async_computation | async-start | bytes 1310720 | tf_op jit(solution)/shard_map/while/body/eval_jaxpr/all_to_all | solution.py:119
  1040.1 17.7 %all-to-all-start = ((bf16[32,3,2560]{2,1,0:T(4,128)(2,1)}), bf16[32,3,2560]{2,1,0:T(4,128)(2,1)S(1)}, u32[]{:S(2)}, u32[]{:S(2)}) async-start(bf16[32,3,2560]{2,1,0:T(4,128)(2,1)} %bitcast.73), calls=%async_computation | async-start | bytes 1310720 | tf_op jit(solution)/shard_map/while/body/eval_jaxpr/all_to_all | solution.py:119
  1128.1 17.7 %all-to-all-start = ((bf16[32,3,2560]{2,1,0:T(4,128)(2,1)}), bf16[32,3,2560]{2,1,0:T(4,128)(2,1)S(1)}, u32[]{:S(2)}, u32[]{:S(2)}) async-start(bf16[32,3,2560]{2,1,0:T(4,128)(2,1)} %bitcast.73), calls=%async_computation | async-start | bytes 1310720 | tf_op jit(solution)/shard_map/while/body/eval_jaxpr/all_to_all | solution.py:119
  1216.0 17.7 %all-to-all-start = ((bf16[32,3,2560]{2,1,0:T(4,128)(2,1)}), bf16[32,3,2560]{2,1,0:T(4,128)(2,1)S(1)}, u32[]{:S(2)}, u32[]{:S(2)}) async-start(bf16[32,3,2560]{2,1,0:T(4,128)(2,1)} %bitcast.73), calls=%async_computation | async-start | bytes 1310720 | tf_op jit(solution)/shard_map/while/body/eval_jaxpr/all_to_all | solution.py:119
  1234.7 17.1 %all-to-all-start.1 = ((bf16[32,3,2560]{2,1,0:T(4,128)(2,1)}), bf16[32,3,2560]{2,1,0:T(4,128)(2,1)S(1)}, u32[]{:S(2)}, u32[]{:S(2)}) async-start(bf16[32,3,2560]{2,1,0:T(4,128)(2,1)} %bitcast.77), calls=%async_computation.1 | async-start | bytes 1310720 | tf_op jit(solution)/shard_map/while/body/eval_jaxpr/all_to_all | solution.py:112
  1304.0 17.7 %all-to-all-start = ((bf16[32,3,2560]{2,1,0:T(4,128)(2,1)}), bf16[32,3,2560]{2,1,0:T(4,128)(2,1)S(1)}, u32[]{:S(2)}, u32[]{:S(2)}) async-start(bf16[32,3,2560]{2,1,0:T(4,128)(2,1)} %bitcast.73), calls=%async_computation | async-start | bytes 1310720 | tf_op jit(solution)/shard_map/while/body/eval_jaxpr/all_to_all | solution.py:119
  (103 other events, 633.4 us)
where the time goes:
time: 1400 us; the launch traced here: 1390 us
  waiting for transfers between devices  748 us (53%)
  local copies, waits for them, and re-layouts  223 us (16%)
  starting transfers between devices  219 us (16%)
  matrix products  93.8 us (7%)
  blocking collectives  57.3 us (4%)
  other arithmetic  48.9 us (3%)
    ppermute x15, waiting for transfers between devices, passed_along(): lax.ppermute(value, axis, [(source, source + steps) for source in range(f...  195 us
    all_to_all x15, waiting for transfers between devices, clock_tick(): lax.all_to_all(spread(input_slots[chosen], experts, capacity), 'expert',...  193 us
    all_to_all x15, waiting for transfers between devices, clock_tick(): lax.all_to_all(slice_part.reshape(devices_wide, capacity, model_width), '...  181 us
    all_to_all x15, waiting for transfers between devices, clock_tick(): lax.all_to_all(spread(grad_slots, experts, capacity), 'expert', split_axi...  178 us
    all_to_all x15, starting transfers between devices, clock_tick(): lax.all_to_all(spread(grad_slots, experts, capacity), 'expert', split_axi...  76.6 us
    all_to_all x15, starting transfers between devices, clock_tick(): lax.all_to_all(spread(input_slots[chosen], experts, capacity), 'expert',...  61.5 us
    all_to_all x15, starting transfers between devices, clock_tick(): lax.all_to_all(slice_part.reshape(devices_wide, capacity, model_width), '...  61.4 us
    cond x128, local copies, waits for them, and re-layouts  58.5 us
  transfers between devices with their start and end apart: 60, of which 60 were waited for; matrix products, arithmetic and copies ran while one was open for 2% of the time, Pallas kernels for 0%

commit v1 on v0

v1 whole, which is shorter than its diff:
```python
import jax
import jax.numpy as jnp
from jax import lax
from jax.sharding import PartitionSpec as P

SPLIT = 2
GROUP = 2
ROOM = 4

ROWS_ROWS = (((0,), (0,)), ((), ()))
COLS_COLS = (((1,), (1,)), ((), ()))


def dot(left, right, dims=(((1,), (0,)), ((), ()))):
    return lax.dot_general(left, right, dims, preferred_element_type=jnp.float32)


def slot_tables(routes, gates, experts):
    batches, tokens, top = routes.shape
    groups = batches // GROUP
    rows = tokens * top
    flat = routes.reshape(batches, rows)
    same = flat[:, :, None] == flat[:, None, :]
    before = jnp.arange(rows)[:, None] > jnp.arange(rows)[None, :]
    position = jnp.sum(jnp.logical_and(same, before[None]).astype(jnp.int32), axis=2)
    half = jnp.arange(batches, dtype=jnp.int32)[:, None] % GROUP
    slot = flat * (GROUP * ROOM) + half * ROOM + position
    slot = slot.reshape(groups, 1, GROUP * tokens, top)
    slots = jnp.arange(experts * GROUP * ROOM, dtype=jnp.int32)[None, :, None, None]
    hit = slots == slot
    gate = jnp.where(hit, gates.reshape(groups, 1, GROUP * tokens, top), 0.0)
    placing = jnp.any(hit, axis=3).astype(jnp.bfloat16)
    return placing, jnp.sum(gate, axis=(2, 3))


def on_device(x_saved, routes, gates, cotangent, w_gate, w_up, w_down):
    sections = lax.axis_size("section")
    devices_wide = lax.axis_size("expert")
    section_index = lax.axis_index("section")
    chips = devices_wide // SPLIT
    _, batches, tokens, width = x_saved.shape
    groups = batches // GROUP
    block = GROUP * ROOM
    rows = chips * block
    hidden = w_gate.shape[1]
    same_core = [[SPLIT * c + k for c in range(chips)] for k in range(SPLIT)]
    swap = [(i, i ^ 1) for i in range(devices_wide)]
    ring = [(i, (i - 1) % sections) for i in range(sections)]

    def across(value):
        shaped = value.reshape(chips, -1, width)
        out = lax.all_to_all(shaped, "expert", 0, 0, axis_index_groups=same_core, tiled=True)
        return out.reshape(value.shape)

    def swapped(value):
        return lax.ppermute(value, "expert", swap)

    gate_rows, up_rows, down_rows = w_gate[0], w_up[0], w_down[0]
    both_rows = jnp.concatenate([gate_rows, up_rows], axis=0)

    by_group = cotangent.reshape(groups, GROUP * tokens, -1)
    order = [(z + 1) % sections if (z + 1) % sections < groups else 0 for z in range(sections)]
    pieces = jnp.stack([by_group[g] for g in order])
    pieces = lax.all_to_all(pieces, "section", 0, 0, tiled=True)
    arriving = pieces.transpose(1, 0, 2).reshape(GROUP * tokens, width)

    placing, slot_gates = slot_tables(routes[0], gates[0], chips)
    placing = jnp.concatenate([placing, jnp.zeros_like(placing[:1])])
    slot_gates = jnp.concatenate([slot_gates, jnp.zeros_like(slot_gates[:1])])

    x_groups = x_saved[0].reshape(groups, GROUP * tokens, width)
    x_slots = jnp.einsum(
        "gst,gtd->gsd", placing[:groups], x_groups, preferred_element_type=jnp.float32
    ).astype(jnp.bfloat16)
    x_slots = x_slots.reshape(groups, chips, block, width).transpose(1, 0, 2, 3)
    x_mine = across(x_slots.reshape(chips * groups * block, width))
    x_mine = x_mine.reshape(chips, groups, block, width).transpose(1, 0, 2, 3)
    x_mine = x_mine.reshape(groups, rows, width)
    x_all = jnp.concatenate([x_mine, swapped(x_mine)], axis=1)
    pre = dot(x_all.reshape(groups * SPLIT * rows, width), both_rows, COLS_COLS)
    pre_gate, pre_up = pre[:, :hidden], pre[:, hidden:]
    sigmoid = jax.nn.sigmoid(pre_gate)
    swished = pre_gate * sigmoid
    hidden_act = (swished * pre_up).astype(jnp.bfloat16)
    gate_slope = pre_up * (sigmoid * (1.0 + pre_gate * (1.0 - sigmoid)))
    slopes = jnp.concatenate([gate_slope, swished], axis=1).reshape(
        groups, SPLIT, rows, 2 * hidden
    )

    results = jnp.zeros((groups + 1, GROUP * tokens, width), jnp.bfloat16)
    kept_rows = jnp.zeros((groups + 1, SPLIT, rows, width), jnp.bfloat16)
    kept_d = jnp.zeros((groups + 1, SPLIT, rows, 2 * hidden), jnp.bfloat16)

    for tick in range(sections + groups - 1):
        group = tick - (sections - 1 - section_index)
        active = jnp.logical_and(group >= 0, group < groups)
        kept = jnp.where(active, group, groups)
        chosen = jnp.clip(group, 0, groups - 1)
        place = placing[kept]
        gate = slot_gates[kept]
        slope = slopes[chosen]

        def hidden_part(rows_grad, slope):
            d_hidden = dot(rows_grad, down_rows, COLS_COLS)
            return (jnp.concatenate([d_hidden, d_hidden], axis=1) * slope).astype(jnp.bfloat16)

        rows_mine = (dot(place, arriving) * gate[:, None]).astype(jnp.bfloat16)
        rows_mine = across(rows_mine)
        rows_other = swapped(rows_mine)
        d_mine = hidden_part(rows_mine, slope[0])
        d_other = hidden_part(rows_other, slope[1])
        part_other = dot(d_other, both_rows).astype(jnp.bfloat16)
        from_other = swapped(part_other)
        part_mine = dot(d_mine, both_rows).astype(jnp.bfloat16)
        summed = part_mine.astype(jnp.float32) + from_other.astype(jnp.float32)
        returned = across(summed.astype(jnp.bfloat16))
        outgoing = (arriving.astype(jnp.float32) + dot(place, returned, ROWS_ROWS)).astype(
            jnp.bfloat16
        )
        arriving = lax.ppermute(outgoing, "section", ring)
        results = lax.dynamic_update_index_in_dim(results, outgoing, kept, 0)
        kept_rows = lax.dynamic_update_slice(kept_rows, rows_mine[None, None], (kept, 0, 0, 0))
        kept_rows = lax.dynamic_update_slice(kept_rows, rows_other[None, None], (kept, 1, 0, 0))
        kept_d = lax.dynamic_update_slice(kept_d, d_mine[None, None], (kept, 0, 0, 0))
        kept_d = lax.dynamic_update_slice(kept_d, d_other[None, None], (kept, 1, 0, 0))

    all_d = kept_d[:groups].reshape(groups * SPLIT * rows, 2 * hidden)
    all_rows = kept_rows[:groups].reshape(groups * SPLIT * rows, width)
    both_grads = (dot(all_d, x_all.reshape(all_rows.shape), ROWS_ROWS) / batches).astype(
        jnp.bfloat16
    )
    grad_down = (dot(hidden_act, all_rows, ROWS_ROWS) / batches).astype(jnp.bfloat16)
    grad_inputs = results[:groups].reshape(1, batches, tokens, width)
    return (grad_inputs, both_grads[None, :hidden], both_grads[None, hidden:], grad_down[None])


def solution(mesh):
    in_specs = (
        P("section", None, "expert", None),
        P("section", None, "expert", None),
        P("section", None, "expert", None),
        P(None, "expert", "section"),
        P("section", "expert", None),
        P("section", "expert", None),
        P("section", "expert", None),
    )
    out_specs = (
        P("section", None, "expert", None),
        P("section", "expert", None),
        P("section", "expert", None),
        P("section", "expert", None),
    )
    return jax.shard_map(
        on_device, mesh=mesh, in_specs=in_specs, out_specs=out_specs, check_vma=False
    )
```

time: 1400 us -> 706 us (0.50)
  waiting for transfers between devices: 748 us -> 190 us
  local copies, waits for them, and re-layouts: 223 us -> 73.7 us
  starting transfers between devices: 219 us -> 123 us
  blocking collectives: 57.3 us -> 148 us
  matrix products: 93.8 us -> 113 us
    all_to_all x45 -> x14, waiting for transfers between devices: 553 us -> 162 us  [the longest x13 152 us: across(): lax.all_to_all(shaped, 'expert', 0, 0, axis_index_groups=same_core, tiled...]
    ppermute x15 -> x33, waiting for transfers between devices: 195 us -> 27.4 us  [the longest x23 14.3 us: swapped(): return lax.ppermute(value, 'expert', swap)]
    all_to_all x0 -> x10, blocking collectives: none -> 148 us  [across(): lax.all_to_all(shaped, 'expert', 0, 0, axis_index_groups=same_core, tiled...]
    all_to_all x45 -> x14, starting transfers between devices: 199 us -> 62.2 us  [the longest x13 54 us: across(): lax.all_to_all(shaped, 'expert', 0, 0, axis_index_groups=same_core, tiled...]
    cond x128 -> x0, local copies, waits for them, and re-layouts: 58.5 us -> none
    all_gather x1 -> x0, blocking collectives: 57.3 us -> none  [on_device(): top_grads = lax.all_gather(cotangent, 'section', axis=2, tiled=True)]
    reshape x47 -> x3, local copies, waits for them, and re-layouts: 52.7 us -> 5.43 us  [the longest x1 3.49 us: on_device(): x_mine = x_mine.reshape(groups, rows, width)]
    ppermute x15 -> x33, starting transfers between devices: 19.2 us -> 61.2 us  [the longest x23 36.7 us: swapped(): return lax.ppermute(value, 'expert', swap)]
  transfers between devices with their start and end apart: 60 -> 47, of which waited for: 60 -> 29; matrix products, arithmetic and copies ran while one was open for 2% -> 14% of each run, Pallas kernels for 0% -> 0%
where the time goes in v1:
time: 706 us; the launch traced here: 694 us
  waiting for transfers between devices  190 us (27%)
  blocking collectives  148 us (21%)
  starting transfers between devices  123 us (17%)
  matrix products  113 us (16%)
  local copies, waits for them, and re-layouts  73.7 us (10%)
  other arithmetic  43.4 us (6%)
    all_to_all x13, waiting for transfers between devices, across(): lax.all_to_all(shaped, 'expert', 0, 0, axis_index_groups=same_core, tiled...  152 us
    all_to_all x10, blocking collectives, across(): lax.all_to_all(shaped, 'expert', 0, 0, axis_index_groups=same_core, tiled...  148 us
    dot_general x69, matrix products, dot(): lax.dot_general(left, right, dims, preferred_element_type=jnp.float32)  111 us
    all_to_all x13, starting transfers between devices, across(): lax.all_to_all(shaped, 'expert', 0, 0, axis_index_groups=same_core, tiled...  54 us
    ppermute x23, starting transfers between devices, swapped(): return lax.ppermute(value, 'expert', swap)  36.7 us
    ppermute x10, starting transfers between devices, on_device(): arriving = lax.ppermute(outgoing, 'section', ring)  24.4 us
    dynamic_update_slice x11, other arithmetic, on_device(): lax.dynamic_update_slice(kept_d, d_mine[None, None], (kept, 0, 0, 0))  18.7 us
    dynamic_update_slice x11, other arithmetic, on_device(): lax.dynamic_update_slice(kept_d, d_other[None, None], (kept, 1, 0, 0))  17.8 us
  transfers between devices with their start and end apart: 47, of which 29 were waited for; matrix products, arithmetic and copies ran while one was open for 14% of the time, Pallas kernels for 0%

profile of v1, /device:TPU:1, one launch (start us, length us, event | category | flops | bytes accessed | tf_op | source)
XLA Modules:
  0.0 693.8 jit_solution(12187773706238781363)
XLA Ops:
  7.0 7.8 %all-to-all-start.2 = ((bf16[16,32,2560]{2,1,0:T(8,128)(2,1)}), bf16[16,32,2560]{2,1,0:T(8,128)(2,1)}, u32[]{:S(2)}, u32[]{:S(2)}) async-start(bf16[16,32,2560]{2,1,0:T(8,128)(2,1)} %bitcast.613), calls=%async_computation.2 | async-start | bytes 5242880 | tf_op jit(solution)/shard_map/all_to_all | solution.py:52
  16.0 37.7 %all-to-all-done.2 = bf16[16,32,2560]{2,1,0:T(8,128)(2,1)} async-done(((bf16[16,32,2560]{2,1,0:T(8,128)(2,1)}), bf16[16,32,2560]{2,1,0:T(8,128)(2,1)}, u32[]{:S(2)}, u32[]{:S(2)}) %all-to-all-start.2) | async-done | bytes 2621472 | tf_op jit(solution)/shard_map/all_to_all | solution.py:52
  62.7 8.2 %all-to-all-start = ((bf16[8,32,320]{2,1,0:T(8,128)(2,1)}), bf16[8,32,320]{2,1,0:T(8,128)(2,1)S(1)}, u32[]{:S(2)}, u32[]{:S(2)}) async-start(bf16[8,32,320]{2,1,0:T(8,128)(2,1)} %bitcast_dynamic-update-slice_fusion.36), calls=%async_computation | async-start | bytes 393216 | tf_op jit(solution)/shard_map/all_to_all | solution.py:64
  71.2 10.5 %all-to-all-done = bf16[8,32,320]{2,1,0:T(8,128)(2,1)S(1)} async-done(((bf16[8,32,320]{2,1,0:T(8,128)(2,1)}), bf16[8,32,320]{2,1,0:T(8,128)(2,1)S(1)}, u32[]{:S(2)}, u32[]{:S(2)}) %all-to-all-start) | async-done | bytes 163872 | tf_op jit(solution)/shard_map/all_to_all | solution.py:64
  82.3 15.0 %all_to_all.120 = bf16[16,8,2560]{2,1,0:T(8,128)(2,1)S(1)} all-to-all(bf16[16,8,2560]{2,1,0:T(8,128)(2,1)S(1)} %fusion.35), channel_id=1, replica_groups={{0,2,4,6,8,10,12,14,16,18,20,22,24,26,28,30},{1,3,5,7,9,11,13,15,17,19,..., dimensions={0} | all-to-all | bytes 1310720 | tf_op jit(solution)/shard_map/all_to_all | solution.py:52
  124.6 15.2 %all_to_all.121 = bf16[16,8,2560]{2,1,0:T(8,128)(2,1)S(1)} all-to-all(bf16[16,8,2560]{2,1,0:T(8,128)(2,1)S(1)} %fusion.82), channel_id=1, replica_groups={{0,2,4,6,8,10,12,14,16,18,20,22,24,26,28,30},{1,3,5,7,9,11,13,15,17,19,..., dimensions={0} | all-to-all | bytes 1310720 | tf_op jit(solution)/shard_map/all_to_all | solution.py:52
  146.4 14.4 %all_to_all.122 = bf16[16,8,2560]{2,1,0:T(8,128)(2,1)S(1)} all-to-all(bf16[16,8,2560]{2,1,0:T(8,128)(2,1)S(1)} %fusion.34), channel_id=1, replica_groups={{0,2,4,6,8,10,12,14,16,18,20,22,24,26,28,30},{1,3,5,7,9,11,13,15,17,19,..., dimensions={0} | all-to-all | bytes 1310720 | tf_op jit(solution)/shard_map/all_to_all | solution.py:52
  174.0 14.9 %all_to_all.123 = bf16[16,8,2560]{2,1,0:T(8,128)(2,1)S(1)} all-to-all(bf16[16,8,2560]{2,1,0:T(8,128)(2,1)S(1)} %fusion.83), channel_id=1, replica_groups={{0,2,4,6,8,10,12,14,16,18,20,22,24,26,28,30},{1,3,5,7,9,11,13,15,17,19,..., dimensions={0} | all-to-all | bytes 1310720 | tf_op jit(solution)/shard_map/all_to_all | solution.py:52
  194.3 14.6 %all_to_all.124 = bf16[16,8,2560]{2,1,0:T(8,128)(2,1)S(1)} all-to-all(bf16[16,8,2560]{2,1,0:T(8,128)(2,1)S(1)} %fusion.33), channel_id=1, replica_groups={{0,2,4,6,8,10,12,14,16,18,20,22,24,26,28,30},{1,3,5,7,9,11,13,15,17,19,..., dimensions={0} | all-to-all | bytes 1310720 | tf_op jit(solution)/shard_map/all_to_all | solution.py:52
  222.2 15.2 %all_to_all.125 = bf16[16,8,2560]{2,1,0:T(8,128)(2,1)S(1)} all-to-all(bf16[16,8,2560]{2,1,0:T(8,128)(2,1)S(1)} %fusion.84), channel_id=1, replica_groups={{0,2,4,6,8,10,12,14,16,18,20,22,24,26,28,30},{1,3,5,7,9,11,13,15,17,19,..., dimensions={0} | all-to-all | bytes 1310720 | tf_op jit(solution)/shard_map/all_to_all | solution.py:52
  243.7 14.0 %all_to_all.126 = bf16[16,8,2560]{2,1,0:T(8,128)(2,1)} all-to-all(bf16[16,8,2560]{2,1,0:T(8,128)(2,1)S(1)} %fusion.32), channel_id=1, replica_groups={{0,2,4,6,8,10,12,14,16,18,20,22,24,26,28,30},{1,3,5,7,9,11,13,15,17,19,..., dimensions={0} | all-to-all | bytes 1310720 | tf_op jit(solution)/shard_map/all_to_all | solution.py:52
  271.8 15.4 %all_to_all.127 = bf16[16,8,2560]{2,1,0:T(8,128)(2,1)S(1)} all-to-all(bf16[16,8,2560]{2,1,0:T(8,128)(2,1)S(1)} %fusion.85), channel_id=1, replica_groups={{0,2,4,6,8,10,12,14,16,18,20,22,24,26,28,30},{1,3,5,7,9,11,13,15,17,19,..., dimensions={0} | all-to-all | bytes 1310720 | tf_op jit(solution)/shard_map/all_to_all | solution.py:52
  294.3 14.1 %all_to_all.128 = bf16[16,8,2560]{2,1,0:T(8,128)(2,1)} all-to-all(bf16[16,8,2560]{2,1,0:T(8,128)(2,1)S(1)} %fusion.31), channel_id=1, replica_groups={{0,2,4,6,8,10,12,14,16,18,20,22,24,26,28,30},{1,3,5,7,9,11,13,15,17,19,..., dimensions={0} | all-to-all | bytes 1310720 | tf_op jit(solution)/shard_map/all_to_all | solution.py:52
  322.2 15.4 %all_to_all.129 = bf16[16,8,2560]{2,1,0:T(8,128)(2,1)S(1)} all-to-all(bf16[16,8,2560]{2,1,0:T(8,128)(2,1)S(1)} %fusion.86), channel_id=1, replica_groups={{0,2,4,6,8,10,12,14,16,18,20,22,24,26,28,30},{1,3,5,7,9,11,13,15,17,19,..., dimensions={0} | all-to-all | bytes 1310720 | tf_op jit(solution)/shard_map/all_to_all | solution.py:52
  350.3 11.0 %all-to-all-done.12 = bf16[16,8,2560]{2,1,0:T(8,128)(2,1)} async-done(((bf16[16,8,2560]{2,1,0:T(8,128)(2,1)}), bf16[16,8,2560]{2,1,0:T(8,128)(2,1)}, u32[]{:S(2)}, u32[]{:S(2)}) %all-to-all-start.12) | async-done | bytes 655392 | tf_op jit(solution)/shard_map/all_to_all | solution.py:52
  384.2 11.7 %all-to-all-done.13 = bf16[16,8,2560]{2,1,0:T(8,128)(2,1)} async-done(((bf16[16,8,2560]{2,1,0:T(8,128)(2,1)}), bf16[16,8,2560]{2,1,0:T(8,128)(2,1)}, u32[]{:S(2)}, u32[]{:S(2)}) %all-to-all-start.13) | async-done | bytes 655392 | tf_op jit(solution)/shard_map/all_to_all | solution.py:52
  413.4 7.6 %all-to-all-done.14 = bf16[16,8,2560]{2,1,0:T(8,128)(2,1)S(1)} async-done(((bf16[16,8,2560]{2,1,0:T(8,128)(2,1)}), bf16[16,8,2560]{2,1,0:T(8,128)(2,1)S(1)}, u32[]{:S(2)}, u32[]{:S(2)}) %all-to-all-start.14) | async-done | bytes 655392 | tf_op jit(solution)/shard_map/all_to_all | solution.py:52
  442.4 10.6 %all-to-all-done.15 = bf16[16,8,2560]{2,1,0:T(8,128)(2,1)S(1)} async-done(((bf16[16,8,2560]{2,1,0:T(8,128)(2,1)}), bf16[16,8,2560]{2,1,0:T(8,128)(2,1)S(1)}, u32[]{:S(2)}, u32[]{:S(2)}) %all-to-all-start.15) | async-done | bytes 655392 | tf_op jit(solution)/shard_map/all_to_all | solution.py:52
  469.4 7.7 %all-to-all-done.16 = bf16[16,8,2560]{2,1,0:T(8,128)(2,1)S(1)} async-done(((bf16[16,8,2560]{2,1,0:T(8,128)(2,1)}), bf16[16,8,2560]{2,1,0:T(8,128)(2,1)S(1)}, u32[]{:S(2)}, u32[]{:S(2)}) %all-to-all-start.16) | async-done | bytes 655392 | tf_op jit(solution)/shard_map/all_to_all | solution.py:52
  499.3 10.4 %all-to-all-done.17 = bf16[16,8,2560]{2,1,0:T(8,128)(2,1)} async-done(((bf16[16,8,2560]{2,1,0:T(8,128)(2,1)}), bf16[16,8,2560]{2,1,0:T(8,128)(2,1)}, u32[]{:S(2)}, u32[]{:S(2)}) %all-to-all-start.17) | async-done | bytes 655392 | tf_op jit(solution)/shard_map/all_to_all | solution.py:52
  556.3 11.7 %all-to-all-done.19 = bf16[16,8,2560]{2,1,0:T(8,128)(2,1)S(1)} async-done(((bf16[16,8,2560]{2,1,0:T(8,128)(2,1)}), bf16[16,8,2560]{2,1,0:T(8,128)(2,1)S(1)}, u32[]{:S(2)}, u32[]{:S(2)}) %all-to-all-start.19) | async-done | bytes 655392 | tf_op jit(solution)/shard_map/all_to_all | solution.py:52
  583.3 8.8 %all-to-all-done.20 = bf16[16,8,2560]{2,1,0:T(8,128)(2,1)S(1)} async-done(((bf16[16,8,2560]{2,1,0:T(8,128)(2,1)}), bf16[16,8,2560]{2,1,0:T(8,128)(2,1)S(1)}, u32[]{:S(2)}, u32[]{:S(2)}) %all-to-all-start.20) | async-done | bytes 655392 | tf_op jit(solution)/shard_map/all_to_all | solution.py:52
  610.7 11.5 %all-to-all-done.21 = bf16[16,8,2560]{2,1,0:T(8,128)(2,1)S(1)} async-done(((bf16[16,8,2560]{2,1,0:T(8,128)(2,1)}), bf16[16,8,2560]{2,1,0:T(8,128)(2,1)S(1)}, u32[]{:S(2)}, u32[]{:S(2)}) %all-to-all-start.21) | async-done | bytes 655392 | tf_op jit(solution)/shard_map/all_to_all | solution.py:52
  636.5 10.3 %all-to-all-done.22 = bf16[16,8,2560]{2,1,0:T(8,128)(2,1)S(1)} async-done(((bf16[16,8,2560]{2,1,0:T(8,128)(2,1)}), bf16[16,8,2560]{2,1,0:T(8,128)(2,1)S(1)}, u32[]{:S(2)}, u32[]{:S(2)}) %all-to-all-start.22) | async-done | bytes 655392 | tf_op jit(solution)/shard_map/all_to_all | solution.py:52
  (417 shorter events, 377.7 us)
Async XLA Ops:
  7.0 46.7 %all-to-all-start.2 = ((bf16[16,32,2560]{2,1,0:T(8,128)(2,1)}), bf16[16,32,2560]{2,1,0:T(8,128)(2,1)}, u32[]{:S(2)}, u32[]{:S(2)}) async-start(bf16[16,32,2560]{2,1,0:T(8,128)(2,1)} %bitcast.613), calls=%async_computation.2 | async-start | bytes 5242880 | tf_op jit(solution)/shard_map/all_to_all | solution.py:52
  57.2 45.3 %collective-permute-start = (bf16[4,128,2560]{2,1,0:T(8,128)(2,1)}, bf16[4,128,2560]{2,1,0:T(8,128)(2,1)}, u32[]{:S(2)}, u32[]{:S(2)}) collective-permute-start(bf16[4,128,2560]{2,1,0:T(8,128)(2,1)} %copy_bitcast_fusion), channel_id=1, source_target_pairs={{0,1},{1,0},{2,3},{3,2},{4,5},{5,4},{6,7},{7,6},{8,9},{9,8},{10,11... | collective-permute-start | bytes 7864328 | tf_op jit(solution)/shard_map/ppermute | solution.py:56
  62.7 19.0 %all-to-all-start = ((bf16[8,32,320]{2,1,0:T(8,128)(2,1)}), bf16[8,32,320]{2,1,0:T(8,128)(2,1)S(1)}, u32[]{:S(2)}, u32[]{:S(2)}) async-start(bf16[8,32,320]{2,1,0:T(8,128)(2,1)} %bitcast_dynamic-update-slice_fusion.36), calls=%async_computation | async-start | bytes 393216 | tf_op jit(solution)/shard_map/all_to_all | solution.py:64
  288.1 5.8 collective-permute-start.12
  338.5 5.6 collective-permute-start.15
  345.9 15.3 %all-to-all-start.12 = ((bf16[16,8,2560]{2,1,0:T(8,128)(2,1)}), bf16[16,8,2560]{2,1,0:T(8,128)(2,1)}, u32[]{:S(2)}, u32[]{:S(2)}) async-start(bf16[16,8,2560]{2,1,0:T(8,128)(2,1)} %fusion.30), calls=%async_computation.12 | async-start | bytes 1310720 | tf_op jit(solution)/shard_map/all_to_all | solution.py:52
  361.2 7.4 %collective-permute-start.16 = (bf16[128,2560]{1,0:T(8,128)(2,1)}, bf16[128,2560]{1,0:T(8,128)(2,1)S(1)}, u32[]{:S(2)}, u32[]{:S(2)}) collective-permute-start(bf16[128,2560]{1,0:T(8,128)(2,1)} %bitcast.67), channel_id=1, source_target_pairs={{0,1},{1,0},{2,3},{3,2},{4,5},{5,4},{6,7},{7,6},{8,9},{9,8},{10,11... | collective-permute-start | bytes 1966088 | tf_op jit(solution)/shard_map/ppermute | solution.py:56
  370.8 6.0 collective-permute-start.17
  379.0 16.9 %all-to-all-start.13 = ((bf16[16,8,2560]{2,1,0:T(8,128)(2,1)}), bf16[16,8,2560]{2,1,0:T(8,128)(2,1)}, u32[]{:S(2)}, u32[]{:S(2)}) async-start(bf16[16,8,2560]{2,1,0:T(8,128)(2,1)} %fusion.87), calls=%async_computation.13 | async-start | bytes 1310720 | tf_op jit(solution)/shard_map/all_to_all | solution.py:52
  397.9 6.8 collective-permute-start.18
  405.9 15.0 %all-to-all-start.14 = ((bf16[16,8,2560]{2,1,0:T(8,128)(2,1)}), bf16[16,8,2560]{2,1,0:T(8,128)(2,1)S(1)}, u32[]{:S(2)}, u32[]{:S(2)}) async-start(bf16[16,8,2560]{2,1,0:T(8,128)(2,1)} %fusion.29), calls=%async_computation.14 | async-start | bytes 1310720 | tf_op jit(solution)/shard_map/all_to_all | solution.py:52
  436.6 16.3 %all-to-all-start.15 = ((bf16[16,8,2560]{2,1,0:T(8,128)(2,1)}), bf16[16,8,2560]{2,1,0:T(8,128)(2,1)S(1)}, u32[]{:S(2)}, u32[]{:S(2)}) async-start(bf16[16,8,2560]{2,1,0:T(8,128)(2,1)} %fusion.88), calls=%async_computation.15 | async-start | bytes 1310720 | tf_op jit(solution)/shard_map/all_to_all | solution.py:52
  454.8 6.1 collective-permute-start.21
  462.1 15.0 %all-to-all-start.16 = ((bf16[16,8,2560]{2,1,0:T(8,128)(2,1)}), bf16[16,8,2560]{2,1,0:T(8,128)(2,1)S(1)}, u32[]{:S(2)}, u32[]{:S(2)}) async-start(bf16[16,8,2560]{2,1,0:T(8,128)(2,1)} %fusion.28), calls=%async_computation.16 | async-start | bytes 1310720 | tf_op jit(solution)/shard_map/all_to_all | solution.py:52
  492.9 16.8 %all-to-all-start.17 = ((bf16[16,8,2560]{2,1,0:T(8,128)(2,1)}), bf16[16,8,2560]{2,1,0:T(8,128)(2,1)}, u32[]{:S(2)}, u32[]{:S(2)}) async-start(bf16[16,8,2560]{2,1,0:T(8,128)(2,1)} %fusion.89), calls=%async_computation.17 | async-start | bytes 1310720 | tf_op jit(solution)/shard_map/all_to_all | solution.py:52
  511.8 6.1 collective-permute-start.24
  519.7 15.6 %all-to-all-start.18 = ((bf16[16,8,2560]{2,1,0:T(8,128)(2,1)}), bf16[16,8,2560]{2,1,0:T(8,128)(2,1)}, u32[]{:S(2)}, u32[]{:S(2)}) async-start(bf16[16,8,2560]{2,1,0:T(8,128)(2,1)} %fusion.27), calls=%async_computation.18 | async-start | bytes 1310720 | tf_op jit(solution)/shard_map/all_to_all | solution.py:52
  551.6 16.3 %all-to-all-start.19 = ((bf16[16,8,2560]{2,1,0:T(8,128)(2,1)}), bf16[16,8,2560]{2,1,0:T(8,128)(2,1)S(1)}, u32[]{:S(2)}, u32[]{:S(2)}) async-start(bf16[16,8,2560]{2,1,0:T(8,128)(2,1)} %fusion.90), calls=%async_computation.19 | async-start | bytes 1310720 | tf_op jit(solution)/shard_map/all_to_all | solution.py:52
  577.1 15.1 %all-to-all-start.20 = ((bf16[16,8,2560]{2,1,0:T(8,128)(2,1)}), bf16[16,8,2560]{2,1,0:T(8,128)(2,1)S(1)}, u32[]{:S(2)}, u32[]{:S(2)}) async-start(bf16[16,8,2560]{2,1,0:T(8,128)(2,1)} %fusion.26), calls=%async_computation.20 | async-start | bytes 1310720 | tf_op jit(solution)/shard_map/all_to_all | solution.py:52
  606.2 16.0 %all-to-all-start.21 = ((bf16[16,8,2560]{2,1,0:T(8,128)(2,1)}), bf16[16,8,2560]{2,1,0:T(8,128)(2,1)S(1)}, u32[]{:S(2)}, u32[]{:S(2)}) async-start(bf16[16,8,2560]{2,1,0:T(8,128)(2,1)} %fusion.91), calls=%async_computation.21 | async-start | bytes 1310720 | tf_op jit(solution)/shard_map/all_to_all | solution.py:52
  624.0 6.2 collective-permute-start.30
  632.0 14.8 %all-to-all-start.22 = ((bf16[16,8,2560]{2,1,0:T(8,128)(2,1)}), bf16[16,8,2560]{2,1,0:T(8,128)(2,1)S(1)}, u32[]{:S(2)}, u32[]{:S(2)}) async-start(bf16[16,8,2560]{2,1,0:T(8,128)(2,1)} %fusion.25), calls=%async_computation.22 | async-start | bytes 1310720 | tf_op jit(solution)/shard_map/all_to_all | solution.py:52
  646.8 6.2 collective-permute-start.31
  674.7 15.8 %all-to-all-start.23 = ((bf16[16,8,2560]{2,1,0:T(8,128)(2,1)}), bf16[16,8,2560]{2,1,0:T(8,128)(2,1)S(1)}, u32[]{:S(2)}, u32[]{:S(2)}) async-start(bf16[16,8,2560]{2,1,0:T(8,128)(2,1)} %fusion.92), calls=%async_computation.23 | async-start | bytes 1310720 | tf_op jit(solution)/shard_map/all_to_all | solution.py:52
  (111 other events, 718.9 us)

commit v2 on v1

v2 whole, which is shorter than its diff:
```python
import jax
import jax.numpy as jnp
from jax import lax
from jax.sharding import PartitionSpec as P

SPLIT = 2
GROUP = 2
ROOM = 4
CAP = 3

ROWS_ROWS = (((0,), (0,)), ((), ()))
COLS_COLS = (((1,), (1,)), ((), ()))


def dot(left, right, dims=(((1,), (0,)), ((), ()))):
    return lax.dot_general(left, right, dims, preferred_element_type=jnp.float32)


def slot_tables(routes, gates, experts):
    batches, tokens, top = routes.shape
    groups = batches // GROUP
    rows = tokens * top
    flat = routes.reshape(batches, rows)
    same = flat[:, :, None] == flat[:, None, :]
    before = jnp.arange(rows)[:, None] > jnp.arange(rows)[None, :]
    position = jnp.sum(jnp.logical_and(same, before[None]).astype(jnp.int32), axis=2)
    batch = jnp.arange(batches, dtype=jnp.int32)[:, None]
    slot = flat * (GROUP * ROOM) + batch % GROUP * ROOM + position
    slot = slot.reshape(groups, 1, GROUP * tokens, top)
    slots = jnp.arange(experts * GROUP * ROOM, dtype=jnp.int32)
    hit = slots[None, :, None, None] == slot
    gate = jnp.where(hit, gates.reshape(groups, 1, GROUP * tokens, top), 0.0)
    placing = jnp.any(hit, axis=3).astype(jnp.bfloat16)
    pack = (flat * batches + batch) * CAP + position
    packs = jnp.arange(experts * batches * CAP, dtype=jnp.int32)
    packing = packs[:, None, None] == pack.reshape(1, batches * tokens, top)
    packing = jnp.any(packing, axis=2).astype(jnp.bfloat16)
    half, place = slots % (GROUP * ROOM) // ROOM, slots % ROOM
    source = slots // (GROUP * ROOM) * batches + half
    source = source + jnp.arange(groups, dtype=jnp.int32)[:, None] * GROUP
    source = jnp.where(place < CAP, source * CAP + place, -1)
    unpacking = (source[:, :, None] == packs[None, None, :]).astype(jnp.bfloat16)
    return placing, jnp.sum(gate, axis=(2, 3)), packing, unpacking


def on_device(x_saved, routes, gates, cotangent, w_gate, w_up, w_down):
    sections = lax.axis_size("section")
    devices_wide = lax.axis_size("expert")
    section_index = lax.axis_index("section")
    chips = devices_wide // SPLIT
    _, batches, tokens, width = x_saved.shape
    groups = batches // GROUP
    block = GROUP * ROOM
    rows = chips * block
    hidden = w_gate.shape[1]
    same_core = [[SPLIT * c + k for c in range(chips)] for k in range(SPLIT)]
    swap = [(i, i ^ 1) for i in range(devices_wide)]
    ring = [(i, (i - 1) % sections) for i in range(sections)]

    def across(value):
        shaped = value.reshape(chips, -1, width)
        out = lax.all_to_all(shaped, "expert", 0, 0, axis_index_groups=same_core, tiled=True)
        return out.reshape(value.shape)

    def swapped(value):
        return lax.ppermute(value, "expert", swap)

    gate_rows, up_rows, down_rows = w_gate[0], w_up[0], w_down[0]
    both_rows = jnp.concatenate([gate_rows, up_rows], axis=0)

    by_group = cotangent.reshape(groups, GROUP * tokens, -1)
    pieces = jnp.concatenate([by_group[1:], by_group[: sections - groups], by_group[:1]])
    placing, slot_gates, packing, unpacking = slot_tables(routes[0], gates[0], chips)
    padded_placing = jnp.concatenate([placing, jnp.zeros_like(placing[:1])])
    padded_gates = jnp.concatenate([slot_gates, jnp.zeros_like(slot_gates[:1])])
    pieces = lax.all_to_all(pieces, "section", 0, 0, tiled=True)

    x_tokens = x_saved[0].reshape(batches * tokens, width)
    packed = packing.shape[0] // chips
    first = section_index == sections - 1
    start_place = jnp.where(first, placing[0], 0).reshape(chips, block, GROUP * tokens)
    start_place = jnp.pad(start_place, ((0, 0), (0, packed), (0, 0)))
    start_pack = jnp.pad(packing.reshape(chips, packed, -1), ((0, 0), (block, 0), (0, 0)))
    start_place = jnp.concatenate([start_place, start_pack], axis=2)
    start_place = start_place.reshape(chips * (block + packed), -1)
    start_gate = jnp.pad(
        slot_gates[0].reshape(chips, block), ((0, 0), (0, packed)), constant_values=1.0
    ).reshape(-1, 1)
    pieces, both_rows, padded_placing, padded_gates, start_place, start_gate, unpacking = (
        lax.optimization_barrier(
            (pieces, both_rows, padded_placing, padded_gates, start_place, start_gate, unpacking)
        )
    )
    arriving = pieces.transpose(1, 0, 2).reshape(GROUP * tokens, width)

    def forward(x_mine, x_other):
        x_both = jnp.concatenate([x_mine, x_other], axis=0)
        pre = dot(x_both, both_rows, COLS_COLS)
        pre_gate, pre_up = pre[:, :hidden], pre[:, hidden:]
        sigmoid = jax.nn.sigmoid(pre_gate)
        swished = pre_gate * sigmoid
        gate_slope = pre_up * (sigmoid * (1.0 + pre_gate * (1.0 - sigmoid)))
        slope = jnp.concatenate([gate_slope, swished], axis=1)
        return x_both, slope, (swished * pre_up).astype(jnp.bfloat16)

    def hidden_part(rows_grad, slope):
        d_hidden = dot(rows_grad, down_rows, COLS_COLS)
        return (jnp.concatenate([d_hidden, d_hidden], axis=1) * slope).astype(jnp.bfloat16)

    x_rows, slopes, hidden_acts = [], [], []
    kept_rows, kept_d, kept_out = [], [], []
    stacked_slopes = None
    ticks = sections + groups - 1
    for tick in range(ticks):
        group = tick - (sections - 1 - section_index)
        active = jnp.logical_and(group >= 0, group < groups)
        place = padded_placing[jnp.where(active, group, groups)]
        gate = padded_gates[jnp.where(active, group, groups)]

        if tick == 0:
            rows_out = dot(start_place, jnp.concatenate([arriving, x_tokens])) * start_gate
            came = across(rows_out.astype(jnp.bfloat16))
            came_other = swapped(came)
            spread = (chips, block + packed, width)
            rows_mine, rows_other = [
                value.reshape(spread)[:, :block].reshape(rows, width)
                for value in (came, came_other)
            ]
            packs = [
                value.reshape(spread)[:, block:].reshape(chips * packed, width)
                for value in (came, came_other)
            ]

            def group_inputs(g, packs):
                found = [dot(unpacking[g], value).astype(jnp.bfloat16) for value in packs]
                return forward(*found)

            parts = [group_inputs(0, packs)]
            slope = parts[0][1]
        else:
            slope = lax.dynamic_index_in_dim(
                stacked_slopes, jnp.clip(group, 0, groups - 1), 0, keepdims=False
            )
            arriving, place, gate, slope = lax.optimization_barrier((arriving, place, gate, slope))
            rows_mine = across((dot(place, arriving) * gate[:, None]).astype(jnp.bfloat16))
            rows_other = swapped(rows_mine)
        d_mine = hidden_part(rows_mine, slope[:rows])
        d_mine, rows_other = lax.optimization_barrier((d_mine, rows_other))
        d_other = hidden_part(rows_other, slope[rows:])
        part_other = dot(d_other, both_rows).astype(jnp.bfloat16)
        from_other = swapped(part_other)
        part_mine = dot(d_mine, both_rows).astype(jnp.bfloat16)
        part_mine, from_other = lax.optimization_barrier((part_mine, from_other))
        summed = part_mine.astype(jnp.float32) + from_other.astype(jnp.float32)
        summed = summed.astype(jnp.bfloat16)
        kept_rows.append((rows_mine, rows_other))
        kept_d.append((d_mine, d_other))
        if tick == 0:
            summed, packs = lax.optimization_barrier((summed, packs))
            parts += [group_inputs(g, packs) for g in range(1, groups)]
            x_rows, slopes, hidden_acts = zip(*parts)
            stacked_slopes = jnp.stack(slopes)
        if tick == ticks - 1:
            summed, kept_rows, kept_d = lax.optimization_barrier((summed, kept_rows, kept_d))
        returned = across(summed)
        outgoing = (arriving.astype(jnp.float32) + dot(place, returned, ROWS_ROWS)).astype(
            jnp.bfloat16
        )
        kept_out.append(outgoing)
        if tick < ticks - 1:
            arriving = lax.ppermute(outgoing, "section", ring)

    all_x = jnp.concatenate(x_rows)
    all_act = jnp.concatenate(hidden_acts)

    def weight_grads(start):
        def products():
            span = range(start, start + groups)
            all_rows = jnp.concatenate([value for t in span for value in kept_rows[t]])
            all_d = jnp.concatenate([value for t in span for value in kept_d[t]])
            pairs = ((all_d[:, :hidden], all_x), (all_d[:, hidden:], all_x), (all_act, all_rows))
            return tuple(
                (dot(left, right, ROWS_ROWS) / batches).astype(jnp.bfloat16)
                for left, right in pairs
            )

        return products

    grads = lax.switch(
        section_index, [weight_grads(sections - 1 - s) for s in range(sections)]
    )
    results = lax.dynamic_slice_in_dim(
        jnp.concatenate(kept_out),
        (sections - 1 - section_index) * GROUP * tokens,
        batches * tokens,
        axis=0,
    )
    return (results.reshape(1, batches, tokens, width),) + tuple(g[None] for g in grads)


def solution(mesh):
    in_specs = (
        P("section", None, "expert", None),
        P("section", None, "expert", None),
        P("section", None, "expert", None),
        P(None, "expert", "section"),
        P("section", "expert", None),
        P("section", "expert", None),
        P("section", "expert", None),
    )
    out_specs = (
        P("section", None, "expert", None),
        P("section", "expert", None),
        P("section", "expert", None),
        P("section", "expert", None),
    )
    return jax.shard_map(
        on_device, mesh=mesh, in_specs=in_specs, out_specs=out_specs, check_vma=False
    )
```

time: 706 us -> 607 us (0.86)
  blocking collectives: 148 us -> 318 us
  waiting for transfers between devices: 190 us -> 39.7 us
  local copies, waits for them, and re-layouts: 73.7 us -> 30.6 us
  matrix products: 113 us -> 73.7 us
  starting transfers between devices: 123 us -> 90.8 us
  loops' own time: 0 us -> 23.8 us
  other arithmetic: 43.4 us -> 19.7 us
    all_to_all x10 -> x20, blocking collectives: 148 us -> 318 us  [across(): lax.all_to_all(shaped, 'expert', 0, 0, axis_index_groups=same_core, tiled...]
    all_to_all x13 -> x2, waiting for transfers between devices: 152 us -> 0.01 us  [across(): lax.all_to_all(shaped, 'expert', 0, 0, axis_index_groups=same_core, tiled...]
    all_to_all x13 -> x2, starting transfers between devices: 54 us -> 8.75 us  [across(): lax.all_to_all(shaped, 'expert', 0, 0, axis_index_groups=same_core, tiled...]
    dot_general x69 -> x81, matrix products: 111 us -> 73.7 us  [dot(): lax.dot_general(left, right, dims, preferred_element_type=jnp.float32)]
    dynamic_update_slice x22 -> x0, other arithmetic: 36.4 us -> none  [the longest x11 18.7 us: on_device(): lax.dynamic_update_slice(kept_d, d_mine[None, None], (kept, 0, 0, 0))]
    dynamic_update_slice x22 -> x0, local copies, waits for them, and re-layouts: 29.9 us -> none  [the longest x11 15.4 us: on_device(): lax.dynamic_update_slice(kept_rows, rows_other[None, None], (kept, 1, 0, 0))]
    another operation x0 -> x1, loops' own time: none -> 23.8 us  [on_device(): lax.switch(section_index, [weight_grads(sections - 1 - s) for s in range(...]
    unnamed x186 -> x119, local copies, waits for them, and re-layouts: 16.6 us -> 3 us
  transfers between devices with their start and end apart: 47 -> 35, of which waited for: 29 -> 28; matrix products, arithmetic and copies ran while one was open for 14% -> 13% of each run, Pallas kernels for 0% -> 0%
where the time goes in v2:
time: 607 us; the launch traced here: 599 us
  blocking collectives  318 us (52%)
  starting transfers between devices  90.8 us (15%)
  matrix products  73.7 us (12%)
  waiting for transfers between devices  39.7 us (7%)
  local copies, waits for them, and re-layouts  30.6 us (5%)
  loops' own time  23.8 us (4%)
  other arithmetic  19.7 us (3%)
    all_to_all x20, blocking collectives, across(): lax.all_to_all(shaped, 'expert', 0, 0, axis_index_groups=same_core, tiled...  318 us
    dot_general x81, matrix products, dot(): lax.dot_general(left, right, dims, preferred_element_type=jnp.float32)  73.7 us
    ppermute x22, starting transfers between devices, swapped(): return lax.ppermute(value, 'expert', swap)  40.7 us
    ppermute x10, starting transfers between devices, on_device(): arriving = lax.ppermute(outgoing, 'section', ring)  32.4 us
    another operation x1, loops' own time, on_device(): lax.switch(section_index, [weight_grads(sections - 1 - s) for s in range(...  23.8 us
    ppermute x10, waiting for transfers between devices, on_device(): arriving = lax.ppermute(outgoing, 'section', ring)  20.8 us
    ppermute x22, waiting for transfers between devices, swapped(): return lax.ppermute(value, 'expert', swap)  18.9 us
  transfers between devices with their start and end apart: 35, of which 28 were waited for; matrix products, arithmetic and copies ran while one was open for 13% of the time, Pallas kernels for 0%

profile of v2, /device:TPU:1, one launch (start us, length us, event | category | flops | bytes accessed | tf_op | source)
XLA Modules:
  0.0 598.5 jit_solution(10017874216902301039)
XLA Ops:
  4.0 9.0 %all-to-all-start = ((bf16[8,32,320]{2,1,0:T(8,128)(2,1)}), bf16[8,32,320]{2,1,0:T(8,128)(2,1)S(1)}, u32[]{:S(2)}, u32[]{:S(2)}) async-start(bf16[8,32,320]{2,1,0:T(8,128)(2,1)} %pad_maximum_fusion.4), calls=%async_computation | async-start | bytes 393216 | tf_op jit(solution)/shard_map/all_to_all | solution.py:76
  24.2 37.9 %all_to_all.115 = bf16[16,32,2560]{2,1,0:T(8,128)(2,1)} all-to-all(bf16[16,32,2560]{2,1,0:T(8,128)(2,1)S(1)} %bitcast.561), channel_id=1, replica_groups={{0,2,4,6,8,10,12,14,16,18,20,22,24,26,28,30},{1,3,5,7,9,11,13,15,17,19,..., dimensions={0} | all-to-all | bytes 5242880 | tf_op jit(solution)/shard_map/all_to_all | solution.py:62
  110.5 4.8 dynamic-slice_bitcast_fusion
  115.7 17.9 %all_to_all.116 = bf16[16,8,2560]{2,1,0:T(8,128)(2,1)S(1)} all-to-all(bf16[16,8,2560]{2,1,0:T(8,128)(2,1)S(1)} %fusion.83), channel_id=1, replica_groups={{0,2,4,6,8,10,12,14,16,18,20,22,24,26,28,30},{1,3,5,7,9,11,13,15,17,19,..., dimensions={0} | all-to-all | bytes 1310720 | tf_op jit(solution)/shard_map/all_to_all | solution.py:62
  142.3 15.4 %all_to_all.117 = bf16[16,8,2560]{2,1,0:T(8,128)(2,1)S(1)} all-to-all(bf16[16,8,2560]{2,1,0:T(8,128)(2,1)S(1)} %fusion.150), channel_id=1, replica_groups={{0,2,4,6,8,10,12,14,16,18,20,22,24,26,28,30},{1,3,5,7,9,11,13,15,17,19,..., dimensions={0} | all-to-all | bytes 1310720 | tf_op jit(solution)/shard_map/all_to_all | solution.py:62
  162.6 14.1 %all_to_all.118 = bf16[16,8,2560]{2,1,0:T(8,128)(2,1)S(1)} all-to-all(bf16[16,8,2560]{2,1,0:T(8,128)(2,1)S(1)} %fusion.82), channel_id=1, replica_groups={{0,2,4,6,8,10,12,14,16,18,20,22,24,26,28,30},{1,3,5,7,9,11,13,15,17,19,..., dimensions={0} | all-to-all | bytes 1310720 | tf_op jit(solution)/shard_map/all_to_all | solution.py:62
  185.5 15.2 %all_to_all.119 = bf16[16,8,2560]{2,1,0:T(8,128)(2,1)S(1)} all-to-all(bf16[16,8,2560]{2,1,0:T(8,128)(2,1)S(1)} %fusion.151), channel_id=1, replica_groups={{0,2,4,6,8,10,12,14,16,18,20,22,24,26,28,30},{1,3,5,7,9,11,13,15,17,19,..., dimensions={0} | all-to-all | bytes 1310720 | tf_op jit(solution)/shard_map/all_to_all | solution.py:62
  206.3 13.8 %all_to_all.120 = bf16[16,8,2560]{2,1,0:T(8,128)(2,1)S(1)} all-to-all(bf16[16,8,2560]{2,1,0:T(8,128)(2,1)S(1)} %fusion.81), channel_id=1, replica_groups={{0,2,4,6,8,10,12,14,16,18,20,22,24,26,28,30},{1,3,5,7,9,11,13,15,17,19,..., dimensions={0} | all-to-all | bytes 1310720 | tf_op jit(solution)/shard_map/all_to_all | solution.py:62
  229.0 15.2 %all_to_all.121 = bf16[16,8,2560]{2,1,0:T(8,128)(2,1)S(1)} all-to-all(bf16[16,8,2560]{2,1,0:T(8,128)(2,1)S(1)} %fusion.152), channel_id=1, replica_groups={{0,2,4,6,8,10,12,14,16,18,20,22,24,26,28,30},{1,3,5,7,9,11,13,15,17,19,..., dimensions={0} | all-to-all | bytes 1310720 | tf_op jit(solution)/shard_map/all_to_all | solution.py:62
  250.7 13.8 %all_to_all.122 = bf16[16,8,2560]{2,1,0:T(8,128)(2,1)S(1)} all-to-all(bf16[16,8,2560]{2,1,0:T(8,128)(2,1)S(1)} %fusion.80), channel_id=1, replica_groups={{0,2,4,6,8,10,12,14,16,18,20,22,24,26,28,30},{1,3,5,7,9,11,13,15,17,19,..., dimensions={0} | all-to-all | bytes 1310720 | tf_op jit(solution)/shard_map/all_to_all | solution.py:62
  273.5 15.2 %all_to_all.123 = bf16[16,8,2560]{2,1,0:T(8,128)(2,1)S(1)} all-to-all(bf16[16,8,2560]{2,1,0:T(8,128)(2,1)S(1)} %fusion.153), channel_id=1, replica_groups={{0,2,4,6,8,10,12,14,16,18,20,22,24,26,28,30},{1,3,5,7,9,11,13,15,17,19,..., dimensions={0} | all-to-all | bytes 1310720 | tf_op jit(solution)/shard_map/all_to_all | solution.py:62
  295.2 13.8 %all_to_all.124 = bf16[16,8,2560]{2,1,0:T(8,128)(2,1)S(1)} all-to-all(bf16[16,8,2560]{2,1,0:T(8,128)(2,1)S(1)} %fusion.79), channel_id=1, replica_groups={{0,2,4,6,8,10,12,14,16,18,20,22,24,26,28,30},{1,3,5,7,9,11,13,15,17,19,..., dimensions={0} | all-to-all | bytes 1310720 | tf_op jit(solution)/shard_map/all_to_all | solution.py:62
  317.8 15.2 %all_to_all.125 = bf16[16,8,2560]{2,1,0:T(8,128)(2,1)S(1)} all-to-all(bf16[16,8,2560]{2,1,0:T(8,128)(2,1)S(1)} %fusion.154), channel_id=1, replica_groups={{0,2,4,6,8,10,12,14,16,18,20,22,24,26,28,30},{1,3,5,7,9,11,13,15,17,19,..., dimensions={0} | all-to-all | bytes 1310720 | tf_op jit(solution)/shard_map/all_to_all | solution.py:62
  339.5 13.9 %all_to_all.126 = bf16[16,8,2560]{2,1,0:T(8,128)(2,1)S(1)} all-to-all(bf16[16,8,2560]{2,1,0:T(8,128)(2,1)S(1)} %fusion.78), channel_id=1, replica_groups={{0,2,4,6,8,10,12,14,16,18,20,22,24,26,28,30},{1,3,5,7,9,11,13,15,17,19,..., dimensions={0} | all-to-all | bytes 1310720 | tf_op jit(solution)/shard_map/all_to_all | solution.py:62
  362.2 15.2 %all_to_all.127 = bf16[16,8,2560]{2,1,0:T(8,128)(2,1)S(1)} all-to-all(bf16[16,8,2560]{2,1,0:T(8,128)(2,1)S(1)} %fusion.155), channel_id=1, replica_groups={{0,2,4,6,8,10,12,14,16,18,20,22,24,26,28,30},{1,3,5,7,9,11,13,15,17,19,..., dimensions={0} | all-to-all | bytes 1310720 | tf_op jit(solution)/shard_map/all_to_all | solution.py:62
  383.8 13.8 %all_to_all.128 = bf16[16,8,2560]{2,1,0:T(8,128)(2,1)S(1)} all-to-all(bf16[16,8,2560]{2,1,0:T(8,128)(2,1)S(1)} %fusion.77), channel_id=1, replica_groups={{0,2,4,6,8,10,12,14,16,18,20,22,24,26,28,30},{1,3,5,7,9,11,13,15,17,19,..., dimensions={0} | all-to-all | bytes 1310720 | tf_op jit(solution)/shard_map/all_to_all | solution.py:62
  406.7 15.2 %all_to_all.129 = bf16[16,8,2560]{2,1,0:T(8,128)(2,1)S(1)} all-to-all(bf16[16,8,2560]{2,1,0:T(8,128)(2,1)S(1)} %fusion.156), channel_id=1, replica_groups={{0,2,4,6,8,10,12,14,16,18,20,22,24,26,28,30},{1,3,5,7,9,11,13,15,17,19,..., dimensions={0} | all-to-all | bytes 1310720 | tf_op jit(solution)/shard_map/all_to_all | solution.py:62
  428.4 13.8 %all_to_all.130 = bf16[16,8,2560]{2,1,0:T(8,128)(2,1)S(1)} all-to-all(bf16[16,8,2560]{2,1,0:T(8,128)(2,1)S(1)} %fusion.76), channel_id=1, replica_groups={{0,2,4,6,8,10,12,14,16,18,20,22,24,26,28,30},{1,3,5,7,9,11,13,15,17,19,..., dimensions={0} | all-to-all | bytes 1310720 | tf_op jit(solution)/shard_map/all_to_all | solution.py:62
  451.1 15.2 %all_to_all.131 = bf16[16,8,2560]{2,1,0:T(8,128)(2,1)S(1)} all-to-all(bf16[16,8,2560]{2,1,0:T(8,128)(2,1)S(1)} %fusion.157), channel_id=1, replica_groups={{0,2,4,6,8,10,12,14,16,18,20,22,24,26,28,30},{1,3,5,7,9,11,13,15,17,19,..., dimensions={0} | all-to-all | bytes 1310720 | tf_op jit(solution)/shard_map/all_to_all | solution.py:62
  472.8 13.8 %all_to_all.132 = bf16[16,8,2560]{2,1,0:T(8,128)(2,1)S(1)} all-to-all(bf16[16,8,2560]{2,1,0:T(8,128)(2,1)S(1)} %fusion.75), channel_id=1, replica_groups={{0,2,4,6,8,10,12,14,16,18,20,22,24,26,28,30},{1,3,5,7,9,11,13,15,17,19,..., dimensions={0} | all-to-all | bytes 1310720 | tf_op jit(solution)/shard_map/all_to_all | solution.py:62
  495.9 15.2 %all_to_all.133 = bf16[16,8,2560]{2,1,0:T(8,128)(2,1)S(1)} all-to-all(bf16[16,8,2560]{2,1,0:T(8,128)(2,1)S(1)} %fusion.158), channel_id=1, replica_groups={{0,2,4,6,8,10,12,14,16,18,20,22,24,26,28,30},{1,3,5,7,9,11,13,15,17,19,..., dimensions={0} | all-to-all | bytes 1310720 | tf_op jit(solution)/shard_map/all_to_all | solution.py:62
  517.6 13.8 %all_to_all.134 = bf16[16,8,2560]{2,1,0:T(8,128)(2,1)S(1)} all-to-all(bf16[16,8,2560]{2,1,0:T(8,128)(2,1)S(1)} %fusion.74), channel_id=1, replica_groups={{0,2,4,6,8,10,12,14,16,18,20,22,24,26,28,30},{1,3,5,7,9,11,13,15,17,19,..., dimensions={0} | all-to-all | bytes 1310720 | tf_op jit(solution)/shard_map/all_to_all | solution.py:62
  547.7 46.5 %conditional.1 = (bf16[1,384,2560]{2,1,0:T(8,128)(2,1)}, bf16[1,384,2560]{2,1,0:T(8,128)(2,1)}, bf16[1,384,2560]{2,1,0:T(8,128)(2,1)}) conditional(s32[]{:T(128)} %clamp.3, (bf16[128,768]{1,0:T(8,128)(2,1)}, bf16[128,768]{1,0:T(8,128)(2,1)}, bf16[128,768]{1,0:T(8,128)(2,1)}, bf16[128,768]{1,0:T(8,128)(2,1)}, ...), branch_computations={%region_4.5_spmd, %region_5.6_spmd, %region_6.7_spmd, %region_7.8_... | conditional | flops 6045696000 | bytes 79036768 | solution.py:189
  552.8 6.1 %fusion.5 = bf16[1,384,2560]{2,1,0:T(8,128)(2,1)} fusion(bf16[1024,2560]{1,0:T(8,128)(2,1)} %get-tuple-element.299, bf16[1024,768]{1,0:T(8,128)(2,1)S(1)} %constant_dynamic-update-slice_fusion), kind=kOutput, calls=%fused_computation.8 | convolution fusion | flops 2015232000 | bytes 7995392 | tf_op jit(solution)/shard_map/cond/branch_0_fun/dot_general | solution.py:16
  (406 shorter events, 234.6 us)
Async XLA Ops:
  4.0 17.9 %all-to-all-start = ((bf16[8,32,320]{2,1,0:T(8,128)(2,1)}), bf16[8,32,320]{2,1,0:T(8,128)(2,1)S(1)}, u32[]{:S(2)}, u32[]{:S(2)}) async-start(bf16[8,32,320]{2,1,0:T(8,128)(2,1)} %pad_maximum_fusion.4), calls=%async_computation | async-start | bytes 393216 | tf_op jit(solution)/shard_map/all_to_all | solution.py:76
  62.0 9.3 %collective-permute-start = (bf16[512,2560]{1,0:T(8,128)(2,1)}, bf16[512,2560]{1,0:T(8,128)(2,1)}, u32[]{:S(2)}, u32[]{:S(2)}) collective-permute-start(bf16[512,2560]{1,0:T(8,128)(2,1)} %bitcast.50), channel_id=1, source_target_pairs={{0,1},{1,0},{2,3},{3,2},{4,5},{5,4},{6,7},{7,6},{8,9},{9,8},{10,11... | collective-permute-start | bytes 7864328 | tf_op jit(solution)/shard_map/ppermute | solution.py:66
  83.3 23.3 %all-to-all-start.2 = ((bf16[16,8,2560]{2,1,0:T(8,128)(2,1)}), bf16[16,8,2560]{2,1,0:T(8,128)(2,1)}, u32[]{:S(2)}, u32[]{:S(2)}) async-start(bf16[16,8,2560]{2,1,0:T(8,128)(2,1)} %bitcast.563), calls=%async_computation.2 | async-start | bytes 1310720 | tf_op jit(solution)/shard_map/all_to_all | solution.py:62
  107.9 7.5 %collective-permute-start.2 = (bf16[32,2560]{1,0:T(8,128)(2,1)S(1)}, bf16[32,2560]{1,0:T(8,128)(2,1)S(1)}, u32[]{:S(2)}, u32[]{:S(2)}) collective-permute-start(bf16[32,2560]{1,0:T(8,128)(2,1)S(1)} %get-tuple-element.805), channel_id=1, source_target_pairs={{0,224},{32,0},{64,32},{96,64},{128,96},{160,128},{192,160},{224,1... | collective-permute-start | bytes 491528 | tf_op jit(solution)/shard_map/ppermute | solution.py:171
  133.7 4.2 collective-permute-start.3
  158.0 4.2 collective-permute-start.5
  176.7 4.9 collective-permute-start.6
  200.9 5.1 collective-permute-start.8
  220.2 5.0 collective-permute-start.9
  244.4 5.9 collective-permute-start.11
  264.5 5.0 collective-permute-start.12
  288.9 5.9 collective-permute-start.14
  309.0 5.0 collective-permute-start.15
  333.3 5.9 collective-permute-start.17
  353.3 5.0 collective-permute-start.18
  377.6 5.9 collective-permute-start.20
  397.7 5.2 collective-permute-start.21
  422.1 5.9 collective-permute-start.23
  442.3 5.0 collective-permute-start.24
  466.5 5.9 collective-permute-start.26
  486.6 5.0 collective-permute-start.27
  511.3 5.9 collective-permute-start.29
  531.4 5.0 collective-permute-start.30
  542.1 52.1 %all-to-all-start.22 = ((bf16[16,8,2560]{2,1,0:T(8,128)(2,1)}), bf16[16,8,2560]{2,1,0:T(8,128)(2,1)}, u32[]{:S(2)}, u32[]{:S(2)}) async-start(bf16[16,8,2560]{2,1,0:T(8,128)(2,1)} %bitcast.562), calls=%async_computation.22 | async-start | bytes 1310720 | tf_op jit(solution)/shard_map/all_to_all | solution.py:62
  (81 other events, 392.3 us)

commit v3 on v2

v3 whole, which is shorter than its diff:
```python
from functools import partial

import jax
import jax.numpy as jnp
from jax import lax
from jax.experimental import pallas as pl
from jax.experimental.pallas import tpu as pltpu
from jax.sharding import PartitionSpec as P

SPLIT = 2
GROUP = 2
ROOM = 4
CAP = 3

ROWS_ROWS = (((0,), (0,)), ((), ()))
COLS_COLS = (((1,), (1,)), ((), ()))


def dot(left, right, dims=(((1,), (0,)), ((), ()))):
    return lax.dot_general(left, right, dims, preferred_element_type=jnp.float32)


def slot_tables(routes, gates, experts):
    batches, tokens, top = routes.shape
    groups = batches // GROUP
    rows = tokens * top
    flat = routes.reshape(batches, rows)
    same = flat[:, :, None] == flat[:, None, :]
    before = jnp.arange(rows)[:, None] > jnp.arange(rows)[None, :]
    position = jnp.sum(jnp.logical_and(same, before[None]).astype(jnp.int32), axis=2)
    batch = jnp.arange(batches, dtype=jnp.int32)[:, None]
    slot = flat * (GROUP * ROOM) + batch % GROUP * ROOM + position
    slot = slot.reshape(groups, 1, GROUP * tokens, top)
    slots = jnp.arange(experts * GROUP * ROOM, dtype=jnp.int32)
    hit = slots[None, :, None, None] == slot
    gate = jnp.where(hit, gates.reshape(groups, 1, GROUP * tokens, top), 0.0)
    placing = jnp.any(hit, axis=3).astype(jnp.bfloat16)
    pack = (flat * batches + batch) * CAP + position
    packs = jnp.arange(experts * batches * CAP, dtype=jnp.int32)
    packing = packs[:, None, None] == pack.reshape(1, batches * tokens, top)
    packing = jnp.any(packing, axis=2).astype(jnp.bfloat16)
    half, place = slots % (GROUP * ROOM) // ROOM, slots % ROOM
    source = slots // (GROUP * ROOM) * batches + half
    source = source + jnp.arange(groups, dtype=jnp.int32)[:, None] * GROUP
    source = jnp.where(place < CAP, source * CAP + place, -1)
    unpacking = (source[:, :, None] == packs[None, None, :]).astype(jnp.bfloat16)
    return placing, jnp.sum(gate, axis=(2, 3)), packing, unpacking


def add_kernel(first, final, batches, chosen, *refs):
    d_halves, row_halves, x_halves, act_halves = refs[:2], refs[2:4], refs[4:6], refs[6:8]
    before, after = (None, refs[8:11]) if first else (refs[8:11], refs[11:14])
    hidden = after[0].shape[0]

    def product(lefts, rights):
        left = jnp.concatenate(lefts, axis=0)
        right = jnp.concatenate(rights, axis=0)
        return dot(left, right, ROWS_ROWS)

    both = product([d[...] for d in d_halves], [x[0] for x in x_halves])
    down = product([act[0] for act in act_halves], [value[...] for value in row_halves])
    for i, term in enumerate((both[:hidden], both[hidden:], down)):
        total = term if first else before[i][...] + term
        after[i][...] = (total / batches).astype(jnp.bfloat16) if final else total


def add_weight_grads(chosen, d_halves, row_halves, x_halves, act_halves, sums, final, batches):
    rows, width = row_halves[0].shape
    hidden = act_halves[0].shape[2]
    tile = 512 if width % 512 == 0 else width
    whole = pl.BlockSpec((rows, 2 * hidden), lambda n, at: (0, 0))
    row_tile = pl.BlockSpec((rows, tile), lambda n, at: (0, n))
    x_tile = pl.BlockSpec((1, rows, tile), lambda n, at: (at[0], 0, n))
    act_tile = pl.BlockSpec((1, rows, hidden), lambda n, at: (at[0], 0, 0))
    sum_tile = pl.BlockSpec((hidden, tile), lambda n, at: (0, n))
    first = sums is None
    held = [] if first else list(sums)
    aliases = {} if first or final else {9 + i: i for i in range(3)}
    held_as = jnp.bfloat16 if final else jnp.float32
    flops = 2 * 3 * SPLIT * rows * hidden * width
    return pl.pallas_call(
        partial(add_kernel, first, final, batches),
        grid_spec=pltpu.PrefetchScalarGridSpec(
            num_scalar_prefetch=1,
            grid=(width // tile,),
            in_specs=[whole] * 2 + [row_tile] * 2 + [x_tile] * 2 + [act_tile] * 2
            + [sum_tile] * len(held),
            out_specs=[sum_tile] * 3,
        ),
        out_shape=[jax.ShapeDtypeStruct((hidden, width), held_as)] * 3,
        input_output_aliases=aliases,
        compiler_params=pltpu.CompilerParams(vmem_limit_bytes=24 * 1024 * 1024),
        cost_estimate=pl.CostEstimate(
            flops=flops, bytes_accessed=6 * 4 * hidden * width, transcendentals=0
        ),
    )(jnp.reshape(chosen, (1,)), *d_halves, *row_halves, *x_halves, *act_halves, *held)


def on_device(x_saved, routes, gates, cotangent, w_gate, w_up, w_down):
    sections = lax.axis_size("section")
    devices_wide = lax.axis_size("expert")
    section_index = lax.axis_index("section")
    chips = devices_wide // SPLIT
    _, batches, tokens, width = x_saved.shape
    groups = batches // GROUP
    block = GROUP * ROOM
    rows = chips * block
    hidden = w_gate.shape[1]
    same_core = [[SPLIT * c + k for c in range(chips)] for k in range(SPLIT)]
    swap = [(i, i ^ 1) for i in range(devices_wide)]
    ring = [(i, (i - 1) % sections) for i in range(sections)]

    def across(value):
        shaped = value.reshape(chips, -1, width)
        out = lax.all_to_all(shaped, "expert", 0, 0, axis_index_groups=same_core, tiled=True)
        return out.reshape(value.shape)

    def swapped(value):
        return lax.ppermute(value, "expert", swap)

    gate_rows, up_rows, down_rows = w_gate[0], w_up[0], w_down[0]
    both_rows = jnp.concatenate([gate_rows, up_rows], axis=0)

    placing, slot_gates, packing, unpacking = slot_tables(routes[0], gates[0], chips)
    x_tokens = x_saved[0].reshape(batches * tokens, width)
    x_packed = across(dot(packing, x_tokens).astype(jnp.bfloat16))

    by_group = cotangent.reshape(groups, GROUP * tokens, -1)
    pieces = jnp.concatenate([by_group[1:], by_group[: sections - groups], by_group[:1]])
    padded_placing = jnp.concatenate([placing, jnp.zeros_like(placing[:1])])
    padded_gates = jnp.concatenate([slot_gates, jnp.zeros_like(slot_gates[:1])])
    x_packed, pieces, both_rows, padded_placing, padded_gates, unpacking = (
        lax.optimization_barrier(
            (x_packed, pieces, both_rows, padded_placing, padded_gates, unpacking)
        )
    )
    pieces = lax.all_to_all(pieces, "section", 0, 0, tiled=True)
    arriving = pieces.transpose(1, 0, 2).reshape(GROUP * tokens, width)

    def forward(packed):
        x = dot(unpacking.reshape(groups * rows, -1), packed).astype(jnp.bfloat16)
        pre = dot(x, both_rows, COLS_COLS)
        pre_gate, pre_up = pre[:, :hidden], pre[:, hidden:]
        sigmoid = jax.nn.sigmoid(pre_gate)
        swished = pre_gate * sigmoid
        gate_slope = pre_up * (sigmoid * (1.0 + pre_gate * (1.0 - sigmoid)))
        slope = jnp.concatenate([gate_slope, swished], axis=1)
        act = (swished * pre_up).astype(jnp.bfloat16)
        return [value.reshape(groups, rows, -1) for value in (x, slope, act)]

    halves = [forward(packed) for packed in (x_packed, swapped(x_packed))]
    x_halves, slope_halves, act_halves = zip(*halves)

    def hidden_part(rows_grad, slope):
        d_hidden = dot(rows_grad, down_rows, COLS_COLS)
        return (jnp.concatenate([d_hidden, d_hidden], axis=1) * slope).astype(jnp.bfloat16)

    kept_out, sums = [], None
    ticks = sections + groups - 1
    for tick in range(ticks):
        group = tick - (sections - 1 - section_index)
        active = jnp.logical_and(group >= 0, group < groups)
        place = padded_placing[jnp.where(active, group, groups)]
        gate = padded_gates[jnp.where(active, group, groups)]
        chosen = jnp.clip(group, 0, groups - 1)
        slopes = [
            lax.dynamic_index_in_dim(value, chosen, 0, keepdims=False) for value in slope_halves
        ]
        if tick > 0:
            arriving, place, gate, slopes = lax.optimization_barrier(
                (arriving, place, gate, slopes)
            )
        rows_mine = across((dot(place, arriving) * gate[:, None]).astype(jnp.bfloat16))
        rows_other = swapped(rows_mine)
        d_mine = hidden_part(rows_mine, slopes[0])
        d_mine, rows_other = lax.optimization_barrier((d_mine, rows_other))
        d_other = hidden_part(rows_other, slopes[1])
        part_other = dot(d_other, both_rows).astype(jnp.bfloat16)
        from_other = swapped(part_other)
        part_mine = dot(d_mine, both_rows).astype(jnp.bfloat16)
        part_mine, from_other = lax.optimization_barrier((part_mine, from_other))
        summed = part_mine.astype(jnp.float32) + from_other.astype(jnp.float32)
        summed = summed.astype(jnp.bfloat16)
        if tick == ticks - 1:
            results = lax.dynamic_slice_in_dim(
                jnp.concatenate(kept_out + [arriving]),
                (sections - 1 - section_index) * GROUP * tokens,
                batches * tokens,
                axis=0,
            )
            summed, results = lax.optimization_barrier((summed, results))
        summed, grads, row_halves = lax.optimization_barrier(
            (summed, (d_mine, d_other), (rows_mine, rows_other))
        )
        sums = add_weight_grads(
            chosen, grads, row_halves, x_halves, act_halves, sums, tick == ticks - 1, batches
        )
        returned = across(summed)
        outgoing = (arriving.astype(jnp.float32) + dot(place, returned, ROWS_ROWS)).astype(
            jnp.bfloat16
        )
        if tick < ticks - 1:
            kept_out.append(outgoing)
            arriving = lax.ppermute(outgoing, "section", ring)

    last = results[-GROUP * tokens :]
    last = jnp.where(section_index == 0, outgoing, last)
    results = lax.dynamic_update_slice(results, last, (results.shape[0] - GROUP * tokens, 0))
    return (results.reshape(1, batches, tokens, width),) + tuple(g[None] for g in sums)


def solution(mesh):
    in_specs = (
        P("section", None, "expert", None),
        P("section", None, "expert", None),
        P("section", None, "expert", None),
        P(None, "expert", "section"),
        P("section", "expert", None),
        P("section", "expert", None),
        P("section", "expert", None),
    )
    out_specs = (
        P("section", None, "expert", None),
        P("section", "expert", None),
        P("section", "expert", None),
        P("section", "expert", None),
    )
    return jax.shard_map(
        on_device, mesh=mesh, in_specs=in_specs, out_specs=out_specs, check_vma=False
    )
```

time: 607 us -> 650 us (1.071)
  blocking collectives: 318 us -> 263 us
  Pallas kernels: 0 us -> 49.5 us
  local copies, waits for them, and re-layouts: 30.6 us -> 65.3 us
  waiting for transfers between devices: 39.7 us -> 71.8 us
  loops' own time: 23.8 us -> 0 us
  starting transfers between devices: 90.8 us -> 108 us
  matrix products: 73.7 us -> 63.9 us
  other arithmetic: 19.7 us -> 13.2 us
    all_to_all x20 -> x18, blocking collectives: 318 us -> 263 us  [across(): lax.all_to_all(shaped, 'expert', 0, 0, axis_index_groups=same_core, tiled...]
    pallas_call x0 -> x11, Pallas kernels: none -> 49.5 us  [add_weight_grads(): pl.pallas_call(partial(add_kernel, first, final, batches), grid_spec=pltp...]
    unnamed x119 -> x259, local copies, waits for them, and re-layouts: 3 us -> 51.7 us
    all_to_all x2 -> x5, waiting for transfers between devices: 0.01 us -> 34.9 us  [across(): lax.all_to_all(shaped, 'expert', 0, 0, axis_index_groups=same_core, tiled...]
    another operation x1 -> x0, loops' own time: 23.8 us -> none  [on_device(): lax.switch(section_index, [weight_grads(sections - 1 - s) for s in range(...]
    all_to_all x2 -> x5, starting transfers between devices: 8.75 us -> 28.2 us  [across(): lax.all_to_all(shaped, 'expert', 0, 0, axis_index_groups=same_core, tiled...]
    cond x39 -> x0, local copies, waits for them, and re-layouts: 9.84 us -> none
    dot_general x81 -> x71, matrix products: 73.7 us -> 63.9 us  [dot(): lax.dot_general(left, right, dims, preferred_element_type=jnp.float32)]
  transfers between devices with their start and end apart: 35 -> 39, of which waited for: 28 -> 31; matrix products, arithmetic and copies ran while one was open for 13% -> 8% of each run, Pallas kernels for 0% -> 8%
where the time goes in v3:
time: 650 us; the launch traced here: 638 us
  blocking collectives  263 us (40%)
  starting transfers between devices  108 us (17%)
  waiting for transfers between devices  71.8 us (11%)
  local copies, waits for them, and re-layouts  65.3 us (10%)
  matrix products  63.9 us (10%)
  Pallas kernels  49.5 us (8%)
  other arithmetic  13.2 us (2%)
    all_to_all x18, blocking collectives, across(): lax.all_to_all(shaped, 'expert', 0, 0, axis_index_groups=same_core, tiled...  263 us
    dot_general x71, matrix products, dot(): lax.dot_general(left, right, dims, preferred_element_type=jnp.float32)  63.9 us
    unnamed x259, local copies, waits for them, and re-layouts  51.7 us
    pallas_call x11, Pallas kernels, add_weight_grads(): pl.pallas_call(partial(add_kernel, first, final, batches), grid_spec=pltp...  49.5 us
    ppermute x23, starting transfers between devices, swapped(): return lax.ppermute(value, 'expert', swap)  41.2 us
    all_to_all x5, waiting for transfers between devices, across(): lax.all_to_all(shaped, 'expert', 0, 0, axis_index_groups=same_core, tiled...  34.9 us
    ppermute x10, starting transfers between devices, on_device(): arriving = lax.ppermute(outgoing, 'section', ring)  30.7 us
    all_to_all x5, starting transfers between devices, across(): lax.all_to_all(shaped, 'expert', 0, 0, axis_index_groups=same_core, tiled...  28.2 us
  transfers between devices with their start and end apart: 39, of which 31 were waited for; matrix products, arithmetic and copies ran while one was open for 8% of the time, Pallas kernels for 8%

profile of v3, /device:TPU:1, one launch (start us, length us, event | category | flops | bytes accessed | tf_op | source)
XLA Modules:
  0.0 638.4 jit_solution(4554460124505608584)
XLA Ops:
  6.1 7.8 %all-to-all-start = ((bf16[16,24,2560]{2,1,0:T(8,128)(2,1)}), bf16[16,24,2560]{2,1,0:T(8,128)(2,1)}, u32[]{:S(2)}, u32[]{:S(2)}) async-start(bf16[16,24,2560]{2,1,0:T(8,128)(2,1)} %bitcast.470), calls=%async_computation | async-start | bytes 3932160 | tf_op jit(solution)/shard_map/all_to_all | solution.py:115
  20.1 22.4 %all-to-all-done = bf16[16,24,2560]{2,1,0:T(8,128)(2,1)} async-done(((bf16[16,24,2560]{2,1,0:T(8,128)(2,1)}), bf16[16,24,2560]{2,1,0:T(8,128)(2,1)}, u32[]{:S(2)}, u32[]{:S(2)}) %all-to-all-start) | async-done | bytes 1966112 | tf_op jit(solution)/shard_map/all_to_all | solution.py:115
  42.6 8.2 %all-to-all-start.1 = ((bf16[8,32,320]{2,1,0:T(8,128)(2,1)}), bf16[8,32,320]{2,1,0:T(8,128)(2,1)S(1)}, u32[]{:S(2)}, u32[]{:S(2)}) async-start(bf16[8,32,320]{2,1,0:T(8,128)(2,1)} %pad_maximum_fusion.3), calls=%async_computation.1 | async-start | bytes 393216 | tf_op jit(solution)/shard_map/all_to_all | solution.py:137
  65.7 6.3 fusion.158
  102.0 7.9 %all-to-all-done.3 = bf16[16,8,2560]{2,1,0:T(8,128)(2,1)S(1)} async-done(((bf16[16,8,2560]{2,1,0:T(8,128)(2,1)}), bf16[16,8,2560]{2,1,0:T(8,128)(2,1)S(1)}, u32[]{:S(2)}, u32[]{:S(2)}) %all-to-all-start.3) | async-done | bytes 655392 | tf_op jit(solution)/shard_map/all_to_all | solution.py:115
  115.7 14.9 %all_to_all.120 = bf16[16,8,2560]{2,1,0:T(8,128)(2,1)S(1)} all-to-all(bf16[16,8,2560]{2,1,0:T(8,128)(2,1)S(1)} %fusion.20), channel_id=1, replica_groups={{0,2,4,6,8,10,12,14,16,18,20,22,24,26,28,30},{1,3,5,7,9,11,13,15,17,19,..., dimensions={0} | all-to-all | bytes 1310720 | tf_op jit(solution)/shard_map/all_to_all | solution.py:115
  139.9 15.4 %all_to_all.121 = bf16[16,8,2560]{2,1,0:T(8,128)(2,1)S(1)} all-to-all(bf16[16,8,2560]{2,1,0:T(8,128)(2,1)S(1)} %bitcast.475), channel_id=1, replica_groups={{0,2,4,6,8,10,12,14,16,18,20,22,24,26,28,30},{1,3,5,7,9,11,13,15,17,19,..., dimensions={0} | all-to-all | bytes 1310720 | tf_op jit(solution)/shard_map/all_to_all | solution.py:115
  160.2 14.3 %all_to_all.122 = bf16[16,8,2560]{2,1,0:T(8,128)(2,1)S(1)} all-to-all(bf16[16,8,2560]{2,1,0:T(8,128)(2,1)S(1)} %fusion.19), channel_id=1, replica_groups={{0,2,4,6,8,10,12,14,16,18,20,22,24,26,28,30},{1,3,5,7,9,11,13,15,17,19,..., dimensions={0} | all-to-all | bytes 1310720 | tf_op jit(solution)/shard_map/all_to_all | solution.py:115
  183.2 15.2 %all_to_all.123 = bf16[16,8,2560]{2,1,0:T(8,128)(2,1)S(1)} all-to-all(bf16[16,8,2560]{2,1,0:T(8,128)(2,1)S(1)} %bitcast.476), channel_id=1, replica_groups={{0,2,4,6,8,10,12,14,16,18,20,22,24,26,28,30},{1,3,5,7,9,11,13,15,17,19,..., dimensions={0} | all-to-all | bytes 1310720 | tf_op jit(solution)/shard_map/all_to_all | solution.py:115
  204.2 13.8 %all_to_all.124 = bf16[16,8,2560]{2,1,0:T(8,128)(2,1)S(1)} all-to-all(bf16[16,8,2560]{2,1,0:T(8,128)(2,1)S(1)} %fusion.18), channel_id=1, replica_groups={{0,2,4,6,8,10,12,14,16,18,20,22,24,26,28,30},{1,3,5,7,9,11,13,15,17,19,..., dimensions={0} | all-to-all | bytes 1310720 | tf_op jit(solution)/shard_map/all_to_all | solution.py:115
  227.4 15.2 %all_to_all.125 = bf16[16,8,2560]{2,1,0:T(8,128)(2,1)S(1)} all-to-all(bf16[16,8,2560]{2,1,0:T(8,128)(2,1)S(1)} %bitcast.477), channel_id=1, replica_groups={{0,2,4,6,8,10,12,14,16,18,20,22,24,26,28,30},{1,3,5,7,9,11,13,15,17,19,..., dimensions={0} | all-to-all | bytes 1310720 | tf_op jit(solution)/shard_map/all_to_all | solution.py:115
  249.1 13.8 %all_to_all.126 = bf16[16,8,2560]{2,1,0:T(8,128)(2,1)S(1)} all-to-all(bf16[16,8,2560]{2,1,0:T(8,128)(2,1)S(1)} %fusion.17), channel_id=1, replica_groups={{0,2,4,6,8,10,12,14,16,18,20,22,24,26,28,30},{1,3,5,7,9,11,13,15,17,19,..., dimensions={0} | all-to-all | bytes 1310720 | tf_op jit(solution)/shard_map/all_to_all | solution.py:115
  271.8 15.2 %all_to_all.127 = bf16[16,8,2560]{2,1,0:T(8,128)(2,1)S(1)} all-to-all(bf16[16,8,2560]{2,1,0:T(8,128)(2,1)S(1)} %bitcast.478), channel_id=1, replica_groups={{0,2,4,6,8,10,12,14,16,18,20,22,24,26,28,30},{1,3,5,7,9,11,13,15,17,19,..., dimensions={0} | all-to-all | bytes 1310720 | tf_op jit(solution)/shard_map/all_to_all | solution.py:115
  293.4 13.8 %all_to_all.128 = bf16[16,8,2560]{2,1,0:T(8,128)(2,1)S(1)} all-to-all(bf16[16,8,2560]{2,1,0:T(8,128)(2,1)S(1)} %fusion.16), channel_id=1, replica_groups={{0,2,4,6,8,10,12,14,16,18,20,22,24,26,28,30},{1,3,5,7,9,11,13,15,17,19,..., dimensions={0} | all-to-all | bytes 1310720 | tf_op jit(solution)/shard_map/all_to_all | solution.py:115
  316.3 15.2 %all_to_all.129 = bf16[16,8,2560]{2,1,0:T(8,128)(2,1)S(1)} all-to-all(bf16[16,8,2560]{2,1,0:T(8,128)(2,1)S(1)} %bitcast.479), channel_id=1, replica_groups={{0,2,4,6,8,10,12,14,16,18,20,22,24,26,28,30},{1,3,5,7,9,11,13,15,17,19,..., dimensions={0} | all-to-all | bytes 1310720 | tf_op jit(solution)/shard_map/all_to_all | solution.py:115
  338.0 13.8 %all_to_all.130 = bf16[16,8,2560]{2,1,0:T(8,128)(2,1)S(1)} all-to-all(bf16[16,8,2560]{2,1,0:T(8,128)(2,1)S(1)} %fusion.15), channel_id=1, replica_groups={{0,2,4,6,8,10,12,14,16,18,20,22,24,26,28,30},{1,3,5,7,9,11,13,15,17,19,..., dimensions={0} | all-to-all | bytes 1310720 | tf_op jit(solution)/shard_map/all_to_all | solution.py:115
  360.6 15.2 %all_to_all.131 = bf16[16,8,2560]{2,1,0:T(8,128)(2,1)S(1)} all-to-all(bf16[16,8,2560]{2,1,0:T(8,128)(2,1)S(1)} %bitcast.480), channel_id=1, replica_groups={{0,2,4,6,8,10,12,14,16,18,20,22,24,26,28,30},{1,3,5,7,9,11,13,15,17,19,..., dimensions={0} | all-to-all | bytes 1310720 | tf_op jit(solution)/shard_map/all_to_all | solution.py:115
  382.3 13.8 %all_to_all.132 = bf16[16,8,2560]{2,1,0:T(8,128)(2,1)S(1)} all-to-all(bf16[16,8,2560]{2,1,0:T(8,128)(2,1)S(1)} %fusion.14), channel_id=1, replica_groups={{0,2,4,6,8,10,12,14,16,18,20,22,24,26,28,30},{1,3,5,7,9,11,13,15,17,19,..., dimensions={0} | all-to-all | bytes 1310720 | tf_op jit(solution)/shard_map/all_to_all | solution.py:115
  404.9 15.2 %all_to_all.133 = bf16[16,8,2560]{2,1,0:T(8,128)(2,1)S(1)} all-to-all(bf16[16,8,2560]{2,1,0:T(8,128)(2,1)S(1)} %bitcast.481), channel_id=1, replica_groups={{0,2,4,6,8,10,12,14,16,18,20,22,24,26,28,30},{1,3,5,7,9,11,13,15,17,19,..., dimensions={0} | all-to-all | bytes 1310720 | tf_op jit(solution)/shard_map/all_to_all | solution.py:115
  426.6 13.8 %all_to_all.134 = bf16[16,8,2560]{2,1,0:T(8,128)(2,1)S(1)} all-to-all(bf16[16,8,2560]{2,1,0:T(8,128)(2,1)S(1)} %fusion.13), channel_id=1, replica_groups={{0,2,4,6,8,10,12,14,16,18,20,22,24,26,28,30},{1,3,5,7,9,11,13,15,17,19,..., dimensions={0} | all-to-all | bytes 1310720 | tf_op jit(solution)/shard_map/all_to_all | solution.py:115
  449.5 15.2 %all_to_all.135 = bf16[16,8,2560]{2,1,0:T(8,128)(2,1)S(1)} all-to-all(bf16[16,8,2560]{2,1,0:T(8,128)(2,1)S(1)} %bitcast.482), channel_id=1, replica_groups={{0,2,4,6,8,10,12,14,16,18,20,22,24,26,28,30},{1,3,5,7,9,11,13,15,17,19,..., dimensions={0} | all-to-all | bytes 1310720 | tf_op jit(solution)/shard_map/all_to_all | solution.py:115
  471.2 13.8 %all_to_all.136 = bf16[16,8,2560]{2,1,0:T(8,128)(2,1)S(1)} all-to-all(bf16[16,8,2560]{2,1,0:T(8,128)(2,1)S(1)} %fusion.12), channel_id=1, replica_groups={{0,2,4,6,8,10,12,14,16,18,20,22,24,26,28,30},{1,3,5,7,9,11,13,15,17,19,..., dimensions={0} | all-to-all | bytes 1310720 | tf_op jit(solution)/shard_map/all_to_all | solution.py:115
  493.9 15.2 %all_to_all.137 = bf16[16,8,2560]{2,1,0:T(8,128)(2,1)S(1)} all-to-all(bf16[16,8,2560]{2,1,0:T(8,128)(2,1)S(1)} %bitcast.483), channel_id=1, replica_groups={{0,2,4,6,8,10,12,14,16,18,20,22,24,26,28,30},{1,3,5,7,9,11,13,15,17,19,..., dimensions={0} | all-to-all | bytes 1310720 | tf_op jit(solution)/shard_map/all_to_all | solution.py:115
  591.9 7.3 %all-to-all-start.23 = ((bf16[16,8,2560]{2,1,0:T(8,128)(2,1)}), bf16[16,8,2560]{2,1,0:T(8,128)(2,1)}, u32[]{:S(2)}, u32[]{:S(2)}) async-start(bf16[16,8,2560]{2,1,0:T(8,128)(2,1)} %bitcast.474), calls=%async_computation.23 | async-start | bytes 1310720 | tf_op jit(solution)/shard_map/all_to_all | solution.py:115
  (493 shorter events, 312.1 us)
Async XLA Ops:
  6.1 36.5 %all-to-all-start = ((bf16[16,24,2560]{2,1,0:T(8,128)(2,1)}), bf16[16,24,2560]{2,1,0:T(8,128)(2,1)}, u32[]{:S(2)}, u32[]{:S(2)}) async-start(bf16[16,24,2560]{2,1,0:T(8,128)(2,1)} %bitcast.470), calls=%async_computation | async-start | bytes 3932160 | tf_op jit(solution)/shard_map/all_to_all | solution.py:115
  42.6 16.9 %all-to-all-start.1 = ((bf16[8,32,320]{2,1,0:T(8,128)(2,1)}), bf16[8,32,320]{2,1,0:T(8,128)(2,1)S(1)}, u32[]{:S(2)}, u32[]{:S(2)}) async-start(bf16[8,32,320]{2,1,0:T(8,128)(2,1)} %pad_maximum_fusion.3), calls=%async_computation.1 | async-start | bytes 393216 | tf_op jit(solution)/shard_map/all_to_all | solution.py:137
  50.8 32.5 %collective-permute-start.1 = (bf16[384,2560]{1,0:T(8,128)(2,1)}, bf16[384,2560]{1,0:T(8,128)(2,1)}, u32[]{:S(2)}, u32[]{:S(2)}) collective-permute-start(bf16[384,2560]{1,0:T(8,128)(2,1)} %bitcast.3), channel_id=1, source_target_pairs={{0,1},{1,0},{2,3},{3,2},{4,5},{5,4},{6,7},{7,6},{8,9},{9,8},{10,11... | collective-permute-start | bytes 5898248 | tf_op jit(solution)/shard_map/ppermute | solution.py:119
  60.9 15.6 %all-to-all-start.2 = ((bf16[16,8,2560]{2,1,0:T(8,128)(2,1)}), bf16[16,8,2560]{2,1,0:T(8,128)(2,1)S(1)}, u32[]{:S(2)}, u32[]{:S(2)}) async-start(bf16[16,8,2560]{2,1,0:T(8,128)(2,1)} %fusion.21), calls=%async_computation.2 | async-start | bytes 1310720 | tf_op jit(solution)/shard_map/all_to_all | solution.py:115
  76.5 5.8 collective-permute-start
  93.5 16.3 %all-to-all-start.3 = ((bf16[16,8,2560]{2,1,0:T(8,128)(2,1)}), bf16[16,8,2560]{2,1,0:T(8,128)(2,1)S(1)}, u32[]{:S(2)}, u32[]{:S(2)}) async-start(bf16[16,8,2560]{2,1,0:T(8,128)(2,1)} %bitcast.473), calls=%async_computation.3 | async-start | bytes 1310720 | tf_op jit(solution)/shard_map/all_to_all | solution.py:115
  198.7 5.2 collective-permute-start.9
  218.1 5.4 collective-permute-start.10
  242.8 6.0 collective-permute-start.12
  262.9 5.0 collective-permute-start.13
  287.2 5.9 collective-permute-start.15
  307.3 5.0 collective-permute-start.16
  331.7 5.9 collective-permute-start.18
  351.8 5.0 collective-permute-start.19
  376.1 5.9 collective-permute-start.21
  396.1 5.0 collective-permute-start.22
  420.4 5.9 collective-permute-start.24
  440.4 5.2 collective-permute-start.25
  464.9 6.0 collective-permute-start.27
  485.0 5.0 collective-permute-start.28
  511.2 20.5 %collective-permute-start.30 = (bf16[32,2560]{1,0:T(8,128)(2,1)}, bf16[32,2560]{1,0:T(8,128)(2,1)}, u32[]{:S(2)}, u32[]{:S(2)}) collective-permute-start(bf16[32,2560]{1,0:T(8,128)(2,1)} %get-tuple-element.385), channel_id=1, source_target_pairs={{0,224},{32,0},{64,32},{96,64},{128,96},{160,128},{192,160},{224,1... | collective-permute-start | bytes 491528 | tf_op jit(solution)/shard_map/ppermute | solution.py:204
  533.8 45.9 %all-to-all-start.22 = ((bf16[16,8,2560]{2,1,0:T(8,128)(2,1)}), bf16[16,8,2560]{2,1,0:T(8,128)(2,1)}, u32[]{:S(2)}, u32[]{:S(2)}) async-start(bf16[16,8,2560]{2,1,0:T(8,128)(2,1)} %fusion.11), calls=%async_computation.22 | async-start | bytes 1310720 | tf_op jit(solution)/shard_map/all_to_all | solution.py:115
  579.7 5.3 collective-permute-start.31
  591.9 43.9 %all-to-all-start.23 = ((bf16[16,8,2560]{2,1,0:T(8,128)(2,1)}), bf16[16,8,2560]{2,1,0:T(8,128)(2,1)}, u32[]{:S(2)}, u32[]{:S(2)}) async-start(bf16[16,8,2560]{2,1,0:T(8,128)(2,1)} %bitcast.474), calls=%async_computation.23 | async-start | bytes 1310720 | tf_op jit(solution)/shard_map/all_to_all | solution.py:115
  (143 other events, 598.6 us)

commit v4 on v3

--- a/solution.py
+++ b/solution.py
@@ -18,6 +18,10 @@
 
 def dot(left, right, dims=(((1,), (0,)), ((), ()))):
     return lax.dot_general(left, right, dims, preferred_element_type=jnp.float32)
+
+
+def together(*values):
+    return lax.optimization_barrier(values)
 
 
 def slot_tables(routes, gates, experts):
@@ -129,79 +133,111 @@
     pieces = jnp.concatenate([by_group[1:], by_group[: sections - groups], by_group[:1]])
     padded_placing = jnp.concatenate([placing, jnp.zeros_like(placing[:1])])
     padded_gates = jnp.concatenate([slot_gates, jnp.zeros_like(slot_gates[:1])])
-    x_packed, pieces, both_rows, padded_placing, padded_gates, unpacking = (
-        lax.optimization_barrier(
-            (x_packed, pieces, both_rows, padded_placing, padded_gates, unpacking)
-        )
-    )
+    x_packed, pieces, both_rows, padded_placing, padded_gates, unpacking = together(
+        x_packed, pieces, both_rows, padded_placing, padded_gates, unpacking
+    )
+    x_packed_other = swapped(x_packed)
     pieces = lax.all_to_all(pieces, "section", 0, 0, tiled=True)
     arriving = pieces.transpose(1, 0, 2).reshape(GROUP * tokens, width)
 
-    def forward(packed):
-        x = dot(unpacking.reshape(groups * rows, -1), packed).astype(jnp.bfloat16)
+    def unpacked(packed):
+        return dot(unpacking.reshape(groups * rows, -1), packed).astype(jnp.bfloat16)
+
+    def forward(x):
         pre = dot(x, both_rows, COLS_COLS)
         pre_gate, pre_up = pre[:, :hidden], pre[:, hidden:]
         sigmoid = jax.nn.sigmoid(pre_gate)
         swished = pre_gate * sigmoid
         gate_slope = pre_up * (sigmoid * (1.0 + pre_gate * (1.0 - sigmoid)))
         slope = jnp.concatenate([gate_slope, swished], axis=1)
-        act = (swished * pre_up).astype(jnp.bfloat16)
-        return [value.reshape(groups, rows, -1) for value in (x, slope, act)]
-
-    halves = [forward(packed) for packed in (x_packed, swapped(x_packed))]
-    x_halves, slope_halves, act_halves = zip(*halves)
+        return slope, (swished * pre_up).astype(jnp.bfloat16)
 
     def hidden_part(rows_grad, slope):
         d_hidden = dot(rows_grad, down_rows, COLS_COLS)
         return (jnp.concatenate([d_hidden, d_hidden], axis=1) * slope).astype(jnp.bfloat16)
 
-    kept_out, sums = [], None
+    def group_at(tick):
+        return tick - (sections - 1 - section_index)
+
+    def chosen_at(tick):
+        return jnp.clip(group_at(tick), 0, groups - 1)
+
+    x_mine = unpacked(x_packed)
+    arriving, x_mine, x_packed_other = together(arriving, x_mine, x_packed_other)
+
+    kept_out, waiting, sums = [], [], None
     ticks = sections + groups - 1
     for tick in range(ticks):
-        group = tick - (sections - 1 - section_index)
+        group = group_at(tick)
         active = jnp.logical_and(group >= 0, group < groups)
         place = padded_placing[jnp.where(active, group, groups)]
         gate = padded_gates[jnp.where(active, group, groups)]
-        chosen = jnp.clip(group, 0, groups - 1)
-        slopes = [
-            lax.dynamic_index_in_dim(value, chosen, 0, keepdims=False) for value in slope_halves
-        ]
-        if tick > 0:
-            arriving, place, gate, slopes = lax.optimization_barrier(
-                (arriving, place, gate, slopes)
-            )
-        rows_mine = across((dot(place, arriving) * gate[:, None]).astype(jnp.bfloat16))
+        chosen = chosen_at(tick)
+        arriving, place, gate = together(arriving, place, gate)
+        rows_out = (dot(place, arriving) * gate[:, None]).astype(jnp.bfloat16)
+
+        if tick == 0:
+            rows_out, x_mine, x_packed_other = together(rows_out, x_mine, x_packed_other)
+            came = across(rows_out)
+            x_other = unpacked(x_packed_other)
+            slopes = [forward(value[:rows])[0] for value in (x_mine, x_other)]
+            came, slopes, x_mine, x_other = together(came, slopes, x_mine, x_other)
+        else:
+            rows_out, waiting, chosen = together(rows_out, waiting, chosen)
+            came = across(rows_out)
+            slopes = [
+                lax.dynamic_index_in_dim(value, chosen, 0, keepdims=False)
+                for value in slope_halves
+            ]
+            if tick > 1:
+                for held in waiting:
+                    sums = add_weight_grads(*held, x_halves, act_halves, sums, False, batches)
+                waiting = []
+                came, slopes, sums = together(came, slopes, sums)
+            else:
+                came, slopes = together(came, slopes)
+
+        rows_mine = came
         rows_other = swapped(rows_mine)
         d_mine = hidden_part(rows_mine, slopes[0])
-        d_mine, rows_other = lax.optimization_barrier((d_mine, rows_other))
+        d_mine, rows_other = together(d_mine, rows_other)
         d_other = hidden_part(rows_other, slopes[1])
         part_other = dot(d_other, both_rows).astype(jnp.bfloat16)
         from_other = swapped(part_other)
         part_mine = dot(d_mine, both_rows).astype(jnp.bfloat16)
-        part_mine, from_other = lax.optimization_barrier((part_mine, from_other))
+        part_mine, from_other = together(part_mine, from_other)
         summed = part_mine.astype(jnp.float32) + from_other.astype(jnp.float32)
         summed = summed.astype(jnp.bfloat16)
+        waiting.append((chosen, (d_mine, d_other), (rows_mine, rows_other)))
+        if tick == 0:
+            summed, x_mine, x_other = together(summed, x_mine, x_other)
+            slope_halves, act_halves = zip(*(forward(value) for value in (x_mine, x_other)))
+            slope_halves, act_halves, x_halves = [
+                [value.reshape(groups, rows, -1) for value in values]
+                for values in (slope_halves, act_halves, (x_mine, x_other))
+            ]
         if tick == ticks - 1:
+            summed, waiting, kept_out = together(summed, waiting, kept_out)
             results = lax.dynamic_slice_in_dim(
                 jnp.concatenate(kept_out + [arriving]),
                 (sections - 1 - section_index) * GROUP * tokens,
                 batches * tokens,
                 axis=0,
             )
-            summed, results = lax.optimization_barrier((summed, results))
-        summed, grads, row_halves = lax.optimization_barrier(
-            (summed, (d_mine, d_other), (rows_mine, rows_other))
-        )
-        sums = add_weight_grads(
-            chosen, grads, row_halves, x_halves, act_halves, sums, tick == ticks - 1, batches
-        )
         returned = across(summed)
+        if tick == ticks - 1:
+            sums = add_weight_grads(*waiting[0], x_halves, act_halves, sums, True, batches)
+            returned, sums, results = together(returned, sums, results)
         outgoing = (arriving.astype(jnp.float32) + dot(place, returned, ROWS_ROWS)).astype(
             jnp.bfloat16
         )
         if tick < ticks - 1:
             kept_out.append(outgoing)
             arriving = lax.ppermute(outgoing, "section", ring)
+        if tick == 0:
+            arriving, slope_halves, act_halves, x_halves = together(
+                arriving, slope_halves, act_halves, x_halves
+            )
 
     last = results[-GROUP * tokens :]
     last = jnp.where(section_index == 0, outgoing, last)

time: 650 us -> 776 us (1.19)
  local copies, waits for them, and re-layouts: 65.3 us -> 220 us
  blocking collectives: 263 us -> 169 us
  matrix products: 63.9 us -> 89.3 us
  starting transfers between devices: 108 us -> 130 us
  other arithmetic: 13.2 us -> 21.3 us
    unnamed x259 -> x473, local copies, waits for them, and re-layouts: 51.7 us -> 182 us
    all_to_all x18 -> x9, blocking collectives: 263 us -> 169 us  [across(): lax.all_to_all(shaped, 'expert', 0, 0, axis_index_groups=same_core, tiled...]
    all_to_all x5 -> x14, starting transfers between devices: 28.2 us -> 62.9 us  [across(): lax.all_to_all(shaped, 'expert', 0, 0, axis_index_groups=same_core, tiled...]
    squeeze x2 -> x20, local copies, waits for them, and re-layouts: 8.33 us -> 36.2 us  [on_device(): lax.dynamic_index_in_dim(value, chosen, 0, keepdims=False)]
    dot_general x71 -> x73, matrix products: 63.9 us -> 89.3 us  [dot(): lax.dot_general(left, right, dims, preferred_element_type=jnp.float32)]
    ppermute x23, starting transfers between devices: 41.2 us -> 30.2 us  [swapped(): return lax.ppermute(value, 'expert', swap)]
    all_to_all x5 -> x14, waiting for transfers between devices: 34.9 us -> 34.7 us  [across(): lax.all_to_all(shaped, 'expert', 0, 0, axis_index_groups=same_core, tiled...]
  transfers between devices with their start and end apart: 39 -> 48, of which waited for: 31 -> 32; matrix products, arithmetic and copies ran while one was open for 8% -> 14% of each run, Pallas kernels for 8% -> 7%
where the time goes in v4:
time: 776 us; the launch traced here: 763 us
  local copies, waits for them, and re-layouts  220 us (28%)
  blocking collectives  169 us (22%)
  starting transfers between devices  130 us (17%)
  matrix products  89.3 us (12%)
  waiting for transfers between devices  79.5 us (10%)
  Pallas kernels  50.1 us (6%)
  other arithmetic  21.3 us (3%)
    unnamed x473, local copies, waits for them, and re-layouts  182 us
    all_to_all x9, blocking collectives, across(): lax.all_to_all(shaped, 'expert', 0, 0, axis_index_groups=same_core, tiled...  169 us
    dot_general x73, matrix products, dot(): lax.dot_general(left, right, dims, preferred_element_type=jnp.float32)  89.3 us
    all_to_all x14, starting transfers between devices, across(): lax.all_to_all(shaped, 'expert', 0, 0, axis_index_groups=same_core, tiled...  62.9 us
    pallas_call x11, Pallas kernels, add_weight_grads(): pl.pallas_call(partial(add_kernel, first, final, batches), grid_spec=pltp...  50.1 us
    squeeze x20, local copies, waits for them, and re-layouts, on_device(): lax.dynamic_index_in_dim(value, chosen, 0, keepdims=False)  36.2 us
    all_to_all x14, waiting for transfers between devices, across(): lax.all_to_all(shaped, 'expert', 0, 0, axis_index_groups=same_core, tiled...  34.7 us
    ppermute x23, starting transfers between devices, swapped(): return lax.ppermute(value, 'expert', swap)  30.2 us
  transfers between devices with their start and end apart: 48, of which 32 were waited for; matrix products, arithmetic and copies ran while one was open for 14% of the time, Pallas kernels for 7%

profile of v4, /device:TPU:1, one launch (start us, length us, event | category | flops | bytes accessed | tf_op | source)
XLA Modules:
  0.0 762.9 jit_solution(1602567482409732592)
XLA Ops:
  6.1 7.8 %all-to-all-start = ((bf16[16,24,2560]{2,1,0:T(8,128)(2,1)}), bf16[16,24,2560]{2,1,0:T(8,128)(2,1)}, u32[]{:S(2)}, u32[]{:S(2)}) async-start(bf16[16,24,2560]{2,1,0:T(8,128)(2,1)} %bitcast.466), calls=%async_computation | async-start | bytes 3932160 | tf_op jit(solution)/shard_map/all_to_all | solution.py:119
  20.0 22.5 %all-to-all-done = bf16[16,24,2560]{2,1,0:T(8,128)(2,1)} async-done(((bf16[16,24,2560]{2,1,0:T(8,128)(2,1)}), bf16[16,24,2560]{2,1,0:T(8,128)(2,1)}, u32[]{:S(2)}, u32[]{:S(2)}) %all-to-all-start) | async-done | bytes 1966112 | tf_op jit(solution)/shard_map/all_to_all | solution.py:119
  44.7 8.2 %all-to-all-start.1 = ((bf16[8,32,320]{2,1,0:T(8,128)(2,1)}), bf16[8,32,320]{2,1,0:T(8,128)(2,1)S(1)}, u32[]{:S(2)}, u32[]{:S(2)}) async-start(bf16[8,32,320]{2,1,0:T(8,128)(2,1)} %pad_maximum_fusion.5), calls=%async_computation.1 | async-start | bytes 393216 | tf_op jit(solution)/shard_map/all_to_all | solution.py:140
  54.1 4.6 convolution_convert_fusion.1
  58.7 5.0 all-to-all-done.1
  96.7 5.3 fusion.147
  116.6 5.6 all-to-all-start.4
  125.8 7.5 all-to-all-done.4
  142.5 15.2 %all_to_all.120 = bf16[16,8,2560]{2,1,0:T(8,128)(2,1)S(1)} all-to-all(bf16[16,8,2560]{2,1,0:T(8,128)(2,1)S(1)} %fusion.60), channel_id=1, replica_groups={{0,2,4,6,8,10,12,14,16,18,20,22,24,26,28,30},{1,3,5,7,9,11,13,15,17,19,..., dimensions={0} | all-to-all | bytes 1310720 | tf_op jit(solution)/shard_map/all_to_all | solution.py:119
  179.9 4.5 shard_map.103
  198.9 19.3 %all_to_all.121 = bf16[16,8,2560]{2,1,0:T(8,128)(2,1)S(1)} all-to-all(bf16[16,8,2560]{2,1,0:T(8,128)(2,1)S(1)} %fusion.61), channel_id=1, replica_groups={{0,2,4,6,8,10,12,14,16,18,20,22,24,26,28,30},{1,3,5,7,9,11,13,15,17,19,..., dimensions={0} | all-to-all | bytes 1310720 | tf_op jit(solution)/shard_map/all_to_all | solution.py:119
  246.1 4.5 shard_map.104
  265.7 19.2 %all_to_all.122 = bf16[16,8,2560]{2,1,0:T(8,128)(2,1)S(1)} all-to-all(bf16[16,8,2560]{2,1,0:T(8,128)(2,1)S(1)} %fusion.62), channel_id=1, replica_groups={{0,2,4,6,8,10,12,14,16,18,20,22,24,26,28,30},{1,3,5,7,9,11,13,15,17,19,..., dimensions={0} | all-to-all | bytes 1310720 | tf_op jit(solution)/shard_map/all_to_all | solution.py:119
  312.0 4.9 shard_map.105
  331.4 19.3 %all_to_all.123 = bf16[16,8,2560]{2,1,0:T(8,128)(2,1)S(1)} all-to-all(bf16[16,8,2560]{2,1,0:T(8,128)(2,1)S(1)} %fusion.63), channel_id=1, replica_groups={{0,2,4,6,8,10,12,14,16,18,20,22,24,26,28,30},{1,3,5,7,9,11,13,15,17,19,..., dimensions={0} | all-to-all | bytes 1310720 | tf_op jit(solution)/shard_map/all_to_all | solution.py:119
  398.9 19.2 %all_to_all.124 = bf16[16,8,2560]{2,1,0:T(8,128)(2,1)S(1)} all-to-all(bf16[16,8,2560]{2,1,0:T(8,128)(2,1)S(1)} %fusion.64), channel_id=1, replica_groups={{0,2,4,6,8,10,12,14,16,18,20,22,24,26,28,30},{1,3,5,7,9,11,13,15,17,19,..., dimensions={0} | all-to-all | bytes 1310720 | tf_op jit(solution)/shard_map/all_to_all | solution.py:119
  445.1 4.9 shard_map.107
  464.3 19.1 %all_to_all.125 = bf16[16,8,2560]{2,1,0:T(8,128)(2,1)S(1)} all-to-all(bf16[16,8,2560]{2,1,0:T(8,128)(2,1)S(1)} %fusion.65), channel_id=1, replica_groups={{0,2,4,6,8,10,12,14,16,18,20,22,24,26,28,30},{1,3,5,7,9,11,13,15,17,19,..., dimensions={0} | all-to-all | bytes 1310720 | tf_op jit(solution)/shard_map/all_to_all | solution.py:119
  528.2 19.2 %all_to_all.126 = bf16[16,8,2560]{2,1,0:T(8,128)(2,1)S(1)} all-to-all(bf16[16,8,2560]{2,1,0:T(8,128)(2,1)S(1)} %fusion.66), channel_id=1, replica_groups={{0,2,4,6,8,10,12,14,16,18,20,22,24,26,28,30},{1,3,5,7,9,11,13,15,17,19,..., dimensions={0} | all-to-all | bytes 1310720 | tf_op jit(solution)/shard_map/all_to_all | solution.py:119
  595.9 19.2 %all_to_all.127 = bf16[16,8,2560]{2,1,0:T(8,128)(2,1)S(1)} all-to-all(bf16[16,8,2560]{2,1,0:T(8,128)(2,1)S(1)} %fusion.67), channel_id=1, replica_groups={{0,2,4,6,8,10,12,14,16,18,20,22,24,26,28,30},{1,3,5,7,9,11,13,15,17,19,..., dimensions={0} | all-to-all | bytes 1310720 | tf_op jit(solution)/shard_map/all_to_all | solution.py:119
  642.2 4.9 shard_map.110
  661.3 19.1 %all_to_all.128 = bf16[16,8,2560]{2,1,0:T(8,128)(2,1)S(1)} all-to-all(bf16[16,8,2560]{2,1,0:T(8,128)(2,1)S(1)} %fusion.68), channel_id=1, replica_groups={{0,2,4,6,8,10,12,14,16,18,20,22,24,26,28,30},{1,3,5,7,9,11,13,15,17,19,..., dimensions={0} | all-to-all | bytes 1310720 | tf_op jit(solution)/shard_map/all_to_all | solution.py:119
  728.9 6.9 all-to-all-start.23
  755.3 4.9 shard_map.112
  (740 shorter events, 488.6 us)
Async XLA Ops:
  6.1 36.5 %all-to-all-start = ((bf16[16,24,2560]{2,1,0:T(8,128)(2,1)}), bf16[16,24,2560]{2,1,0:T(8,128)(2,1)}, u32[]{:S(2)}, u32[]{:S(2)}) async-start(bf16[16,24,2560]{2,1,0:T(8,128)(2,1)} %bitcast.466), calls=%async_computation | async-start | bytes 3932160 | tf_op jit(solution)/shard_map/all_to_all | solution.py:119
  42.6 21.4 %collective-permute-start = (bf16[384,2560]{1,0:T(8,128)(2,1)}, bf16[384,2560]{1,0:T(8,128)(2,1)}, u32[]{:S(2)}, u32[]{:S(2)}) collective-permute-start(bf16[384,2560]{1,0:T(8,128)(2,1)} %bitcast.3), channel_id=1, source_target_pairs={{0,1},{1,0},{2,3},{3,2},{4,5},{5,4},{6,7},{7,6},{8,9},{9,8},{10,11... | collective-permute-start | bytes 5898248 | tf_op jit(solution)/shard_map/ppermute | solution.py:123
  44.7 19.0 %all-to-all-start.1 = ((bf16[8,32,320]{2,1,0:T(8,128)(2,1)}), bf16[8,32,320]{2,1,0:T(8,128)(2,1)S(1)}, u32[]{:S(2)}, u32[]{:S(2)}) async-start(bf16[8,32,320]{2,1,0:T(8,128)(2,1)} %pad_maximum_fusion.5), calls=%async_computation.1 | async-start | bytes 393216 | tf_op jit(solution)/shard_map/all_to_all | solution.py:140
  65.1 15.7 %all-to-all-start.2 = ((bf16[16,8,2560]{2,1,0:T(8,128)(2,1)}), bf16[16,8,2560]{2,1,0:T(8,128)(2,1)S(1)}, u32[]{:S(2)}, u32[]{:S(2)}) async-start(bf16[16,8,2560]{2,1,0:T(8,128)(2,1)} %bitcast.471), calls=%async_computation.2 | async-start | bytes 1310720 | tf_op jit(solution)/shard_map/all_to_all | solution.py:119
  92.2 16.7 %all-to-all-start.3 = ((bf16[16,8,2560]{2,1,0:T(8,128)(2,1)}), bf16[16,8,2560]{2,1,0:T(8,128)(2,1)}, u32[]{:S(2)}, u32[]{:S(2)}) async-start(bf16[16,8,2560]{2,1,0:T(8,128)(2,1)} %bitcast.16), calls=%async_computation.3 | async-start | bytes 1310720 | tf_op jit(solution)/shard_map/all_to_all | solution.py:119
  116.6 16.8 %all-to-all-start.4 = ((bf16[16,8,2560]{2,1,0:T(8,128)(2,1)}), bf16[16,8,2560]{2,1,0:T(8,128)(2,1)S(1)}, u32[]{:S(2)}, u32[]{:S(2)}) async-start(bf16[16,8,2560]{2,1,0:T(8,128)(2,1)} %bitcast.479), calls=%async_computation.4 | async-start | bytes 1310720 | tf_op jit(solution)/shard_map/all_to_all | solution.py:119
  163.4 26.7 %all-to-all-start.6 = ((bf16[16,8,2560]{2,1,0:T(8,128)(2,1)}), bf16[16,8,2560]{2,1,0:T(8,128)(2,1)S(1)}, u32[]{:S(2)}, u32[]{:S(2)}) async-start(bf16[16,8,2560]{2,1,0:T(8,128)(2,1)} %bitcast.469), calls=%async_computation.6 | async-start | bytes 1310720 | tf_op jit(solution)/shard_map/all_to_all | solution.py:119
  219.1 5.3 collective-permute-start.9
  226.5 29.7 %all-to-all-start.8 = ((bf16[16,8,2560]{2,1,0:T(8,128)(2,1)}), bf16[16,8,2560]{2,1,0:T(8,128)(2,1)}, u32[]{:S(2)}, u32[]{:S(2)}) async-start(bf16[16,8,2560]{2,1,0:T(8,128)(2,1)} %bitcast.472), calls=%async_computation.8 | async-start | bytes 1310720 | tf_op jit(solution)/shard_map/all_to_all | solution.py:119
  286.1 5.7 collective-permute-start.12
  293.1 29.5 %all-to-all-start.10 = ((bf16[16,8,2560]{2,1,0:T(8,128)(2,1)}), bf16[16,8,2560]{2,1,0:T(8,128)(2,1)S(1)}, u32[]{:S(2)}, u32[]{:S(2)}) async-start(bf16[16,8,2560]{2,1,0:T(8,128)(2,1)} %bitcast.473), calls=%async_computation.10 | async-start | bytes 1310720 | tf_op jit(solution)/shard_map/all_to_all | solution.py:119
  351.5 6.0 collective-permute-start.15
  359.6 29.7 %all-to-all-start.12 = ((bf16[16,8,2560]{2,1,0:T(8,128)(2,1)}), bf16[16,8,2560]{2,1,0:T(8,128)(2,1)}, u32[]{:S(2)}, u32[]{:S(2)}) async-start(bf16[16,8,2560]{2,1,0:T(8,128)(2,1)} %bitcast.474), calls=%async_computation.12 | async-start | bytes 1310720 | tf_op jit(solution)/shard_map/all_to_all | solution.py:119
  419.2 5.8 collective-permute-start.18
  426.2 29.5 %all-to-all-start.14 = ((bf16[16,8,2560]{2,1,0:T(8,128)(2,1)}), bf16[16,8,2560]{2,1,0:T(8,128)(2,1)S(1)}, u32[]{:S(2)}, u32[]{:S(2)}) async-start(bf16[16,8,2560]{2,1,0:T(8,128)(2,1)} %bitcast.475), calls=%async_computation.14 | async-start | bytes 1310720 | tf_op jit(solution)/shard_map/all_to_all | solution.py:119
  483.6 5.8 collective-permute-start.21
  490.6 29.1 %all-to-all-start.16 = ((bf16[16,8,2560]{2,1,0:T(8,128)(2,1)}), bf16[16,8,2560]{2,1,0:T(8,128)(2,1)S(1)}, u32[]{:S(2)}, u32[]{:S(2)}) async-start(bf16[16,8,2560]{2,1,0:T(8,128)(2,1)} %bitcast.476), calls=%async_computation.16 | async-start | bytes 1310720 | tf_op jit(solution)/shard_map/all_to_all | solution.py:119
  548.3 6.0 collective-permute-start.24
  556.4 29.7 %all-to-all-start.18 = ((bf16[16,8,2560]{2,1,0:T(8,128)(2,1)}), bf16[16,8,2560]{2,1,0:T(8,128)(2,1)}, u32[]{:S(2)}, u32[]{:S(2)}) async-start(bf16[16,8,2560]{2,1,0:T(8,128)(2,1)} %bitcast.477), calls=%async_computation.18 | async-start | bytes 1310720 | tf_op jit(solution)/shard_map/all_to_all | solution.py:119
  616.3 5.7 collective-permute-start.27
  623.2 29.5 %all-to-all-start.20 = ((bf16[16,8,2560]{2,1,0:T(8,128)(2,1)}), bf16[16,8,2560]{2,1,0:T(8,128)(2,1)S(1)}, u32[]{:S(2)}, u32[]{:S(2)}) async-start(bf16[16,8,2560]{2,1,0:T(8,128)(2,1)} %bitcast.478), calls=%async_computation.20 | async-start | bytes 1310720 | tf_op jit(solution)/shard_map/all_to_all | solution.py:119
  680.6 5.8 collective-permute-start.30
  687.5 29.1 %all-to-all-start.22 = ((bf16[16,8,2560]{2,1,0:T(8,128)(2,1)}), bf16[16,8,2560]{2,1,0:T(8,128)(2,1)S(1)}, u32[]{:S(2)}, u32[]{:S(2)}) async-start(bf16[16,8,2560]{2,1,0:T(8,128)(2,1)} %bitcast.470), calls=%async_computation.22 | async-start | bytes 1310720 | tf_op jit(solution)/shard_map/all_to_all | solution.py:119
  728.9 31.3 %all-to-all-start.23 = ((bf16[16,8,2560]{2,1,0:T(8,128)(2,1)}), bf16[16,8,2560]{2,1,0:T(8,128)(2,1)}, u32[]{:S(2)}, u32[]{:S(2)}) async-start(bf16[16,8,2560]{2,1,0:T(8,128)(2,1)} %bitcast.480), calls=%async_computation.23 | async-start | bytes 1310720 | tf_op jit(solution)/shard_map/all_to_all | solution.py:119
  (254 other events, 1234.1 us)

commit v5 on v4

--- a/solution.py
+++ b/solution.py
@@ -11,6 +11,7 @@
 GROUP = 2
 ROOM = 4
 CAP = 3
+CHUNKS = 2
 
 ROWS_ROWS = (((0,), (0,)), ((), ()))
 COLS_COLS = (((1,), (1,)), ((), ()))
@@ -51,53 +52,121 @@
     return placing, jnp.sum(gate, axis=(2, 3)), packing, unpacking
 
 
-def add_kernel(first, final, batches, chosen, *refs):
-    d_halves, row_halves, x_halves, act_halves = refs[:2], refs[2:4], refs[4:6], refs[6:8]
-    before, after = (None, refs[8:11]) if first else (refs[8:11], refs[11:14])
-    hidden = after[0].shape[0]
-
-    def product(lefts, rights):
-        left = jnp.concatenate(lefts, axis=0)
-        right = jnp.concatenate(rights, axis=0)
-        return dot(left, right, ROWS_ROWS)
-
-    both = product([d[...] for d in d_halves], [x[0] for x in x_halves])
-    down = product([act[0] for act in act_halves], [value[...] for value in row_halves])
-    for i, term in enumerate((both[:hidden], both[hidden:], down)):
-        total = term if first else before[i][...] + term
-        after[i][...] = (total / batches).astype(jnp.bfloat16) if final else total
-
-
-def add_weight_grads(chosen, d_halves, row_halves, x_halves, act_halves, sums, final, batches):
-    rows, width = row_halves[0].shape
+def grads_kernel(sections, batches, first_ref, *refs):
+    groups = refs[-5].shape[0]
+    ticks = sections + groups - 1
+    kept = [refs[4 * t : 4 * t + 4] for t in range(ticks)]
+    x_halves, act_halves = refs[4 * ticks : 4 * ticks + 2], refs[4 * ticks + 2 : 4 * ticks + 4]
+    outs = refs[4 * ticks + 4 : 4 * ticks + 7]
+    d_buf, act_buf, rows_buf, x_buf, sems = refs[-5:]
+    chunk = rows_buf.shape[-1]
+    hidden = act_buf.shape[-1]
+    step = pl.program_id(0)
+    pairs = [(g, h) for g in range(groups) for h in range(SPLIT)]
+
+    def columns(c):
+        return pl.ds(c * chunk, chunk)
+
+    def d_copies(first):
+        return [
+            pltpu.make_async_copy(kept[first + g][h], d_buf.at[g, h], sems.at[g * SPLIT + h])
+            for g, h in pairs
+        ]
+
+    def act_copies():
+        at = len(pairs)
+        return [
+            pltpu.make_async_copy(act_halves[h], act_buf.at[:, h], sems.at[at + h])
+            for h in range(SPLIT)
+        ]
+
+    def x_copies(c):
+        at = len(pairs) + SPLIT + c * SPLIT
+        return [
+            pltpu.make_async_copy(
+                x_halves[h].at[:, :, columns(c)], x_buf.at[c, :, h], sems.at[at + h]
+            )
+            for h in range(SPLIT)
+        ]
+
+    def row_copies(c, first):
+        at = len(pairs) + SPLIT + CHUNKS * SPLIT + c * len(pairs)
+        return [
+            pltpu.make_async_copy(
+                kept[first + g][SPLIT + h].at[:, columns(c)],
+                rows_buf.at[c, g, h],
+                sems.at[at + g * SPLIT + h],
+            )
+            for g, h in pairs
+        ]
+
+    @pl.when(step == 0)
+    def start():
+        for copy in x_copies(0) + act_copies():
+            copy.start()
+        for first in range(sections):
+
+            @pl.when(first_ref[0] == first)
+            def start_kept():
+                copies = d_copies(first)
+                for c in range(CHUNKS):
+                    copies = copies + row_copies(c, first)
+                for copy in copies:
+                    copy.start()
+
+        for c in range(1, CHUNKS):
+            for copy in x_copies(c):
+                copy.start()
+        for copy in d_copies(0) + act_copies():
+            copy.wait()
+
+    def merged(value):
+        return value.reshape(-1, value.shape[-1])
+
+    for c in range(CHUNKS):
+
+        @pl.when(step == c)
+        def compute():
+            for copy in x_copies(c) + row_copies(c, 0):
+                copy.wait()
+            both = dot(merged(d_buf[...]), merged(x_buf[c]), ROWS_ROWS) / batches
+            outs[0][...] = both[:hidden].astype(jnp.bfloat16)
+            outs[1][...] = both[hidden:].astype(jnp.bfloat16)
+            down = dot(merged(act_buf[...]), merged(rows_buf[c]), ROWS_ROWS) / batches
+            outs[2][...] = down.astype(jnp.bfloat16)
+
+
+def weight_grads(first, kept, x_halves, act_halves, sections, batches):
+    groups, rows, width = x_halves[0].shape
     hidden = act_halves[0].shape[2]
-    tile = 512 if width % 512 == 0 else width
-    whole = pl.BlockSpec((rows, 2 * hidden), lambda n, at: (0, 0))
-    row_tile = pl.BlockSpec((rows, tile), lambda n, at: (0, n))
-    x_tile = pl.BlockSpec((1, rows, tile), lambda n, at: (at[0], 0, n))
-    act_tile = pl.BlockSpec((1, rows, hidden), lambda n, at: (at[0], 0, 0))
-    sum_tile = pl.BlockSpec((hidden, tile), lambda n, at: (0, n))
-    first = sums is None
-    held = [] if first else list(sums)
-    aliases = {} if first or final else {9 + i: i for i in range(3)}
-    held_as = jnp.bfloat16 if final else jnp.float32
-    flops = 2 * 3 * SPLIT * rows * hidden * width
+    chunk = width // CHUNKS
+    operands = [value for tick in kept for value in tick] + list(x_halves) + list(act_halves)
+    anywhere = pl.BlockSpec(memory_space=pl.ANY)
+    copies = (1 + CHUNKS) * (groups + 1) * SPLIT
+    halves = (groups, SPLIT, rows)
+    work = groups * SPLIT * rows * width
     return pl.pallas_call(
-        partial(add_kernel, first, final, batches),
+        partial(grads_kernel, sections, batches),
         grid_spec=pltpu.PrefetchScalarGridSpec(
             num_scalar_prefetch=1,
-            grid=(width // tile,),
-            in_specs=[whole] * 2 + [row_tile] * 2 + [x_tile] * 2 + [act_tile] * 2
-            + [sum_tile] * len(held),
-            out_specs=[sum_tile] * 3,
+            grid=(CHUNKS,),
+            in_specs=[anywhere] * len(operands),
+            out_specs=[pl.BlockSpec((hidden, chunk), lambda n, first: (0, n))] * 3,
+            scratch_shapes=[
+                pltpu.VMEM(halves + (2 * hidden,), jnp.bfloat16),
+                pltpu.VMEM(halves + (hidden,), jnp.bfloat16),
+                pltpu.VMEM((CHUNKS,) + halves + (chunk,), jnp.bfloat16),
+                pltpu.VMEM((CHUNKS,) + halves + (chunk,), jnp.bfloat16),
+                pltpu.SemaphoreType.DMA((copies,)),
+            ],
         ),
-        out_shape=[jax.ShapeDtypeStruct((hidden, width), held_as)] * 3,
-        input_output_aliases=aliases,
-        compiler_params=pltpu.CompilerParams(vmem_limit_bytes=24 * 1024 * 1024),
+        out_shape=[jax.ShapeDtypeStruct((hidden, width), jnp.bfloat16)] * 3,
+        compiler_params=pltpu.CompilerParams(vmem_limit_bytes=56 * 1024 * 1024),
         cost_estimate=pl.CostEstimate(
-            flops=flops, bytes_accessed=6 * 4 * hidden * width, transcendentals=0
+            flops=6 * work * hidden, bytes_accessed=4 * work + 6 * hidden * width,
+            transcendentals=0,
         ),
-    )(jnp.reshape(chosen, (1,)), *d_halves, *row_halves, *x_halves, *act_halves, *held)
+    )(jnp.reshape(first, (1,)), *operands)
 
 
 def on_device(x_saved, routes, gates, cotangent, w_gate, w_up, w_down):
@@ -165,39 +234,27 @@
     x_mine = unpacked(x_packed)
     arriving, x_mine, x_packed_other = together(arriving, x_mine, x_packed_other)
 
-    kept_out, waiting, sums = [], [], None
+    kept_out, kept = [], []
     ticks = sections + groups - 1
     for tick in range(ticks):
         group = group_at(tick)
         active = jnp.logical_and(group >= 0, group < groups)
         place = padded_placing[jnp.where(active, group, groups)]
         gate = padded_gates[jnp.where(active, group, groups)]
-        chosen = chosen_at(tick)
-        arriving, place, gate = together(arriving, place, gate)
-        rows_out = (dot(place, arriving) * gate[:, None]).astype(jnp.bfloat16)
-
         if tick == 0:
+            rows_out = (dot(place, arriving) * gate[:, None]).astype(jnp.bfloat16)
             rows_out, x_mine, x_packed_other = together(rows_out, x_mine, x_packed_other)
             came = across(rows_out)
             x_other = unpacked(x_packed_other)
             slopes = [forward(value[:rows])[0] for value in (x_mine, x_other)]
-            came, slopes, x_mine, x_other = together(came, slopes, x_mine, x_other)
+            rows_mine, slopes, x_mine, x_other = together(came, slopes, x_mine, x_other)
         else:
-            rows_out, waiting, chosen = together(rows_out, waiting, chosen)
-            came = across(rows_out)
             slopes = [
-                lax.dynamic_index_in_dim(value, chosen, 0, keepdims=False)
+                lax.dynamic_index_in_dim(value, chosen_at(tick), 0, keepdims=False)
                 for value in slope_halves
             ]
-            if tick > 1:
-                for held in waiting:
-                    sums = add_weight_grads(*held, x_halves, act_halves, sums, False, batches)
-                waiting = []
-                came, slopes, sums = together(came, slopes, sums)
-            else:
-                came, slopes = together(came, slopes)
-
-        rows_mine = came
+            arriving, place, gate, slopes = together(arriving, place, gate, slopes)
+            rows_mine = across((dot(place, arriving) * gate[:, None]).astype(jnp.bfloat16))
         rows_other = swapped(rows_mine)
         d_mine = hidden_part(rows_mine, slopes[0])
         d_mine, rows_other = together(d_mine, rows_other)
@@ -208,7 +265,6 @@
         part_mine, from_other = together(part_mine, from_other)
         summed = part_mine.astype(jnp.float32) + from_other.astype(jnp.float32)
         summed = summed.astype(jnp.bfloat16)
-        waiting.append((chosen, (d_mine, d_other), (rows_mine, rows_other)))
         if tick == 0:
             summed, x_mine, x_other = together(summed, x_mine, x_other)
             slope_halves, act_halves = zip(*(forward(value) for value in (x_mine, x_other)))
@@ -217,32 +273,32 @@
                 for values in (slope_halves, act_halves, (x_mine, x_other))
             ]
         if tick == ticks - 1:
-            summed, waiting, kept_out = together(summed, waiting, kept_out)
+            first = sections - 1 - section_index
+            summed, d_mine, d_other, rows_mine, rows_other, first = together(
+                summed, d_mine, d_other, rows_mine, rows_other, first
+            )
+        kept.append((d_mine, d_other, rows_mine, rows_other))
+        returned = across(summed)
+        if tick == ticks - 1:
+            grads = weight_grads(first, kept, x_halves, act_halves, sections, batches)
             results = lax.dynamic_slice_in_dim(
                 jnp.concatenate(kept_out + [arriving]),
-                (sections - 1 - section_index) * GROUP * tokens,
+                first * (GROUP * tokens),
                 batches * tokens,
                 axis=0,
             )
-        returned = across(summed)
-        if tick == ticks - 1:
-            sums = add_weight_grads(*waiting[0], x_halves, act_halves, sums, True, batches)
-            returned, sums, results = together(returned, sums, results)
+            returned, results, grads = together(returned, results, grads)
         outgoing = (arriving.astype(jnp.float32) + dot(place, returned, ROWS_ROWS)).astype(
             jnp.bfloat16
         )
         if tick < ticks - 1:
             kept_out.append(outgoing)
             arriving = lax.ppermute(outgoing, "section", ring)
-        if tick == 0:
-            arriving, slope_halves, act_halves, x_halves = together(
-                arriving, slope_halves, act_halves, x_halves
-            )
 
     last = results[-GROUP * tokens :]
     last = jnp.where(section_index == 0, outgoing, last)
     results = lax.dynamic_update_slice(results, last, (results.shape[0] - GROUP * tokens, 0))
-    return (results.reshape(1, batches, tokens, width),) + tuple(g[None] for g in sums)
+    return (results.reshape(1, batches, tokens, width),) + tuple(g[None] for g in grads)
 
 
 def solution(mesh):

time: 776 us -> 574 us (0.74)
  local copies, waits for them, and re-layouts: 220 us -> 16.4 us
  blocking collectives: 169 us -> 280 us
  Pallas kernels: 50.1 us -> 11.7 us
  starting transfers between devices: 130 us -> 98.4 us
  matrix products: 89.3 us -> 65 us
    unnamed x473 -> x185, local copies, waits for them, and re-layouts: 182 us -> 9.2 us
    all_to_all x9 -> x19, blocking collectives: 169 us -> 280 us  [across(): lax.all_to_all(shaped, 'expert', 0, 0, axis_index_groups=same_core, tiled...]
    all_to_all x14 -> x4, starting transfers between devices: 62.9 us -> 19.4 us  [across(): lax.all_to_all(shaped, 'expert', 0, 0, axis_index_groups=same_core, tiled...]
    pallas_call x11 -> x1, Pallas kernels: 50.1 us -> 11.7 us  [weight_grads(): pl.pallas_call(partial(grads_kernel, sections, batches), grid_spec=pltpu....]
    squeeze x20 -> x2, local copies, waits for them, and re-layouts: 36.2 us -> 3 us  [on_device(): lax.dynamic_index_in_dim(value, chosen_at(tick), 0, keepdims=False)]
    dot_general x73, matrix products: 89.3 us -> 65 us  [dot(): lax.dot_general(left, right, dims, preferred_element_type=jnp.float32)]
    ppermute x23, starting transfers between devices: 30.2 us -> 40.7 us  [swapped(): return lax.ppermute(value, 'expert', swap)]
    all_to_all x14 -> x4, waiting for transfers between devices: 34.7 us -> 25.2 us  [across(): lax.all_to_all(shaped, 'expert', 0, 0, axis_index_groups=same_core, tiled...]
  transfers between devices with their start and end apart: 48 -> 38, of which waited for: 32 -> 34; matrix products, arithmetic and copies ran while one was open for 14% -> 10% of each run, Pallas kernels for 7% -> 2%
where the time goes in v5:
time: 574 us; the launch traced here: 565 us
  blocking collectives  280 us (49%)
  starting transfers between devices  98.4 us (17%)
  waiting for transfers between devices  75 us (13%)
  matrix products  65 us (11%)
  local copies, waits for them, and re-layouts  16.4 us (3%)
  other arithmetic  15.5 us (3%)
  Pallas kernels  11.7 us (2%)
    all_to_all x19, blocking collectives, across(): lax.all_to_all(shaped, 'expert', 0, 0, axis_index_groups=same_core, tiled...  280 us
    dot_general x73, matrix products, dot(): lax.dot_general(left, right, dims, preferred_element_type=jnp.float32)  65 us
    ppermute x23, starting transfers between devices, swapped(): return lax.ppermute(value, 'expert', swap)  40.7 us
    ppermute x10, starting transfers between devices, on_device(): arriving = lax.ppermute(outgoing, 'section', ring)  30.1 us
    all_to_all x4, waiting for transfers between devices, across(): lax.all_to_all(shaped, 'expert', 0, 0, axis_index_groups=same_core, tiled...  25.2 us
    ppermute x10, waiting for transfers between devices, on_device(): arriving = lax.ppermute(outgoing, 'section', ring)  24.2 us
    ppermute x23, waiting for transfers between devices, swapped(): return lax.ppermute(value, 'expert', swap)  20 us
    all_to_all x4, starting transfers between devices, across(): lax.all_to_all(shaped, 'expert', 0, 0, axis_index_groups=same_core, tiled...  19.4 us
  transfers between devices with their start and end apart: 38, of which 34 were waited for; matrix products, arithmetic and copies ran while one was open for 10% of the time, Pallas kernels for 2%

profile of v5, /device:TPU:1, one launch (start us, length us, event | category | flops | bytes accessed | tf_op | source)
XLA Modules:
  0.0 564.8 jit_solution(16191481089674231799)
XLA Ops:
  6.1 7.8 %all-to-all-start = ((bf16[16,24,2560]{2,1,0:T(8,128)(2,1)}), bf16[16,24,2560]{2,1,0:T(8,128)(2,1)}, u32[]{:S(2)}, u32[]{:S(2)}) async-start(bf16[16,24,2560]{2,1,0:T(8,128)(2,1)} %bitcast.402), calls=%async_computation | async-start | bytes 3932160 | tf_op jit(solution)/shard_map/all_to_all | solution.py:188
  20.0 22.5 %all-to-all-done = bf16[16,24,2560]{2,1,0:T(8,128)(2,1)} async-done(((bf16[16,24,2560]{2,1,0:T(8,128)(2,1)}), bf16[16,24,2560]{2,1,0:T(8,128)(2,1)}, u32[]{:S(2)}, u32[]{:S(2)}) %all-to-all-start) | async-done | bytes 1966112 | tf_op jit(solution)/shard_map/all_to_all | solution.py:188
  44.7 8.2 %all-to-all-start.1 = ((bf16[8,32,320]{2,1,0:T(8,128)(2,1)}), bf16[8,32,320]{2,1,0:T(8,128)(2,1)S(1)}, u32[]{:S(2)}, u32[]{:S(2)}) async-start(bf16[8,32,320]{2,1,0:T(8,128)(2,1)} %pad_maximum_fusion.5), calls=%async_computation.1 | async-start | bytes 393216 | tf_op jit(solution)/shard_map/all_to_all | solution.py:209
  58.1 5.6 all-to-all-done.1
  115.8 18.2 %all_to_all.120 = bf16[16,8,2560]{2,1,0:T(8,128)(2,1)S(1)} all-to-all(bf16[16,8,2560]{2,1,0:T(8,128)(2,1)S(1)} %fusion.20), channel_id=1, replica_groups={{0,2,4,6,8,10,12,14,16,18,20,22,24,26,28,30},{1,3,5,7,9,11,13,15,17,19,..., dimensions={0} | all-to-all | bytes 1310720 | tf_op jit(solution)/shard_map/all_to_all | solution.py:188
  143.0 15.4 %all_to_all.121 = bf16[16,8,2560]{2,1,0:T(8,128)(2,1)S(1)} all-to-all(bf16[16,8,2560]{2,1,0:T(8,128)(2,1)S(1)} %fusion.68), channel_id=1, replica_groups={{0,2,4,6,8,10,12,14,16,18,20,22,24,26,28,30},{1,3,5,7,9,11,13,15,17,19,..., dimensions={0} | all-to-all | bytes 1310720 | tf_op jit(solution)/shard_map/all_to_all | solution.py:188
  163.2 14.1 %all_to_all.122 = bf16[16,8,2560]{2,1,0:T(8,128)(2,1)S(1)} all-to-all(bf16[16,8,2560]{2,1,0:T(8,128)(2,1)S(1)} %fusion.19), channel_id=1, replica_groups={{0,2,4,6,8,10,12,14,16,18,20,22,24,26,28,30},{1,3,5,7,9,11,13,15,17,19,..., dimensions={0} | all-to-all | bytes 1310720 | tf_op jit(solution)/shard_map/all_to_all | solution.py:188
  187.0 15.2 %all_to_all.123 = bf16[16,8,2560]{2,1,0:T(8,128)(2,1)S(1)} all-to-all(bf16[16,8,2560]{2,1,0:T(8,128)(2,1)S(1)} %fusion.69), channel_id=1, replica_groups={{0,2,4,6,8,10,12,14,16,18,20,22,24,26,28,30},{1,3,5,7,9,11,13,15,17,19,..., dimensions={0} | all-to-all | bytes 1310720 | tf_op jit(solution)/shard_map/all_to_all | solution.py:188
  207.9 13.8 %all_to_all.124 = bf16[16,8,2560]{2,1,0:T(8,128)(2,1)S(1)} all-to-all(bf16[16,8,2560]{2,1,0:T(8,128)(2,1)S(1)} %fusion.18), channel_id=1, replica_groups={{0,2,4,6,8,10,12,14,16,18,20,22,24,26,28,30},{1,3,5,7,9,11,13,15,17,19,..., dimensions={0} | all-to-all | bytes 1310720 | tf_op jit(solution)/shard_map/all_to_all | solution.py:188
  231.0 15.2 %all_to_all.125 = bf16[16,8,2560]{2,1,0:T(8,128)(2,1)S(1)} all-to-all(bf16[16,8,2560]{2,1,0:T(8,128)(2,1)S(1)} %fusion.70), channel_id=1, replica_groups={{0,2,4,6,8,10,12,14,16,18,20,22,24,26,28,30},{1,3,5,7,9,11,13,15,17,19,..., dimensions={0} | all-to-all | bytes 1310720 | tf_op jit(solution)/shard_map/all_to_all | solution.py:188
  252.7 13.8 %all_to_all.126 = bf16[16,8,2560]{2,1,0:T(8,128)(2,1)S(1)} all-to-all(bf16[16,8,2560]{2,1,0:T(8,128)(2,1)S(1)} %fusion.17), channel_id=1, replica_groups={{0,2,4,6,8,10,12,14,16,18,20,22,24,26,28,30},{1,3,5,7,9,11,13,15,17,19,..., dimensions={0} | all-to-all | bytes 1310720 | tf_op jit(solution)/shard_map/all_to_all | solution.py:188
  275.9 15.2 %all_to_all.127 = bf16[16,8,2560]{2,1,0:T(8,128)(2,1)S(1)} all-to-all(bf16[16,8,2560]{2,1,0:T(8,128)(2,1)S(1)} %fusion.71), channel_id=1, replica_groups={{0,2,4,6,8,10,12,14,16,18,20,22,24,26,28,30},{1,3,5,7,9,11,13,15,17,19,..., dimensions={0} | all-to-all | bytes 1310720 | tf_op jit(solution)/shard_map/all_to_all | solution.py:188
  297.7 13.8 %all_to_all.128 = bf16[16,8,2560]{2,1,0:T(8,128)(2,1)S(1)} all-to-all(bf16[16,8,2560]{2,1,0:T(8,128)(2,1)S(1)} %fusion.16), channel_id=1, replica_groups={{0,2,4,6,8,10,12,14,16,18,20,22,24,26,28,30},{1,3,5,7,9,11,13,15,17,19,..., dimensions={0} | all-to-all | bytes 1310720 | tf_op jit(solution)/shard_map/all_to_all | solution.py:188
  320.9 15.2 %all_to_all.129 = bf16[16,8,2560]{2,1,0:T(8,128)(2,1)S(1)} all-to-all(bf16[16,8,2560]{2,1,0:T(8,128)(2,1)S(1)} %fusion.72), channel_id=1, replica_groups={{0,2,4,6,8,10,12,14,16,18,20,22,24,26,28,30},{1,3,5,7,9,11,13,15,17,19,..., dimensions={0} | all-to-all | bytes 1310720 | tf_op jit(solution)/shard_map/all_to_all | solution.py:188
  342.5 13.8 %all_to_all.130 = bf16[16,8,2560]{2,1,0:T(8,128)(2,1)S(1)} all-to-all(bf16[16,8,2560]{2,1,0:T(8,128)(2,1)S(1)} %fusion.15), channel_id=1, replica_groups={{0,2,4,6,8,10,12,14,16,18,20,22,24,26,28,30},{1,3,5,7,9,11,13,15,17,19,..., dimensions={0} | all-to-all | bytes 1310720 | tf_op jit(solution)/shard_map/all_to_all | solution.py:188
  365.7 15.2 %all_to_all.131 = bf16[16,8,2560]{2,1,0:T(8,128)(2,1)S(1)} all-to-all(bf16[16,8,2560]{2,1,0:T(8,128)(2,1)S(1)} %fusion.73), channel_id=1, replica_groups={{0,2,4,6,8,10,12,14,16,18,20,22,24,26,28,30},{1,3,5,7,9,11,13,15,17,19,..., dimensions={0} | all-to-all | bytes 1310720 | tf_op jit(solution)/shard_map/all_to_all | solution.py:188
  387.4 13.8 %all_to_all.132 = bf16[16,8,2560]{2,1,0:T(8,128)(2,1)S(1)} all-to-all(bf16[16,8,2560]{2,1,0:T(8,128)(2,1)S(1)} %fusion.14), channel_id=1, replica_groups={{0,2,4,6,8,10,12,14,16,18,20,22,24,26,28,30},{1,3,5,7,9,11,13,15,17,19,..., dimensions={0} | all-to-all | bytes 1310720 | tf_op jit(solution)/shard_map/all_to_all | solution.py:188
  410.7 15.2 %all_to_all.133 = bf16[16,8,2560]{2,1,0:T(8,128)(2,1)S(1)} all-to-all(bf16[16,8,2560]{2,1,0:T(8,128)(2,1)S(1)} %fusion.74), channel_id=1, replica_groups={{0,2,4,6,8,10,12,14,16,18,20,22,24,26,28,30},{1,3,5,7,9,11,13,15,17,19,..., dimensions={0} | all-to-all | bytes 1310720 | tf_op jit(solution)/shard_map/all_to_all | solution.py:188
  432.4 13.8 %all_to_all.134 = bf16[16,8,2560]{2,1,0:T(8,128)(2,1)S(1)} all-to-all(bf16[16,8,2560]{2,1,0:T(8,128)(2,1)S(1)} %fusion.13), channel_id=1, replica_groups={{0,2,4,6,8,10,12,14,16,18,20,22,24,26,28,30},{1,3,5,7,9,11,13,15,17,19,..., dimensions={0} | all-to-all | bytes 1310720 | tf_op jit(solution)/shard_map/all_to_all | solution.py:188
  455.5 15.2 %all_to_all.135 = bf16[16,8,2560]{2,1,0:T(8,128)(2,1)S(1)} all-to-all(bf16[16,8,2560]{2,1,0:T(8,128)(2,1)S(1)} %fusion.75), channel_id=1, replica_groups={{0,2,4,6,8,10,12,14,16,18,20,22,24,26,28,30},{1,3,5,7,9,11,13,15,17,19,..., dimensions={0} | all-to-all | bytes 1310720 | tf_op jit(solution)/shard_map/all_to_all | solution.py:188
  477.2 13.8 %all_to_all.136 = bf16[16,8,2560]{2,1,0:T(8,128)(2,1)S(1)} all-to-all(bf16[16,8,2560]{2,1,0:T(8,128)(2,1)S(1)} %fusion.12), channel_id=1, replica_groups={{0,2,4,6,8,10,12,14,16,18,20,22,24,26,28,30},{1,3,5,7,9,11,13,15,17,19,..., dimensions={0} | all-to-all | bytes 1310720 | tf_op jit(solution)/shard_map/all_to_all | solution.py:188
  500.6 15.2 %all_to_all.137 = bf16[16,8,2560]{2,1,0:T(8,128)(2,1)S(1)} all-to-all(bf16[16,8,2560]{2,1,0:T(8,128)(2,1)S(1)} %fusion.76), channel_id=1, replica_groups={{0,2,4,6,8,10,12,14,16,18,20,22,24,26,28,30},{1,3,5,7,9,11,13,15,17,19,..., dimensions={0} | all-to-all | bytes 1310720 | tf_op jit(solution)/shard_map/all_to_all | solution.py:188
  522.3 13.8 %all_to_all.138 = bf16[16,8,2560]{2,1,0:T(8,128)(2,1)S(1)} all-to-all(bf16[16,8,2560]{2,1,0:T(8,128)(2,1)S(1)} %fusion.11), channel_id=1, replica_groups={{0,2,4,6,8,10,12,14,16,18,20,22,24,26,28,30},{1,3,5,7,9,11,13,15,17,19,..., dimensions={0} | all-to-all | bytes 1310720 | tf_op jit(solution)/shard_map/all_to_all | solution.py:188
  551.5 11.7 %shard_map.102 = (bf16[384,2560]{1,0:T(8,128)(2,1)}, bf16[384,2560]{1,0:T(8,128)(2,1)}, bf16[384,2560]{1,0:T(8,128)(2,1)}) custom-call(s32[1]{0:T(128)} %bitcast.100.first_ref, bf16[128,768]{1,0:T(8,128)(2,1)} %copy-done.30, bf16[128,768]{1,0:T(8,128)(2,1)} %copy-done.31, bf16[128,2560]{1,0:T(8,128)(2,1)} %bitcast.405, bf16[128,2560]{1,0:T(8,128)(2,1)} %copy-done.19, ...), custom_call_target="tpu_custom_call" | custom-call | flops 6039797760 | bytes 16384000 | tf_op jit(solution)/shard_map/pallas_call | solution.py:148
  (414 shorter events, 226.3 us)
Async XLA Ops:
  6.1 36.5 %all-to-all-start = ((bf16[16,24,2560]{2,1,0:T(8,128)(2,1)}), bf16[16,24,2560]{2,1,0:T(8,128)(2,1)}, u32[]{:S(2)}, u32[]{:S(2)}) async-start(bf16[16,24,2560]{2,1,0:T(8,128)(2,1)} %bitcast.402), calls=%async_computation | async-start | bytes 3932160 | tf_op jit(solution)/shard_map/all_to_all | solution.py:188
  42.6 21.4 %collective-permute-start = (bf16[384,2560]{1,0:T(8,128)(2,1)}, bf16[384,2560]{1,0:T(8,128)(2,1)}, u32[]{:S(2)}, u32[]{:S(2)}) collective-permute-start(bf16[384,2560]{1,0:T(8,128)(2,1)} %bitcast.3), channel_id=1, source_target_pairs={{0,1},{1,0},{2,3},{3,2},{4,5},{5,4},{6,7},{7,6},{8,9},{9,8},{10,11... | collective-permute-start | bytes 5898248 | tf_op jit(solution)/shard_map/ppermute | solution.py:192
  44.7 19.0 %all-to-all-start.1 = ((bf16[8,32,320]{2,1,0:T(8,128)(2,1)}), bf16[8,32,320]{2,1,0:T(8,128)(2,1)S(1)}, u32[]{:S(2)}, u32[]{:S(2)}) async-start(bf16[8,32,320]{2,1,0:T(8,128)(2,1)} %pad_maximum_fusion.5), calls=%async_computation.1 | async-start | bytes 393216 | tf_op jit(solution)/shard_map/all_to_all | solution.py:209
  65.1 15.7 %all-to-all-start.2 = ((bf16[16,8,2560]{2,1,0:T(8,128)(2,1)}), bf16[16,8,2560]{2,1,0:T(8,128)(2,1)S(1)}, u32[]{:S(2)}, u32[]{:S(2)}) async-start(bf16[16,8,2560]{2,1,0:T(8,128)(2,1)} %bitcast.429), calls=%async_computation.2 | async-start | bytes 1310720 | tf_op jit(solution)/shard_map/all_to_all | solution.py:188
  92.2 17.3 %all-to-all-start.3 = ((bf16[16,8,2560]{2,1,0:T(8,128)(2,1)}), bf16[16,8,2560]{2,1,0:T(8,128)(2,1)}, u32[]{:S(2)}, u32[]{:S(2)}) async-start(bf16[16,8,2560]{2,1,0:T(8,128)(2,1)} %bitcast.16), calls=%async_computation.3 | async-start | bytes 1310720 | tf_op jit(solution)/shard_map/all_to_all | solution.py:188
  110.8 4.6 collective-permute-start.3
  177.4 4.9 collective-permute-start.7
  202.4 5.1 collective-permute-start.9
  221.7 5.0 collective-permute-start.10
  246.5 5.9 %collective-permute-start.12 = (bf16[32,2560]{1,0:T(8,128)(2,1)S(1)}, bf16[32,2560]{1,0:T(8,128)(2,1)S(1)}, u32[]{:S(2)}, u32[]{:S(2)}) collective-permute-start(bf16[32,2560]{1,0:T(8,128)(2,1)S(1)} %get-tuple-element.273), channel_id=1, source_target_pairs={{0,224},{32,0},{64,32},{96,64},{128,96},{160,128},{192,160},{224,1... | collective-permute-start | bytes 491528 | tf_op jit(solution)/shard_map/ppermute | solution.py:296
  266.6 5.0 collective-permute-start.13
  291.3 6.1 %collective-permute-start.15 = (bf16[32,2560]{1,0:T(8,128)(2,1)S(1)}, bf16[32,2560]{1,0:T(8,128)(2,1)S(1)}, u32[]{:S(2)}, u32[]{:S(2)}) collective-permute-start(bf16[32,2560]{1,0:T(8,128)(2,1)S(1)} %get-tuple-element.271), channel_id=1, source_target_pairs={{0,224},{32,0},{64,32},{96,64},{128,96},{160,128},{192,160},{224,1... | collective-permute-start | bytes 491528 | tf_op jit(solution)/shard_map/ppermute | solution.py:296
  311.6 5.0 collective-permute-start.16
  336.3 5.9 %collective-permute-start.18 = (bf16[32,2560]{1,0:T(8,128)(2,1)S(1)}, bf16[32,2560]{1,0:T(8,128)(2,1)S(1)}, u32[]{:S(2)}, u32[]{:S(2)}) collective-permute-start(bf16[32,2560]{1,0:T(8,128)(2,1)S(1)} %get-tuple-element.269), channel_id=1, source_target_pairs={{0,224},{32,0},{64,32},{96,64},{128,96},{160,128},{192,160},{224,1... | collective-permute-start | bytes 491528 | tf_op jit(solution)/shard_map/ppermute | solution.py:296
  356.4 5.0 collective-permute-start.19
  381.1 5.9 %collective-permute-start.21 = (bf16[32,2560]{1,0:T(8,128)(2,1)S(1)}, bf16[32,2560]{1,0:T(8,128)(2,1)S(1)}, u32[]{:S(2)}, u32[]{:S(2)}) collective-permute-start(bf16[32,2560]{1,0:T(8,128)(2,1)S(1)} %get-tuple-element.267), channel_id=1, source_target_pairs={{0,224},{32,0},{64,32},{96,64},{128,96},{160,128},{192,160},{224,1... | collective-permute-start | bytes 491528 | tf_op jit(solution)/shard_map/ppermute | solution.py:296
  401.2 5.2 collective-permute-start.22
  426.1 5.9 %collective-permute-start.24 = (bf16[32,2560]{1,0:T(8,128)(2,1)S(1)}, bf16[32,2560]{1,0:T(8,128)(2,1)S(1)}, u32[]{:S(2)}, u32[]{:S(2)}) collective-permute-start(bf16[32,2560]{1,0:T(8,128)(2,1)S(1)} %get-tuple-element.265), channel_id=1, source_target_pairs={{0,224},{32,0},{64,32},{96,64},{128,96},{160,128},{192,160},{224,1... | collective-permute-start | bytes 491528 | tf_op jit(solution)/shard_map/ppermute | solution.py:296
  446.2 5.0 collective-permute-start.25
  471.0 5.9 %collective-permute-start.27 = (bf16[32,2560]{1,0:T(8,128)(2,1)S(1)}, bf16[32,2560]{1,0:T(8,128)(2,1)S(1)}, u32[]{:S(2)}, u32[]{:S(2)}) collective-permute-start(bf16[32,2560]{1,0:T(8,128)(2,1)S(1)} %get-tuple-element.263), channel_id=1, source_target_pairs={{0,224},{32,0},{64,32},{96,64},{128,96},{160,128},{192,160},{224,1... | collective-permute-start | bytes 491528 | tf_op jit(solution)/shard_map/ppermute | solution.py:296
  491.0 5.0 collective-permute-start.28
  516.0 5.9 %collective-permute-start.30 = (bf16[32,2560]{1,0:T(8,128)(2,1)S(1)}, bf16[32,2560]{1,0:T(8,128)(2,1)S(1)}, u32[]{:S(2)}, u32[]{:S(2)}) collective-permute-start(bf16[32,2560]{1,0:T(8,128)(2,1)S(1)} %get-tuple-element.261), channel_id=1, source_target_pairs={{0,224},{32,0},{64,32},{96,64},{128,96},{160,128},{192,160},{224,1... | collective-permute-start | bytes 491528 | tf_op jit(solution)/shard_map/ppermute | solution.py:296
  536.1 5.1 collective-permute-start.31
  546.8 16.5 %all-to-all-start.23 = ((bf16[16,8,2560]{2,1,0:T(8,128)(2,1)}), bf16[16,8,2560]{2,1,0:T(8,128)(2,1)S(1)}, u32[]{:S(2)}, u32[]{:S(2)}) async-start(bf16[16,8,2560]{2,1,0:T(8,128)(2,1)} %bitcast.98), calls=%async_computation.23 | async-start | bytes 1310720 | tf_op jit(solution)/shard_map/all_to_all | solution.py:188
  (105 other events, 792.5 us)

commit v6 on v5

--- a/solution.py
+++ b/solution.py
@@ -196,21 +196,37 @@
 
     placing, slot_gates, packing, unpacking = slot_tables(routes[0], gates[0], chips)
     x_tokens = x_saved[0].reshape(batches * tokens, width)
-    x_packed = across(dot(packing, x_tokens).astype(jnp.bfloat16))
+    x_out = dot(packing, x_tokens).astype(jnp.bfloat16)
 
     by_group = cotangent.reshape(groups, GROUP * tokens, -1)
-    pieces = jnp.concatenate([by_group[1:], by_group[: sections - groups], by_group[:1]])
+    blocks = []
+    for ahead in range(sections):
+        wanted = (section_index + ahead + 1) % sections
+        wanted = jnp.where(wanted < groups, wanted, 0)
+        blocks.append(lax.dynamic_index_in_dim(by_group, wanted, 0, keepdims=False))
+    x_packed = across(x_out)
+    step = 1
+    while step < sections:
+        moved = [k for k in range(sections) if k & step]
+        pairs = [(z, (z + step) % sections) for z in range(sections)]
+        sent = jnp.concatenate([blocks[k] for k in moved])
+        sent = lax.ppermute(sent, "section", pairs).reshape(len(moved), GROUP * tokens, -1)
+        for i, k in enumerate(moved):
+            blocks[k] = sent[i]
+        step *= 2
+    arriving = jnp.concatenate(
+        [lax.select_n((section_index - j) % sections, *blocks) for j in range(sections)], axis=1
+    )
     padded_placing = jnp.concatenate([placing, jnp.zeros_like(placing[:1])])
     padded_gates = jnp.concatenate([slot_gates, jnp.zeros_like(slot_gates[:1])])
-    x_packed, pieces, both_rows, padded_placing, padded_gates, unpacking = together(
-        x_packed, pieces, both_rows, padded_placing, padded_gates, unpacking
+    x_packed, arriving, both_rows, padded_placing, padded_gates, unpacking = together(
+        x_packed, arriving, both_rows, padded_placing, padded_gates, unpacking
     )
     x_packed_other = swapped(x_packed)
-    pieces = lax.all_to_all(pieces, "section", 0, 0, tiled=True)
-    arriving = pieces.transpose(1, 0, 2).reshape(GROUP * tokens, width)
-
-    def unpacked(packed):
-        return dot(unpacking.reshape(groups * rows, -1), packed).astype(jnp.bfloat16)
+
+    def unpacked(packed, count):
+        place = unpacking[:count].reshape(count * rows, -1)
+        return dot(place, packed).astype(jnp.bfloat16)
 
     def forward(x):
         pre = dot(x, both_rows, COLS_COLS)
@@ -228,11 +244,9 @@
     def group_at(tick):
         return tick - (sections - 1 - section_index)
 
-    def chosen_at(tick):
-        return jnp.clip(group_at(tick), 0, groups - 1)
-
-    x_mine = unpacked(x_packed)
-    arriving, x_mine, x_packed_other = together(arriving, x_mine, x_packed_other)
+    def sliced(value, tick):
+        chosen = jnp.clip(group_at(tick), 0, groups - 1)
+        return lax.dynamic_slice_in_dim(value, chosen * rows, rows, axis=0)
 
     kept_out, kept = [], []
     ticks = sections + groups - 1
@@ -243,16 +257,28 @@
         gate = padded_gates[jnp.where(active, group, groups)]
         if tick == 0:
             rows_out = (dot(place, arriving) * gate[:, None]).astype(jnp.bfloat16)
-            rows_out, x_mine, x_packed_other = together(rows_out, x_mine, x_packed_other)
+            rows_out, x_packed, x_packed_other = together(rows_out, x_packed, x_packed_other)
             came = across(rows_out)
-            x_other = unpacked(x_packed_other)
-            slopes = [forward(value[:rows])[0] for value in (x_mine, x_other)]
-            rows_mine, slopes, x_mine, x_other = together(came, slopes, x_mine, x_other)
+            x_mine = unpacked(x_packed, groups)
+            slopes = [forward(x_mine[:rows])[0], forward(unpacked(x_packed_other, 1))[0]]
+            rows_mine, slopes, x_mine = together(came, slopes, x_mine)
+        elif tick == 1:
+            slope_mine = sliced(slope_mine_all, tick)
+            arriving, place, gate, slope_mine, x_other = together(
+                arriving, place, gate, slope_mine, x_other
+            )
+            rows_out = (dot(place, arriving) * gate[:, None]).astype(jnp.bfloat16)
+            rows_out, x_other = together(rows_out, x_other)
+            came = across(rows_out)
+            slope_other_all, act_other = forward(x_other)
+            rows_mine, slope_other = together(came, sliced(slope_other_all, tick))
+            slopes = [slope_mine, slope_other]
+            x_halves, act_halves = [
+                [value.reshape(groups, rows, -1) for value in values]
+                for values in ((x_mine, x_other), (act_mine, act_other))
+            ]
         else:
-            slopes = [
-                lax.dynamic_index_in_dim(value, chosen_at(tick), 0, keepdims=False)
-                for value in slope_halves
-            ]
+            slopes = [sliced(slope_mine_all, tick), sliced(slope_other_all, tick)]
             arriving, place, gate, slopes = together(arriving, place, gate, slopes)
             rows_mine = across((dot(place, arriving) * gate[:, None]).astype(jnp.bfloat16))
         rows_other = swapped(rows_mine)
@@ -266,12 +292,9 @@
         summed = part_mine.astype(jnp.float32) + from_other.astype(jnp.float32)
         summed = summed.astype(jnp.bfloat16)
         if tick == 0:
-            summed, x_mine, x_other = together(summed, x_mine, x_other)
-            slope_halves, act_halves = zip(*(forward(value) for value in (x_mine, x_other)))
-            slope_halves, act_halves, x_halves = [
-                [value.reshape(groups, rows, -1) for value in values]
-                for values in (slope_halves, act_halves, (x_mine, x_other))
-            ]
+            summed, x_mine, x_packed_other = together(summed, x_mine, x_packed_other)
+            slope_mine_all, act_mine = forward(x_mine)
+            x_other = unpacked(x_packed_other, groups)
         if tick == ticks - 1:
             first = sections - 1 - section_index
             summed, d_mine, d_other, rows_mine, rows_other, first = together(

time: 574 us -> 573 us (level)
  blocking collectives: 280 us -> 247 us
  starting transfers between devices: 98.4 us -> 115 us
  matrix products: 65 us -> 78.3 us
    all_to_all x19 -> x17, blocking collectives: 280 us -> 247 us  [across(): lax.all_to_all(shaped, 'expert', 0, 0, axis_index_groups=same_core, tiled...]
    dot_general x73, matrix products: 65 us -> 78.3 us  [dot(): lax.dot_general(left, right, dims, preferred_element_type=jnp.float32)]
    ppermute x0 -> x3, starting transfers between devices: none -> 9.45 us  [on_device(): lax.ppermute(sent, 'section', pairs).reshape(len(moved), GROUP * tokens, -1)]
    all_to_all x4 -> x6, starting transfers between devices: 19.4 us -> 28.7 us  [across(): lax.all_to_all(shaped, 'expert', 0, 0, axis_index_groups=same_core, tiled...]
    ppermute x0 -> x3, waiting for transfers between devices: none -> 8.82 us  [on_device(): lax.ppermute(sent, 'section', pairs).reshape(len(moved), GROUP * tokens, -1)]
    all_to_all x1 -> x0, starting transfers between devices: 8.18 us -> none  [on_device(): pieces = lax.all_to_all(pieces, 'section', 0, 0, tiled=True)]
    ppermute x10, starting transfers between devices: 30.1 us -> 36.2 us  [on_device(): arriving = lax.ppermute(outgoing, 'section', ring)]
    all_to_all x4 -> x6, waiting for transfers between devices: 25.2 us -> 25 us  [across(): lax.all_to_all(shaped, 'expert', 0, 0, axis_index_groups=same_core, tiled...]
  transfers between devices with their start and end apart: 38 -> 42, of which waited for: 34 -> 38; matrix products, arithmetic and copies ran while one was open for 10% -> 12% of each run, Pallas kernels for 2% -> 2%
where the time goes in v6:
time: 573 us; the launch traced here: 563 us
  blocking collectives  247 us (43%)
  starting transfers between devices  115 us (20%)
  matrix products  78.3 us (14%)
  waiting for transfers between devices  76.1 us (13%)
  other arithmetic  17.6 us (3%)
  local copies, waits for them, and re-layouts  13.1 us (2%)
  Pallas kernels  11.7 us (2%)
    all_to_all x17, blocking collectives, across(): lax.all_to_all(shaped, 'expert', 0, 0, axis_index_groups=same_core, tiled...  247 us
    dot_general x73, matrix products, dot(): lax.dot_general(left, right, dims, preferred_element_type=jnp.float32)  78.3 us
    ppermute x23, starting transfers between devices, swapped(): return lax.ppermute(value, 'expert', swap)  40.6 us
    ppermute x10, starting transfers between devices, on_device(): arriving = lax.ppermute(outgoing, 'section', ring)  36.2 us
    all_to_all x6, starting transfers between devices, across(): lax.all_to_all(shaped, 'expert', 0, 0, axis_index_groups=same_core, tiled...  28.7 us
    all_to_all x6, waiting for transfers between devices, across(): lax.all_to_all(shaped, 'expert', 0, 0, axis_index_groups=same_core, tiled...  25 us
    ppermute x23, waiting for transfers between devices, swapped(): return lax.ppermute(value, 'expert', swap)  21.4 us
    ppermute x10, waiting for transfers between devices, on_device(): arriving = lax.ppermute(outgoing, 'section', ring)  20.9 us
  transfers between devices with their start and end apart: 42, of which 38 were waited for; matrix products, arithmetic and copies ran while one was open for 12% of the time, Pallas kernels for 2%

profile of v6, /device:TPU:1, one launch (start us, length us, event | category | flops | bytes accessed | tf_op | source)
XLA Modules:
  0.0 562.6 jit_solution(17280415800831201280)
XLA Ops:
  9.6 6.9 %all-to-all-start = ((bf16[16,24,2560]{2,1,0:T(8,128)(2,1)}), bf16[16,24,2560]{2,1,0:T(8,128)(2,1)}, u32[]{:S(2)}, u32[]{:S(2)}) async-start(bf16[16,24,2560]{2,1,0:T(8,128)(2,1)} %bitcast.409), calls=%async_computation | async-start | bytes 3932160 | tf_op jit(solution)/shard_map/all_to_all | solution.py:188
  25.3 5.5 collective-permute-done.1
  38.6 5.8 %all-to-all-done = bf16[16,24,2560]{2,1,0:T(8,128)(2,1)} async-done(((bf16[16,24,2560]{2,1,0:T(8,128)(2,1)}), bf16[16,24,2560]{2,1,0:T(8,128)(2,1)}, u32[]{:S(2)}, u32[]{:S(2)}) %all-to-all-start) | async-done | bytes 1966112 | tf_op jit(solution)/shard_map/all_to_all | solution.py:188
  105.0 5.6 %all-to-all-start.3 = ((bf16[16,8,2560]{2,1,0:T(8,128)(2,1)}), bf16[16,8,2560]{2,1,0:T(8,128)(2,1)}, u32[]{:S(2)}, u32[]{:S(2)}) async-start(bf16[16,8,2560]{2,1,0:T(8,128)(2,1)} %bitcast.435), calls=%async_computation.3 | async-start | bytes 1310720 | tf_op jit(solution)/shard_map/all_to_all | solution.py:188
  110.6 5.1 fusion.208
  131.9 15.7 %all_to_all.115 = bf16[16,8,2560]{2,1,0:T(8,128)(2,1)S(1)} all-to-all(bf16[16,8,2560]{2,1,0:T(8,128)(2,1)S(1)} %fusion.69), channel_id=1, replica_groups={{0,2,4,6,8,10,12,14,16,18,20,22,24,26,28,30},{1,3,5,7,9,11,13,15,17,19,..., dimensions={0} | all-to-all | bytes 1310720 | tf_op jit(solution)/shard_map/all_to_all | solution.py:188
  154.6 13.7 %all_to_all.116 = bf16[16,8,2560]{2,1,0:T(8,128)(2,1)S(1)} all-to-all(bf16[16,8,2560]{2,1,0:T(8,128)(2,1)S(1)} %fusion.19), channel_id=1, replica_groups={{0,2,4,6,8,10,12,14,16,18,20,22,24,26,28,30},{1,3,5,7,9,11,13,15,17,19,..., dimensions={0} | all-to-all | bytes 1310720 | tf_op jit(solution)/shard_map/all_to_all | solution.py:188
  177.3 15.2 %all_to_all.117 = bf16[16,8,2560]{2,1,0:T(8,128)(2,1)S(1)} all-to-all(bf16[16,8,2560]{2,1,0:T(8,128)(2,1)S(1)} %fusion.70), channel_id=1, replica_groups={{0,2,4,6,8,10,12,14,16,18,20,22,24,26,28,30},{1,3,5,7,9,11,13,15,17,19,..., dimensions={0} | all-to-all | bytes 1310720 | tf_op jit(solution)/shard_map/all_to_all | solution.py:188
  199.6 14.0 %all_to_all.118 = bf16[16,8,2560]{2,1,0:T(8,128)(2,1)S(1)} all-to-all(bf16[16,8,2560]{2,1,0:T(8,128)(2,1)S(1)} %fusion.18), channel_id=1, replica_groups={{0,2,4,6,8,10,12,14,16,18,20,22,24,26,28,30},{1,3,5,7,9,11,13,15,17,19,..., dimensions={0} | all-to-all | bytes 1310720 | tf_op jit(solution)/shard_map/all_to_all | solution.py:188
  222.4 15.2 %all_to_all.119 = bf16[16,8,2560]{2,1,0:T(8,128)(2,1)S(1)} all-to-all(bf16[16,8,2560]{2,1,0:T(8,128)(2,1)S(1)} %fusion.71), channel_id=1, replica_groups={{0,2,4,6,8,10,12,14,16,18,20,22,24,26,28,30},{1,3,5,7,9,11,13,15,17,19,..., dimensions={0} | all-to-all | bytes 1310720 | tf_op jit(solution)/shard_map/all_to_all | solution.py:188
  244.7 14.0 %all_to_all.120 = bf16[16,8,2560]{2,1,0:T(8,128)(2,1)S(1)} all-to-all(bf16[16,8,2560]{2,1,0:T(8,128)(2,1)S(1)} %fusion.17), channel_id=1, replica_groups={{0,2,4,6,8,10,12,14,16,18,20,22,24,26,28,30},{1,3,5,7,9,11,13,15,17,19,..., dimensions={0} | all-to-all | bytes 1310720 | tf_op jit(solution)/shard_map/all_to_all | solution.py:188
  267.9 15.2 %all_to_all.121 = bf16[16,8,2560]{2,1,0:T(8,128)(2,1)S(1)} all-to-all(bf16[16,8,2560]{2,1,0:T(8,128)(2,1)S(1)} %fusion.72), channel_id=1, replica_groups={{0,2,4,6,8,10,12,14,16,18,20,22,24,26,28,30},{1,3,5,7,9,11,13,15,17,19,..., dimensions={0} | all-to-all | bytes 1310720 | tf_op jit(solution)/shard_map/all_to_all | solution.py:188
  290.2 14.0 %all_to_all.122 = bf16[16,8,2560]{2,1,0:T(8,128)(2,1)S(1)} all-to-all(bf16[16,8,2560]{2,1,0:T(8,128)(2,1)S(1)} %fusion.16), channel_id=1, replica_groups={{0,2,4,6,8,10,12,14,16,18,20,22,24,26,28,30},{1,3,5,7,9,11,13,15,17,19,..., dimensions={0} | all-to-all | bytes 1310720 | tf_op jit(solution)/shard_map/all_to_all | solution.py:188
  318.1 12.4 %all-to-all-done.12 = bf16[16,8,2560]{2,1,0:T(8,128)(2,1)} async-done(((bf16[16,8,2560]{2,1,0:T(8,128)(2,1)}), bf16[16,8,2560]{2,1,0:T(8,128)(2,1)}, u32[]{:S(2)}, u32[]{:S(2)}) %all-to-all-start.12) | async-done | bytes 655392 | tf_op jit(solution)/shard_map/all_to_all | solution.py:188
  338.8 14.4 %all_to_all.123 = bf16[16,8,2560]{2,1,0:T(8,128)(2,1)S(1)} all-to-all(bf16[16,8,2560]{2,1,0:T(8,128)(2,1)S(1)} %fusion.15), channel_id=1, replica_groups={{0,2,4,6,8,10,12,14,16,18,20,22,24,26,28,30},{1,3,5,7,9,11,13,15,17,19,..., dimensions={0} | all-to-all | bytes 1310720 | tf_op jit(solution)/shard_map/all_to_all | solution.py:188
  362.6 15.4 %all_to_all.124 = bf16[16,8,2560]{2,1,0:T(8,128)(2,1)S(1)} all-to-all(bf16[16,8,2560]{2,1,0:T(8,128)(2,1)S(1)} %fusion.74), channel_id=1, replica_groups={{0,2,4,6,8,10,12,14,16,18,20,22,24,26,28,30},{1,3,5,7,9,11,13,15,17,19,..., dimensions={0} | all-to-all | bytes 1310720 | tf_op jit(solution)/shard_map/all_to_all | solution.py:188
  385.1 13.6 %all_to_all.125 = bf16[16,8,2560]{2,1,0:T(8,128)(2,1)S(1)} all-to-all(bf16[16,8,2560]{2,1,0:T(8,128)(2,1)S(1)} %fusion.14), channel_id=1, replica_groups={{0,2,4,6,8,10,12,14,16,18,20,22,24,26,28,30},{1,3,5,7,9,11,13,15,17,19,..., dimensions={0} | all-to-all | bytes 1310720 | tf_op jit(solution)/shard_map/all_to_all | solution.py:188
  407.5 15.2 %all_to_all.126 = bf16[16,8,2560]{2,1,0:T(8,128)(2,1)S(1)} all-to-all(bf16[16,8,2560]{2,1,0:T(8,128)(2,1)S(1)} %fusion.75), channel_id=1, replica_groups={{0,2,4,6,8,10,12,14,16,18,20,22,24,26,28,30},{1,3,5,7,9,11,13,15,17,19,..., dimensions={0} | all-to-all | bytes 1310720 | tf_op jit(solution)/shard_map/all_to_all | solution.py:188
  429.8 13.8 %all_to_all.127 = bf16[16,8,2560]{2,1,0:T(8,128)(2,1)S(1)} all-to-all(bf16[16,8,2560]{2,1,0:T(8,128)(2,1)S(1)} %fusion.13), channel_id=1, replica_groups={{0,2,4,6,8,10,12,14,16,18,20,22,24,26,28,30},{1,3,5,7,9,11,13,15,17,19,..., dimensions={0} | all-to-all | bytes 1310720 | tf_op jit(solution)/shard_map/all_to_all | solution.py:188
  452.5 15.2 %all_to_all.128 = bf16[16,8,2560]{2,1,0:T(8,128)(2,1)S(1)} all-to-all(bf16[16,8,2560]{2,1,0:T(8,128)(2,1)S(1)} %fusion.76), channel_id=1, replica_groups={{0,2,4,6,8,10,12,14,16,18,20,22,24,26,28,30},{1,3,5,7,9,11,13,15,17,19,..., dimensions={0} | all-to-all | bytes 1310720 | tf_op jit(solution)/shard_map/all_to_all | solution.py:188
  474.7 13.8 %all_to_all.129 = bf16[16,8,2560]{2,1,0:T(8,128)(2,1)S(1)} all-to-all(bf16[16,8,2560]{2,1,0:T(8,128)(2,1)S(1)} %fusion.12), channel_id=1, replica_groups={{0,2,4,6,8,10,12,14,16,18,20,22,24,26,28,30},{1,3,5,7,9,11,13,15,17,19,..., dimensions={0} | all-to-all | bytes 1310720 | tf_op jit(solution)/shard_map/all_to_all | solution.py:188
  497.6 15.2 %all_to_all.130 = bf16[16,8,2560]{2,1,0:T(8,128)(2,1)S(1)} all-to-all(bf16[16,8,2560]{2,1,0:T(8,128)(2,1)S(1)} %fusion.77), channel_id=1, replica_groups={{0,2,4,6,8,10,12,14,16,18,20,22,24,26,28,30},{1,3,5,7,9,11,13,15,17,19,..., dimensions={0} | all-to-all | bytes 1310720 | tf_op jit(solution)/shard_map/all_to_all | solution.py:188
  519.9 13.8 %all_to_all.131 = bf16[16,8,2560]{2,1,0:T(8,128)(2,1)S(1)} all-to-all(bf16[16,8,2560]{2,1,0:T(8,128)(2,1)S(1)} %fusion.11), channel_id=1, replica_groups={{0,2,4,6,8,10,12,14,16,18,20,22,24,26,28,30},{1,3,5,7,9,11,13,15,17,19,..., dimensions={0} | all-to-all | bytes 1310720 | tf_op jit(solution)/shard_map/all_to_all | solution.py:188
  549.3 11.7 %shard_map.102 = (bf16[384,2560]{1,0:T(8,128)(2,1)}, bf16[384,2560]{1,0:T(8,128)(2,1)}, bf16[384,2560]{1,0:T(8,128)(2,1)}) custom-call(s32[1]{0:T(128)} %bitcast.84.first_ref, bf16[128,768]{1,0:T(8,128)(2,1)} %copy-done.34, bf16[128,768]{1,0:T(8,128)(2,1)} %copy-done.35, bf16[128,2560]{1,0:T(8,128)(2,1)} %bitcast.412, bf16[128,2560]{1,0:T(8,128)(2,1)} %copy-done.23, ...), custom_call_target="tpu_custom_call" | custom-call | flops 6039797760 | bytes 16384000 | tf_op jit(solution)/shard_map/pallas_call | solution.py:148
  (446 shorter events, 258.7 us)
Async XLA Ops:
  1.8 20.3 %collective-permute-start = (bf16[128,320]{1,0:T(8,128)(2,1)S(1)}, bf16[128,320]{1,0:T(8,128)(2,1)S(1)}, u32[]{:S(2)}, u32[]{:S(2)}) collective-permute-start(bf16[128,320]{1,0:T(8,128)(2,1)S(1)} %pad_maximum_fusion.3), channel_id=1, source_target_pairs={{0,32},{32,64},{64,96},{96,128},{128,160},{160,192},{192,224},{224... | collective-permute-start | bytes 245768 | tf_op jit(solution)/shard_map/ppermute | solution.py:213
  9.6 34.7 %all-to-all-start = ((bf16[16,24,2560]{2,1,0:T(8,128)(2,1)}), bf16[16,24,2560]{2,1,0:T(8,128)(2,1)}, u32[]{:S(2)}, u32[]{:S(2)}) async-start(bf16[16,24,2560]{2,1,0:T(8,128)(2,1)} %bitcast.409), calls=%async_computation | async-start | bytes 3932160 | tf_op jit(solution)/shard_map/all_to_all | solution.py:188
  22.1 8.7 %collective-permute-start.1 = (bf16[128,320]{1,0:T(8,128)(2,1)S(1)}, bf16[128,320]{1,0:T(8,128)(2,1)S(1)}, u32[]{:S(2)}, u32[]{:S(2)}) collective-permute-start(bf16[128,320]{1,0:T(8,128)(2,1)S(1)} %pad_maximum_fusion.4), channel_id=1, source_target_pairs={{0,64},{32,96},{64,128},{96,160},{128,192},{160,224},{192,0},{224,... | collective-permute-start | bytes 245768 | tf_op jit(solution)/shard_map/ppermute | solution.py:213
  30.8 7.5 %collective-permute-start.2 = (bf16[128,320]{1,0:T(8,128)(2,1)S(1)}, bf16[128,320]{1,0:T(8,128)(2,1)S(1)}, u32[]{:S(2)}, u32[]{:S(2)}) collective-permute-start(bf16[128,320]{1,0:T(8,128)(2,1)S(1)} %pad_maximum_fusion.5), channel_id=1, source_target_pairs={{0,128},{32,160},{64,192},{96,224},{128,0},{160,32},{192,64},{224,... | collective-permute-start | bytes 245768 | tf_op jit(solution)/shard_map/ppermute | solution.py:213
  44.3 6.5 %collective-permute-start.3 = (bf16[384,2560]{1,0:T(8,128)(2,1)}, bf16[384,2560]{1,0:T(8,128)(2,1)}, u32[]{:S(2)}, u32[]{:S(2)}) collective-permute-start(bf16[384,2560]{1,0:T(8,128)(2,1)} %bitcast.3), channel_id=1, source_target_pairs={{0,1},{1,0},{2,3},{3,2},{4,5},{5,4},{6,7},{7,6},{8,9},{9,8},{10,11... | collective-permute-start | bytes 5898248 | tf_op jit(solution)/shard_map/ppermute | solution.py:192
  50.8 16.0 %all-to-all-start.1 = ((bf16[16,8,2560]{2,1,0:T(8,128)(2,1)}), bf16[16,8,2560]{2,1,0:T(8,128)(2,1)S(1)}, u32[]{:S(2)}, u32[]{:S(2)}) async-start(bf16[16,8,2560]{2,1,0:T(8,128)(2,1)} %bitcast.434), calls=%async_computation.1 | async-start | bytes 1310720 | tf_op jit(solution)/shard_map/all_to_all | solution.py:188
  77.2 17.2 %all-to-all-start.2 = ((bf16[16,8,2560]{2,1,0:T(8,128)(2,1)}), bf16[16,8,2560]{2,1,0:T(8,128)(2,1)}, u32[]{:S(2)}, u32[]{:S(2)}) async-start(bf16[16,8,2560]{2,1,0:T(8,128)(2,1)} %bitcast.22), calls=%async_computation.2 | async-start | bytes 1310720 | tf_op jit(solution)/shard_map/all_to_all | solution.py:188
  96.5 6.7 %collective-permute-start.6 = (bf16[32,2560]{1,0:T(8,128)(2,1)S(1)}, bf16[32,2560]{1,0:T(8,128)(2,1)S(1)}, u32[]{:S(2)}, u32[]{:S(2)}) collective-permute-start(bf16[32,2560]{1,0:T(8,128)(2,1)S(1)} %get-tuple-element.340), channel_id=1, source_target_pairs={{0,224},{32,0},{64,32},{96,64},{128,96},{160,128},{192,160},{224,1... | collective-permute-start | bytes 491528 | tf_op jit(solution)/shard_map/ppermute | solution.py:319
  105.0 17.3 %all-to-all-start.3 = ((bf16[16,8,2560]{2,1,0:T(8,128)(2,1)}), bf16[16,8,2560]{2,1,0:T(8,128)(2,1)}, u32[]{:S(2)}, u32[]{:S(2)}) async-start(bf16[16,8,2560]{2,1,0:T(8,128)(2,1)} %bitcast.435), calls=%async_computation.3 | async-start | bytes 1310720 | tf_op jit(solution)/shard_map/all_to_all | solution.py:188
  148.5 5.7 %collective-permute-start.9 = (bf16[32,2560]{1,0:T(8,128)(2,1)S(1)}, bf16[32,2560]{1,0:T(8,128)(2,1)S(1)}, u32[]{:S(2)}, u32[]{:S(2)}) collective-permute-start(bf16[32,2560]{1,0:T(8,128)(2,1)S(1)} %get-tuple-element.277), channel_id=1, source_target_pairs={{0,224},{32,0},{64,32},{96,64},{128,96},{160,128},{192,160},{224,1... | collective-permute-start | bytes 491528 | tf_op jit(solution)/shard_map/ppermute | solution.py:319
  168.3 5.2 collective-permute-start.10
  193.4 5.8 %collective-permute-start.12 = (bf16[32,2560]{1,0:T(8,128)(2,1)S(1)}, bf16[32,2560]{1,0:T(8,128)(2,1)S(1)}, u32[]{:S(2)}, u32[]{:S(2)}) collective-permute-start(bf16[32,2560]{1,0:T(8,128)(2,1)S(1)} %get-tuple-element.275), channel_id=1, source_target_pairs={{0,224},{32,0},{64,32},{96,64},{128,96},{160,128},{192,160},{224,1... | collective-permute-start | bytes 491528 | tf_op jit(solution)/shard_map/ppermute | solution.py:319
  238.5 5.8 %collective-permute-start.15 = (bf16[32,2560]{1,0:T(8,128)(2,1)S(1)}, bf16[32,2560]{1,0:T(8,128)(2,1)S(1)}, u32[]{:S(2)}, u32[]{:S(2)}) collective-permute-start(bf16[32,2560]{1,0:T(8,128)(2,1)S(1)} %get-tuple-element.273), channel_id=1, source_target_pairs={{0,224},{32,0},{64,32},{96,64},{128,96},{160,128},{192,160},{224,1... | collective-permute-start | bytes 491528 | tf_op jit(solution)/shard_map/ppermute | solution.py:319
  258.7 5.0 collective-permute-start.16
  284.0 5.8 %collective-permute-start.18 = (bf16[32,2560]{1,0:T(8,128)(2,1)S(1)}, bf16[32,2560]{1,0:T(8,128)(2,1)S(1)}, u32[]{:S(2)}, u32[]{:S(2)}) collective-permute-start(bf16[32,2560]{1,0:T(8,128)(2,1)S(1)} %get-tuple-element.271), channel_id=1, source_target_pairs={{0,224},{32,0},{64,32},{96,64},{128,96},{160,128},{192,160},{224,1... | collective-permute-start | bytes 491528 | tf_op jit(solution)/shard_map/ppermute | solution.py:319
  313.8 16.7 %all-to-all-start.12 = ((bf16[16,8,2560]{2,1,0:T(8,128)(2,1)}), bf16[16,8,2560]{2,1,0:T(8,128)(2,1)}, u32[]{:S(2)}, u32[]{:S(2)}) async-start(bf16[16,8,2560]{2,1,0:T(8,128)(2,1)} %fusion.73), calls=%async_computation.12 | async-start | bytes 1310720 | tf_op jit(solution)/shard_map/all_to_all | solution.py:188
  332.7 5.8 %collective-permute-start.21 = (bf16[32,2560]{1,0:T(8,128)(2,1)S(1)}, bf16[32,2560]{1,0:T(8,128)(2,1)S(1)}, u32[]{:S(2)}, u32[]{:S(2)}) collective-permute-start(bf16[32,2560]{1,0:T(8,128)(2,1)S(1)} %get-tuple-element.269), channel_id=1, source_target_pairs={{0,224},{32,0},{64,32},{96,64},{128,96},{160,128},{192,160},{224,1... | collective-permute-start | bytes 491528 | tf_op jit(solution)/shard_map/ppermute | solution.py:319
  378.9 5.8 %collective-permute-start.24 = (bf16[32,2560]{1,0:T(8,128)(2,1)S(1)}, bf16[32,2560]{1,0:T(8,128)(2,1)S(1)}, u32[]{:S(2)}, u32[]{:S(2)}) collective-permute-start(bf16[32,2560]{1,0:T(8,128)(2,1)S(1)} %get-tuple-element.267), channel_id=1, source_target_pairs={{0,224},{32,0},{64,32},{96,64},{128,96},{160,128},{192,160},{224,1... | collective-permute-start | bytes 491528 | tf_op jit(solution)/shard_map/ppermute | solution.py:319
  423.6 5.8 %collective-permute-start.27 = (bf16[32,2560]{1,0:T(8,128)(2,1)S(1)}, bf16[32,2560]{1,0:T(8,128)(2,1)S(1)}, u32[]{:S(2)}, u32[]{:S(2)}) collective-permute-start(bf16[32,2560]{1,0:T(8,128)(2,1)S(1)} %get-tuple-element.265), channel_id=1, source_target_pairs={{0,224},{32,0},{64,32},{96,64},{128,96},{160,128},{192,160},{224,1... | collective-permute-start | bytes 491528 | tf_op jit(solution)/shard_map/ppermute | solution.py:319
  468.6 5.8 %collective-permute-start.30 = (bf16[32,2560]{1,0:T(8,128)(2,1)S(1)}, bf16[32,2560]{1,0:T(8,128)(2,1)S(1)}, u32[]{:S(2)}, u32[]{:S(2)}) collective-permute-start(bf16[32,2560]{1,0:T(8,128)(2,1)S(1)} %get-tuple-element.263), channel_id=1, source_target_pairs={{0,224},{32,0},{64,32},{96,64},{128,96},{160,128},{192,160},{224,1... | collective-permute-start | bytes 491528 | tf_op jit(solution)/shard_map/ppermute | solution.py:319
  488.6 5.2 collective-permute-start.31
  513.7 5.8 %collective-permute-start.33 = (bf16[32,2560]{1,0:T(8,128)(2,1)S(1)}, bf16[32,2560]{1,0:T(8,128)(2,1)S(1)}, u32[]{:S(2)}, u32[]{:S(2)}) collective-permute-start(bf16[32,2560]{1,0:T(8,128)(2,1)S(1)} %get-tuple-element.261), channel_id=1, source_target_pairs={{0,224},{32,0},{64,32},{96,64},{128,96},{160,128},{192,160},{224,1... | collective-permute-start | bytes 491528 | tf_op jit(solution)/shard_map/ppermute | solution.py:319
  533.7 5.0 collective-permute-start.34
  544.3 16.8 %all-to-all-start.22 = ((bf16[16,8,2560]{2,1,0:T(8,128)(2,1)}), bf16[16,8,2560]{2,1,0:T(8,128)(2,1)S(1)}, u32[]{:S(2)}, u32[]{:S(2)}) async-start(bf16[16,8,2560]{2,1,0:T(8,128)(2,1)} %bitcast.82), calls=%async_computation.22 | async-start | bytes 1310720 | tf_op jit(solution)/shard_map/all_to_all | solution.py:188
  (117 other events, 899.6 us)

commit v7 on v6

--- a/solution.py
+++ b/solution.py
@@ -57,7 +57,8 @@
     ticks = sections + groups - 1
     kept = [refs[4 * t : 4 * t + 4] for t in range(ticks)]
     x_halves, act_halves = refs[4 * ticks : 4 * ticks + 2], refs[4 * ticks + 2 : 4 * ticks + 4]
-    outs = refs[4 * ticks + 4 : 4 * ticks + 7]
+    kept_out, results = refs[4 * ticks + 4 : 5 * ticks + 3], refs[5 * ticks + 3]
+    outs = refs[5 * ticks + 4 : 5 * ticks + 7]
     d_buf, act_buf, rows_buf, x_buf, sems = refs[-5:]
     chunk = rows_buf.shape[-1]
     hidden = act_buf.shape[-1]
@@ -100,24 +101,31 @@
             for g, h in pairs
         ]
 
+    def result_copies(first):
+        at = len(pairs) + SPLIT + CHUNKS * (SPLIT + len(pairs))
+        block = kept_out[0].shape[0]
+        return [
+            pltpu.make_async_copy(
+                kept_out[min(first + g, ticks - 2)],
+                results.at[pl.ds(g * block, block)],
+                sems.at[at + g],
+            )
+            for g in range(groups)
+        ]
+
     @pl.when(step == 0)
     def start():
-        for copy in x_copies(0) + act_copies():
-            copy.start()
         for first in range(sections):
 
             @pl.when(first_ref[0] == first)
             def start_kept():
-                copies = d_copies(first)
-                for c in range(CHUNKS):
-                    copies = copies + row_copies(c, first)
-                for copy in copies:
+                copies = d_copies(first) + x_copies(0) + act_copies() + row_copies(0, first)
+                for c in range(1, CHUNKS):
+                    copies = copies + x_copies(c) + row_copies(c, first)
+                for copy in copies + result_copies(first):
                     copy.start()
 
-        for c in range(1, CHUNKS):
-            for copy in x_copies(c):
-                copy.start()
-        for copy in d_copies(0) + act_copies():
+        for copy in d_copies(0):
             copy.wait()
 
     def merged(value):
@@ -127,22 +135,29 @@
 
         @pl.when(step == c)
         def compute():
-            for copy in x_copies(c) + row_copies(c, 0):
+            for copy in x_copies(c):
                 copy.wait()
             both = dot(merged(d_buf[...]), merged(x_buf[c]), ROWS_ROWS) / batches
             outs[0][...] = both[:hidden].astype(jnp.bfloat16)
             outs[1][...] = both[hidden:].astype(jnp.bfloat16)
+            for copy in row_copies(c, 0) + (act_copies() if c == 0 else []):
+                copy.wait()
             down = dot(merged(act_buf[...]), merged(rows_buf[c]), ROWS_ROWS) / batches
             outs[2][...] = down.astype(jnp.bfloat16)
-
-
-def weight_grads(first, kept, x_halves, act_halves, sections, batches):
+            if c == CHUNKS - 1:
+                for copy in result_copies(0):
+                    copy.wait()
+
+
+def weight_grads(first, kept, kept_out, x_halves, act_halves, sections, batches):
     groups, rows, width = x_halves[0].shape
     hidden = act_halves[0].shape[2]
     chunk = width // CHUNKS
     operands = [value for tick in kept for value in tick] + list(x_halves) + list(act_halves)
+    operands = operands + kept_out
     anywhere = pl.BlockSpec(memory_space=pl.ANY)
-    copies = (1 + CHUNKS) * (groups + 1) * SPLIT
+    copies = (1 + CHUNKS) * (groups + 1) * SPLIT + groups
+    results = jax.ShapeDtypeStruct((groups * kept_out[0].shape[0], width), jnp.bfloat16)
     halves = (groups, SPLIT, rows)
     work = groups * SPLIT * rows * width
     return pl.pallas_call(
@@ -151,7 +166,7 @@
             num_scalar_prefetch=1,
             grid=(CHUNKS,),
             in_specs=[anywhere] * len(operands),
-            out_specs=[pl.BlockSpec((hidden, chunk), lambda n, first: (0, n))] * 3,
+            out_specs=[anywhere] + [pl.BlockSpec((hidden, chunk), lambda n, first: (0, n))] * 3,
             scratch_shapes=[
                 pltpu.VMEM(halves + (2 * hidden,), jnp.bfloat16),
                 pltpu.VMEM(halves + (hidden,), jnp.bfloat16),
@@ -160,7 +175,7 @@
                 pltpu.SemaphoreType.DMA((copies,)),
             ],
         ),
-        out_shape=[jax.ShapeDtypeStruct((hidden, width), jnp.bfloat16)] * 3,
+        out_shape=[results] + [jax.ShapeDtypeStruct((hidden, width), jnp.bfloat16)] * 3,
         compiler_params=pltpu.CompilerParams(vmem_limit_bytes=56 * 1024 * 1024),
         cost_estimate=pl.CostEstimate(
             flops=6 * work * hidden, bytes_accessed=4 * work + 6 * hidden * width,
@@ -197,6 +212,7 @@
     placing, slot_gates, packing, unpacking = slot_tables(routes[0], gates[0], chips)
     x_tokens = x_saved[0].reshape(batches * tokens, width)
     x_out = dot(packing, x_tokens).astype(jnp.bfloat16)
+    x_out, cotangent = together(x_out, cotangent)
 
     by_group = cotangent.reshape(groups, GROUP * tokens, -1)
     blocks = []
@@ -257,7 +273,7 @@
         gate = padded_gates[jnp.where(active, group, groups)]
         if tick == 0:
             rows_out = (dot(place, arriving) * gate[:, None]).astype(jnp.bfloat16)
-            rows_out, x_packed, x_packed_other = together(rows_out, x_packed, x_packed_other)
+            rows_out, x_packed = together(rows_out, x_packed)
             came = across(rows_out)
             x_mine = unpacked(x_packed, groups)
             slopes = [forward(x_mine[:rows])[0], forward(unpacked(x_packed_other, 1))[0]]
@@ -292,9 +308,8 @@
         summed = part_mine.astype(jnp.float32) + from_other.astype(jnp.float32)
         summed = summed.astype(jnp.bfloat16)
         if tick == 0:
-            summed, x_mine, x_packed_other = together(summed, x_mine, x_packed_other)
+            summed, x_mine = together(summed, x_mine)
             slope_mine_all, act_mine = forward(x_mine)
-            x_other = unpacked(x_packed_other, groups)
         if tick == ticks - 1:
             first = sections - 1 - section_index
             summed, d_mine, d_other, rows_mine, rows_other, first = together(
@@ -303,17 +318,16 @@
         kept.append((d_mine, d_other, rows_mine, rows_other))
         returned = across(summed)
         if tick == ticks - 1:
-            grads = weight_grads(first, kept, x_halves, act_halves, sections, batches)
-            results = lax.dynamic_slice_in_dim(
-                jnp.concatenate(kept_out + [arriving]),
-                first * (GROUP * tokens),
-                batches * tokens,
-                axis=0,
+            results, *grads = weight_grads(
+                first, kept, kept_out, x_halves, act_halves, sections, batches
             )
             returned, results, grads = together(returned, results, grads)
         outgoing = (arriving.astype(jnp.float32) + dot(place, returned, ROWS_ROWS)).astype(
             jnp.bfloat16
         )
+        if tick == 0:
+            outgoing, x_packed_other = together(outgoing, x_packed_other)
+            x_other = unpacked(x_packed_other, groups)
         if tick < ticks - 1:
             kept_out.append(outgoing)
             arriving = lax.ppermute(outgoing, "section", ring)

time: 573 us -> 573 us (level)
  Pallas kernels: 11.7 us -> 23.1 us
    pallas_call x1, Pallas kernels: 11.7 us -> 23.1 us  [weight_grads(): pl.pallas_call(partial(grads_kernel, sections, batches), grid_spec=pltpu....]
  transfers between devices with their start and end apart: 42 -> 42, of which waited for: 38 -> 37; matrix products, arithmetic and copies ran while one was open for 12% -> 11% of each run, Pallas kernels for 2% -> 4%
where the time goes in v7:
time: 573 us; the launch traced here: 564 us
  blocking collectives  249 us (43%)
  starting transfers between devices  111 us (19%)
  waiting for transfers between devices  75.3 us (13%)
  matrix products  74.1 us (13%)
  Pallas kernels  23.1 us (4%)
  other arithmetic  18.8 us (3%)
  local copies, waits for them, and re-layouts  8.55 us (1%)
    all_to_all x17, blocking collectives, across(): lax.all_to_all(shaped, 'expert', 0, 0, axis_index_groups=same_core, tiled...  249 us
    dot_general x73, matrix products, dot(): lax.dot_general(left, right, dims, preferred_element_type=jnp.float32)  74.1 us
    ppermute x23, starting transfers between devices, swapped(): return lax.ppermute(value, 'expert', swap)  39.4 us
    ppermute x10, starting transfers between devices, on_device(): arriving = lax.ppermute(outgoing, 'section', ring)  35.5 us
    all_to_all x6, starting transfers between devices, across(): lax.all_to_all(shaped, 'expert', 0, 0, axis_index_groups=same_core, tiled...  28.9 us
    all_to_all x6, waiting for transfers between devices, across(): lax.all_to_all(shaped, 'expert', 0, 0, axis_index_groups=same_core, tiled...  25.1 us
    pallas_call x1, Pallas kernels, weight_grads(): pl.pallas_call(partial(grads_kernel, sections, batches), grid_spec=pltpu....  23.1 us
    ppermute x10, waiting for transfers between devices, on_device(): arriving = lax.ppermute(outgoing, 'section', ring)  20.4 us
  transfers between devices with their start and end apart: 42, of which 37 were waited for; matrix products, arithmetic and copies ran while one was open for 11% of the time, Pallas kernels for 4%

profile of v7, /device:TPU:1, one launch (start us, length us, event | category | flops | bytes accessed | tf_op | source)
XLA Modules:
  0.0 563.6 jit_solution(15230326320863488964)
XLA Ops:
  6.1 7.8 %all-to-all-start = ((bf16[16,24,2560]{2,1,0:T(8,128)(2,1)}), bf16[16,24,2560]{2,1,0:T(8,128)(2,1)}, u32[]{:S(2)}, u32[]{:S(2)}) async-start(bf16[16,24,2560]{2,1,0:T(8,128)(2,1)} %bitcast.405), calls=%async_computation | async-start | bytes 3932160 | tf_op jit(solution)/shard_map/all_to_all | solution.py:203
  24.4 5.5 collective-permute-done.1
  55.1 5.2 fusion.65
  91.4 5.7 %collective-permute-start.6 = (bf16[32,2560]{1,0:T(8,128)(2,1)S(1)}, bf16[32,2560]{1,0:T(8,128)(2,1)S(1)}, u32[]{:S(2)}, u32[]{:S(2)}) collective-permute-start(bf16[32,2560]{1,0:T(8,128)(2,1)S(1)} %fusion.20.refs_48_), channel_id=1, source_target_pairs={{0,224},{32,0},{64,32},{96,64},{128,96},{160,128},{192,160},{224,1... | collective-permute-start | bytes 491528 | tf_op jit(solution)/shard_map/ppermute | solution.py:333
  108.0 5.1 fusion.208
  129.3 16.2 %all_to_all.115 = bf16[16,8,2560]{2,1,0:T(8,128)(2,1)S(1)} all-to-all(bf16[16,8,2560]{2,1,0:T(8,128)(2,1)S(1)} %fusion.69), channel_id=1, replica_groups={{0,2,4,6,8,10,12,14,16,18,20,22,24,26,28,30},{1,3,5,7,9,11,13,15,17,19,..., dimensions={0} | all-to-all | bytes 1310720 | tf_op jit(solution)/shard_map/all_to_all | solution.py:203
  150.3 14.3 %all_to_all.116 = bf16[16,8,2560]{2,1,0:T(8,128)(2,1)S(1)} all-to-all(bf16[16,8,2560]{2,1,0:T(8,128)(2,1)S(1)} %fusion.19), channel_id=1, replica_groups={{0,2,4,6,8,10,12,14,16,18,20,22,24,26,28,30},{1,3,5,7,9,11,13,15,17,19,..., dimensions={0} | all-to-all | bytes 1310720 | tf_op jit(solution)/shard_map/all_to_all | solution.py:203
  173.5 15.2 %all_to_all.117 = bf16[16,8,2560]{2,1,0:T(8,128)(2,1)S(1)} all-to-all(bf16[16,8,2560]{2,1,0:T(8,128)(2,1)S(1)} %fusion.70), channel_id=1, replica_groups={{0,2,4,6,8,10,12,14,16,18,20,22,24,26,28,30},{1,3,5,7,9,11,13,15,17,19,..., dimensions={0} | all-to-all | bytes 1310720 | tf_op jit(solution)/shard_map/all_to_all | solution.py:203
  194.4 14.0 %all_to_all.118 = bf16[16,8,2560]{2,1,0:T(8,128)(2,1)S(1)} all-to-all(bf16[16,8,2560]{2,1,0:T(8,128)(2,1)S(1)} %fusion.18), channel_id=1, replica_groups={{0,2,4,6,8,10,12,14,16,18,20,22,24,26,28,30},{1,3,5,7,9,11,13,15,17,19,..., dimensions={0} | all-to-all | bytes 1310720 | tf_op jit(solution)/shard_map/all_to_all | solution.py:203
  217.2 15.2 %all_to_all.119 = bf16[16,8,2560]{2,1,0:T(8,128)(2,1)S(1)} all-to-all(bf16[16,8,2560]{2,1,0:T(8,128)(2,1)S(1)} %fusion.71), channel_id=1, replica_groups={{0,2,4,6,8,10,12,14,16,18,20,22,24,26,28,30},{1,3,5,7,9,11,13,15,17,19,..., dimensions={0} | all-to-all | bytes 1310720 | tf_op jit(solution)/shard_map/all_to_all | solution.py:203
  238.9 14.0 %all_to_all.120 = bf16[16,8,2560]{2,1,0:T(8,128)(2,1)S(1)} all-to-all(bf16[16,8,2560]{2,1,0:T(8,128)(2,1)S(1)} %fusion.17), channel_id=1, replica_groups={{0,2,4,6,8,10,12,14,16,18,20,22,24,26,28,30},{1,3,5,7,9,11,13,15,17,19,..., dimensions={0} | all-to-all | bytes 1310720 | tf_op jit(solution)/shard_map/all_to_all | solution.py:203
  262.2 15.2 %all_to_all.121 = bf16[16,8,2560]{2,1,0:T(8,128)(2,1)S(1)} all-to-all(bf16[16,8,2560]{2,1,0:T(8,128)(2,1)S(1)} %fusion.72), channel_id=1, replica_groups={{0,2,4,6,8,10,12,14,16,18,20,22,24,26,28,30},{1,3,5,7,9,11,13,15,17,19,..., dimensions={0} | all-to-all | bytes 1310720 | tf_op jit(solution)/shard_map/all_to_all | solution.py:203
  283.9 14.0 %all_to_all.122 = bf16[16,8,2560]{2,1,0:T(8,128)(2,1)S(1)} all-to-all(bf16[16,8,2560]{2,1,0:T(8,128)(2,1)S(1)} %fusion.16), channel_id=1, replica_groups={{0,2,4,6,8,10,12,14,16,18,20,22,24,26,28,30},{1,3,5,7,9,11,13,15,17,19,..., dimensions={0} | all-to-all | bytes 1310720 | tf_op jit(solution)/shard_map/all_to_all | solution.py:203
  311.8 12.4 %all-to-all-done.12 = bf16[16,8,2560]{2,1,0:T(8,128)(2,1)} async-done(((bf16[16,8,2560]{2,1,0:T(8,128)(2,1)}), bf16[16,8,2560]{2,1,0:T(8,128)(2,1)}, u32[]{:S(2)}, u32[]{:S(2)}) %all-to-all-start.12) | async-done | bytes 655392 | tf_op jit(solution)/shard_map/all_to_all | solution.py:203
  332.0 14.5 %all_to_all.123 = bf16[16,8,2560]{2,1,0:T(8,128)(2,1)S(1)} all-to-all(bf16[16,8,2560]{2,1,0:T(8,128)(2,1)S(1)} %fusion.15), channel_id=1, replica_groups={{0,2,4,6,8,10,12,14,16,18,20,22,24,26,28,30},{1,3,5,7,9,11,13,15,17,19,..., dimensions={0} | all-to-all | bytes 1310720 | tf_op jit(solution)/shard_map/all_to_all | solution.py:203
  355.7 15.4 %all_to_all.124 = bf16[16,8,2560]{2,1,0:T(8,128)(2,1)S(1)} all-to-all(bf16[16,8,2560]{2,1,0:T(8,128)(2,1)S(1)} %fusion.74), channel_id=1, replica_groups={{0,2,4,6,8,10,12,14,16,18,20,22,24,26,28,30},{1,3,5,7,9,11,13,15,17,19,..., dimensions={0} | all-to-all | bytes 1310720 | tf_op jit(solution)/shard_map/all_to_all | solution.py:203
  377.6 13.6 %all_to_all.125 = bf16[16,8,2560]{2,1,0:T(8,128)(2,1)S(1)} all-to-all(bf16[16,8,2560]{2,1,0:T(8,128)(2,1)S(1)} %fusion.14), channel_id=1, replica_groups={{0,2,4,6,8,10,12,14,16,18,20,22,24,26,28,30},{1,3,5,7,9,11,13,15,17,19,..., dimensions={0} | all-to-all | bytes 1310720 | tf_op jit(solution)/shard_map/all_to_all | solution.py:203
  400.1 15.2 %all_to_all.126 = bf16[16,8,2560]{2,1,0:T(8,128)(2,1)S(1)} all-to-all(bf16[16,8,2560]{2,1,0:T(8,128)(2,1)S(1)} %fusion.75), channel_id=1, replica_groups={{0,2,4,6,8,10,12,14,16,18,20,22,24,26,28,30},{1,3,5,7,9,11,13,15,17,19,..., dimensions={0} | all-to-all | bytes 1310720 | tf_op jit(solution)/shard_map/all_to_all | solution.py:203
  421.8 13.8 %all_to_all.127 = bf16[16,8,2560]{2,1,0:T(8,128)(2,1)S(1)} all-to-all(bf16[16,8,2560]{2,1,0:T(8,128)(2,1)S(1)} %fusion.13), channel_id=1, replica_groups={{0,2,4,6,8,10,12,14,16,18,20,22,24,26,28,30},{1,3,5,7,9,11,13,15,17,19,..., dimensions={0} | all-to-all | bytes 1310720 | tf_op jit(solution)/shard_map/all_to_all | solution.py:203
  444.4 15.2 %all_to_all.128 = bf16[16,8,2560]{2,1,0:T(8,128)(2,1)S(1)} all-to-all(bf16[16,8,2560]{2,1,0:T(8,128)(2,1)S(1)} %fusion.76), channel_id=1, replica_groups={{0,2,4,6,8,10,12,14,16,18,20,22,24,26,28,30},{1,3,5,7,9,11,13,15,17,19,..., dimensions={0} | all-to-all | bytes 1310720 | tf_op jit(solution)/shard_map/all_to_all | solution.py:203
  466.1 13.8 %all_to_all.129 = bf16[16,8,2560]{2,1,0:T(8,128)(2,1)S(1)} all-to-all(bf16[16,8,2560]{2,1,0:T(8,128)(2,1)S(1)} %fusion.12), channel_id=1, replica_groups={{0,2,4,6,8,10,12,14,16,18,20,22,24,26,28,30},{1,3,5,7,9,11,13,15,17,19,..., dimensions={0} | all-to-all | bytes 1310720 | tf_op jit(solution)/shard_map/all_to_all | solution.py:203
  489.0 15.2 %all_to_all.130 = bf16[16,8,2560]{2,1,0:T(8,128)(2,1)S(1)} all-to-all(bf16[16,8,2560]{2,1,0:T(8,128)(2,1)S(1)} %fusion.77), channel_id=1, replica_groups={{0,2,4,6,8,10,12,14,16,18,20,22,24,26,28,30},{1,3,5,7,9,11,13,15,17,19,..., dimensions={0} | all-to-all | bytes 1310720 | tf_op jit(solution)/shard_map/all_to_all | solution.py:203
  510.7 14.0 %all_to_all.131 = bf16[16,8,2560]{2,1,0:T(8,128)(2,1)S(1)} all-to-all(bf16[16,8,2560]{2,1,0:T(8,128)(2,1)S(1)} %fusion.11), channel_id=1, replica_groups={{0,2,4,6,8,10,12,14,16,18,20,22,24,26,28,30},{1,3,5,7,9,11,13,15,17,19,..., dimensions={0} | all-to-all | bytes 1310720 | tf_op jit(solution)/shard_map/all_to_all | solution.py:203
  538.2 23.1 %shard_map.102 = (bf16[128,2560]{1,0:T(8,128)(2,1)}, bf16[384,2560]{1,0:T(8,128)(2,1)}, bf16[384,2560]{1,0:T(8,128)(2,1)}, bf16[384,2560]{1,0:T(8,128)(2,1)}) custom-call(s32[1]{0:T(128)} %bitcast.84.first_ref, bf16[128,768]{1,0:T(8,128)(2,1)} %copy-done.32, bf16[128,768]{1,0:T(8,128)(2,1)} %copy-done.33, bf16[128,2560]{1,0:T(8,128)(2,1)} %bitcast.408, ...), custom_call_target="tpu_custom_call" | custom-call | flops 6039797760 | bytes 16384000 | tf_op jit(solution)/shard_map/pallas_call | solution.py:163
  (456 shorter events, 246.6 us)
Async XLA Ops:
  6.1 36.5 %all-to-all-start = ((bf16[16,24,2560]{2,1,0:T(8,128)(2,1)}), bf16[16,24,2560]{2,1,0:T(8,128)(2,1)}, u32[]{:S(2)}, u32[]{:S(2)}) async-start(bf16[16,24,2560]{2,1,0:T(8,128)(2,1)} %bitcast.405), calls=%async_computation | async-start | bytes 3932160 | tf_op jit(solution)/shard_map/all_to_all | solution.py:203
  14.1 8.1 %collective-permute-start = (bf16[128,320]{1,0:T(8,128)(2,1)S(1)}, bf16[128,320]{1,0:T(8,128)(2,1)S(1)}, u32[]{:S(2)}, u32[]{:S(2)}) collective-permute-start(bf16[128,320]{1,0:T(8,128)(2,1)S(1)} %pad_maximum_fusion.3), channel_id=1, source_target_pairs={{0,32},{32,64},{64,96},{96,128},{128,160},{160,192},{192,224},{224... | collective-permute-start | bytes 245768 | tf_op jit(solution)/shard_map/ppermute | solution.py:229
  22.1 7.8 %collective-permute-start.1 = (bf16[128,320]{1,0:T(8,128)(2,1)S(1)}, bf16[128,320]{1,0:T(8,128)(2,1)S(1)}, u32[]{:S(2)}, u32[]{:S(2)}) collective-permute-start(bf16[128,320]{1,0:T(8,128)(2,1)S(1)} %pad_maximum_fusion.4), channel_id=1, source_target_pairs={{0,64},{32,96},{64,128},{96,160},{128,192},{160,224},{192,0},{224,... | collective-permute-start | bytes 245768 | tf_op jit(solution)/shard_map/ppermute | solution.py:229
  29.9 7.5 %collective-permute-start.2 = (bf16[128,320]{1,0:T(8,128)(2,1)S(1)}, bf16[128,320]{1,0:T(8,128)(2,1)S(1)}, u32[]{:S(2)}, u32[]{:S(2)}) collective-permute-start(bf16[128,320]{1,0:T(8,128)(2,1)S(1)} %pad_maximum_fusion.5), channel_id=1, source_target_pairs={{0,128},{32,160},{64,192},{96,224},{128,0},{160,32},{192,64},{224,... | collective-permute-start | bytes 245768 | tf_op jit(solution)/shard_map/ppermute | solution.py:229
  42.6 12.5 %collective-permute-start.3 = (bf16[384,2560]{1,0:T(8,128)(2,1)}, bf16[384,2560]{1,0:T(8,128)(2,1)}, u32[]{:S(2)}, u32[]{:S(2)}) collective-permute-start(bf16[384,2560]{1,0:T(8,128)(2,1)} %bitcast.3), channel_id=1, source_target_pairs={{0,1},{1,0},{2,3},{3,2},{4,5},{5,4},{6,7},{7,6},{8,9},{9,8},{10,11... | collective-permute-start | bytes 5898248 | tf_op jit(solution)/shard_map/ppermute | solution.py:207
  46.5 16.8 %all-to-all-start.1 = ((bf16[16,8,2560]{2,1,0:T(8,128)(2,1)}), bf16[16,8,2560]{2,1,0:T(8,128)(2,1)S(1)}, u32[]{:S(2)}, u32[]{:S(2)}) async-start(bf16[16,8,2560]{2,1,0:T(8,128)(2,1)} %bitcast.430), calls=%async_computation.1 | async-start | bytes 1310720 | tf_op jit(solution)/shard_map/all_to_all | solution.py:203
  72.6 17.4 %all-to-all-start.2 = ((bf16[16,8,2560]{2,1,0:T(8,128)(2,1)}), bf16[16,8,2560]{2,1,0:T(8,128)(2,1)}, u32[]{:S(2)}, u32[]{:S(2)}) async-start(bf16[16,8,2560]{2,1,0:T(8,128)(2,1)} %bitcast.22), calls=%async_computation.2 | async-start | bytes 1310720 | tf_op jit(solution)/shard_map/all_to_all | solution.py:203
  91.4 10.4 %collective-permute-start.6 = (bf16[32,2560]{1,0:T(8,128)(2,1)S(1)}, bf16[32,2560]{1,0:T(8,128)(2,1)S(1)}, u32[]{:S(2)}, u32[]{:S(2)}) collective-permute-start(bf16[32,2560]{1,0:T(8,128)(2,1)S(1)} %fusion.20.refs_48_), channel_id=1, source_target_pairs={{0,224},{32,0},{64,32},{96,64},{128,96},{160,128},{192,160},{224,1... | collective-permute-start | bytes 491528 | tf_op jit(solution)/shard_map/ppermute | solution.py:333
  103.7 15.4 %all-to-all-start.3 = ((bf16[16,8,2560]{2,1,0:T(8,128)(2,1)}), bf16[16,8,2560]{2,1,0:T(8,128)(2,1)}, u32[]{:S(2)}, u32[]{:S(2)}) async-start(bf16[16,8,2560]{2,1,0:T(8,128)(2,1)} %bitcast.431), calls=%async_computation.3 | async-start | bytes 1310720 | tf_op jit(solution)/shard_map/all_to_all | solution.py:203
  164.6 5.1 collective-permute-start.10
  189.0 5.1 collective-permute-start.12
  232.7 5.9 %collective-permute-start.15 = (bf16[32,2560]{1,0:T(8,128)(2,1)S(1)}, bf16[32,2560]{1,0:T(8,128)(2,1)S(1)}, u32[]{:S(2)}, u32[]{:S(2)}) collective-permute-start(bf16[32,2560]{1,0:T(8,128)(2,1)S(1)} %add_convert_fusion.18.refs_51_), channel_id=1, source_target_pairs={{0,224},{32,0},{64,32},{96,64},{128,96},{160,128},{192,160},{224,1... | collective-permute-start | bytes 491528 | tf_op jit(solution)/shard_map/ppermute | solution.py:333
  277.6 5.9 %collective-permute-start.18 = (bf16[32,2560]{1,0:T(8,128)(2,1)S(1)}, bf16[32,2560]{1,0:T(8,128)(2,1)S(1)}, u32[]{:S(2)}, u32[]{:S(2)}) collective-permute-start(bf16[32,2560]{1,0:T(8,128)(2,1)S(1)} %add_convert_fusion.17.refs_52_), channel_id=1, source_target_pairs={{0,224},{32,0},{64,32},{96,64},{128,96},{160,128},{192,160},{224,1... | collective-permute-start | bytes 491528 | tf_op jit(solution)/shard_map/ppermute | solution.py:333
  297.8 5.0 collective-permute-start.19
  307.5 16.7 %all-to-all-start.12 = ((bf16[16,8,2560]{2,1,0:T(8,128)(2,1)}), bf16[16,8,2560]{2,1,0:T(8,128)(2,1)}, u32[]{:S(2)}, u32[]{:S(2)}) async-start(bf16[16,8,2560]{2,1,0:T(8,128)(2,1)} %fusion.73), calls=%async_computation.12 | async-start | bytes 1310720 | tf_op jit(solution)/shard_map/all_to_all | solution.py:203
  325.7 5.9 %collective-permute-start.21 = (bf16[32,2560]{1,0:T(8,128)(2,1)S(1)}, bf16[32,2560]{1,0:T(8,128)(2,1)S(1)}, u32[]{:S(2)}, u32[]{:S(2)}) collective-permute-start(bf16[32,2560]{1,0:T(8,128)(2,1)S(1)} %add_convert_fusion.16.refs_53_), channel_id=1, source_target_pairs={{0,224},{32,0},{64,32},{96,64},{128,96},{160,128},{192,160},{224,1... | collective-permute-start | bytes 491528 | tf_op jit(solution)/shard_map/ppermute | solution.py:333
  371.4 5.9 %collective-permute-start.24 = (bf16[32,2560]{1,0:T(8,128)(2,1)S(1)}, bf16[32,2560]{1,0:T(8,128)(2,1)S(1)}, u32[]{:S(2)}, u32[]{:S(2)}) collective-permute-start(bf16[32,2560]{1,0:T(8,128)(2,1)S(1)} %add_convert_fusion.15.refs_54_), channel_id=1, source_target_pairs={{0,224},{32,0},{64,32},{96,64},{128,96},{160,128},{192,160},{224,1... | collective-permute-start | bytes 491528 | tf_op jit(solution)/shard_map/ppermute | solution.py:333
  415.5 5.9 %collective-permute-start.27 = (bf16[32,2560]{1,0:T(8,128)(2,1)S(1)}, bf16[32,2560]{1,0:T(8,128)(2,1)S(1)}, u32[]{:S(2)}, u32[]{:S(2)}) collective-permute-start(bf16[32,2560]{1,0:T(8,128)(2,1)S(1)} %add_convert_fusion.14.refs_55_), channel_id=1, source_target_pairs={{0,224},{32,0},{64,32},{96,64},{128,96},{160,128},{192,160},{224,1... | collective-permute-start | bytes 491528 | tf_op jit(solution)/shard_map/ppermute | solution.py:333
  435.6 5.0 collective-permute-start.28
  459.9 5.9 %collective-permute-start.30 = (bf16[32,2560]{1,0:T(8,128)(2,1)S(1)}, bf16[32,2560]{1,0:T(8,128)(2,1)S(1)}, u32[]{:S(2)}, u32[]{:S(2)}) collective-permute-start(bf16[32,2560]{1,0:T(8,128)(2,1)S(1)} %add_convert_fusion.13.refs_56_), channel_id=1, source_target_pairs={{0,224},{32,0},{64,32},{96,64},{128,96},{160,128},{192,160},{224,1... | collective-permute-start | bytes 491528 | tf_op jit(solution)/shard_map/ppermute | solution.py:333
  480.0 5.2 collective-permute-start.31
  504.4 5.9 %collective-permute-start.33 = (bf16[32,2560]{1,0:T(8,128)(2,1)S(1)}, bf16[32,2560]{1,0:T(8,128)(2,1)S(1)}, u32[]{:S(2)}, u32[]{:S(2)}) collective-permute-start(bf16[32,2560]{1,0:T(8,128)(2,1)S(1)} %add_convert_fusion.12.refs_57_), channel_id=1, source_target_pairs={{0,224},{32,0},{64,32},{96,64},{128,96},{160,128},{192,160},{224,1... | collective-permute-start | bytes 491528 | tf_op jit(solution)/shard_map/ppermute | solution.py:333
  524.7 5.0 collective-permute-start.34
  534.4 27.0 %all-to-all-start.22 = ((bf16[16,8,2560]{2,1,0:T(8,128)(2,1)}), bf16[16,8,2560]{2,1,0:T(8,128)(2,1)S(1)}, u32[]{:S(2)}, u32[]{:S(2)}) async-start(bf16[16,8,2560]{2,1,0:T(8,128)(2,1)} %bitcast.82), calls=%async_computation.22 | async-start | bytes 1310720 | tf_op jit(solution)/shard_map/all_to_all | solution.py:203
  (123 other events, 999.7 us)

commit v8 on v7

--- a/solution.py
+++ b/solution.py
@@ -166,7 +166,8 @@
             num_scalar_prefetch=1,
             grid=(CHUNKS,),
             in_specs=[anywhere] * len(operands),
-            out_specs=[anywhere] + [pl.BlockSpec((hidden, chunk), lambda n, first: (0, n))] * 3,
+            out_specs=[pl.BlockSpec(results.shape, lambda n, first: (0, 0))]
+            + [pl.BlockSpec((hidden, chunk), lambda n, first: (0, n))] * 3,
             scratch_shapes=[
                 pltpu.VMEM(halves + (2 * hidden,), jnp.bfloat16),
                 pltpu.VMEM(halves + (hidden,), jnp.bfloat16),
@@ -276,7 +277,8 @@
             rows_out, x_packed = together(rows_out, x_packed)
             came = across(rows_out)
             x_mine = unpacked(x_packed, groups)
-            slopes = [forward(x_mine[:rows])[0], forward(unpacked(x_packed_other, 1))[0]]
+            (x_first,) = together(unpacked(x_packed_other, 1))
+            slopes = [forward(x_mine[:rows])[0], forward(x_first)[0]]
             rows_mine, slopes, x_mine = together(came, slopes, x_mine)
         elif tick == 1:
             slope_mine = sliced(slope_mine_all, tick)

time: 573 us -> 562 us (0.981)
  Pallas kernels: 23.1 us -> 12.3 us
    pallas_call x1, Pallas kernels: 23.1 us -> 12.3 us  [weight_grads(): pl.pallas_call(partial(grads_kernel, sections, batches), grid_spec=pltpu....]
    dot_general x73 -> x74, matrix products: 74.1 us -> 72.3 us  [dot(): lax.dot_general(left, right, dims, preferred_element_type=jnp.float32)]
  transfers between devices with their start and end apart: 42 -> 42, of which waited for: 37 -> 37; matrix products, arithmetic and copies ran while one was open for 11% -> 10% of each run, Pallas kernels for 4% -> 2%
where the time goes in v8:
time: 562 us; the launch traced here: 552 us
  blocking collectives  249 us (44%)
  starting transfers between devices  111 us (20%)
  waiting for transfers between devices  78.3 us (14%)
  matrix products  72.3 us (13%)
  other arithmetic  17.8 us (3%)
  Pallas kernels  12.3 us (2%)
  local copies, waits for them, and re-layouts  8.55 us (2%)
    all_to_all x17, blocking collectives, across(): lax.all_to_all(shaped, 'expert', 0, 0, axis_index_groups=same_core, tiled...  249 us
    dot_general x74, matrix products, dot(): lax.dot_general(left, right, dims, preferred_element_type=jnp.float32)  72.3 us
    ppermute x23, starting transfers between devices, swapped(): return lax.ppermute(value, 'expert', swap)  39.3 us
    ppermute x10, starting transfers between devices, on_device(): arriving = lax.ppermute(outgoing, 'section', ring)  35.5 us
    all_to_all x6, starting transfers between devices, across(): lax.all_to_all(shaped, 'expert', 0, 0, axis_index_groups=same_core, tiled...  28.2 us
    all_to_all x6, waiting for transfers between devices, across(): lax.all_to_all(shaped, 'expert', 0, 0, axis_index_groups=same_core, tiled...  28.1 us
    ppermute x10, waiting for transfers between devices, on_device(): arriving = lax.ppermute(outgoing, 'section', ring)  20.4 us
    ppermute x23, waiting for transfers between devices, swapped(): return lax.ppermute(value, 'expert', swap)  20.1 us
  transfers between devices with their start and end apart: 42, of which 37 were waited for; matrix products, arithmetic and copies ran while one was open for 10% of the time, Pallas kernels for 2%

profile of v8, /device:TPU:1, one launch (start us, length us, event | category | flops | bytes accessed | tf_op | source)
XLA Modules:
  0.0 552.1 jit_solution(4470524221145197035)
XLA Ops:
  6.1 7.8 %all-to-all-start = ((bf16[16,24,2560]{2,1,0:T(8,128)(2,1)}), bf16[16,24,2560]{2,1,0:T(8,128)(2,1)}, u32[]{:S(2)}, u32[]{:S(2)}) async-start(bf16[16,24,2560]{2,1,0:T(8,128)(2,1)} %bitcast.405), calls=%async_computation | async-start | bytes 3932160 | tf_op jit(solution)/shard_map/all_to_all | solution.py:204
  24.4 5.5 collective-permute-done.1
  77.1 5.1 fusion.205
  90.8 5.7 %collective-permute-start.6 = (bf16[32,2560]{1,0:T(8,128)(2,1)S(1)}, bf16[32,2560]{1,0:T(8,128)(2,1)S(1)}, u32[]{:S(2)}, u32[]{:S(2)}) collective-permute-start(bf16[32,2560]{1,0:T(8,128)(2,1)S(1)} %fusion.20.refs_48_), channel_id=1, source_target_pairs={{0,224},{32,0},{64,32},{96,64},{128,96},{160,128},{192,160},{224,1... | collective-permute-start | bytes 491528 | tf_op jit(solution)/shard_map/ppermute | solution.py:335
  107.3 5.1 fusion.206
  128.6 16.1 %all_to_all.115 = bf16[16,8,2560]{2,1,0:T(8,128)(2,1)S(1)} all-to-all(bf16[16,8,2560]{2,1,0:T(8,128)(2,1)S(1)} %fusion.68), channel_id=1, replica_groups={{0,2,4,6,8,10,12,14,16,18,20,22,24,26,28,30},{1,3,5,7,9,11,13,15,17,19,..., dimensions={0} | all-to-all | bytes 1310720 | tf_op jit(solution)/shard_map/all_to_all | solution.py:204
  149.6 14.3 %all_to_all.116 = bf16[16,8,2560]{2,1,0:T(8,128)(2,1)S(1)} all-to-all(bf16[16,8,2560]{2,1,0:T(8,128)(2,1)S(1)} %fusion.19), channel_id=1, replica_groups={{0,2,4,6,8,10,12,14,16,18,20,22,24,26,28,30},{1,3,5,7,9,11,13,15,17,19,..., dimensions={0} | all-to-all | bytes 1310720 | tf_op jit(solution)/shard_map/all_to_all | solution.py:204
  172.8 15.2 %all_to_all.117 = bf16[16,8,2560]{2,1,0:T(8,128)(2,1)S(1)} all-to-all(bf16[16,8,2560]{2,1,0:T(8,128)(2,1)S(1)} %fusion.69), channel_id=1, replica_groups={{0,2,4,6,8,10,12,14,16,18,20,22,24,26,28,30},{1,3,5,7,9,11,13,15,17,19,..., dimensions={0} | all-to-all | bytes 1310720 | tf_op jit(solution)/shard_map/all_to_all | solution.py:204
  193.7 14.0 %all_to_all.118 = bf16[16,8,2560]{2,1,0:T(8,128)(2,1)S(1)} all-to-all(bf16[16,8,2560]{2,1,0:T(8,128)(2,1)S(1)} %fusion.18), channel_id=1, replica_groups={{0,2,4,6,8,10,12,14,16,18,20,22,24,26,28,30},{1,3,5,7,9,11,13,15,17,19,..., dimensions={0} | all-to-all | bytes 1310720 | tf_op jit(solution)/shard_map/all_to_all | solution.py:204
  216.5 15.2 %all_to_all.119 = bf16[16,8,2560]{2,1,0:T(8,128)(2,1)S(1)} all-to-all(bf16[16,8,2560]{2,1,0:T(8,128)(2,1)S(1)} %fusion.70), channel_id=1, replica_groups={{0,2,4,6,8,10,12,14,16,18,20,22,24,26,28,30},{1,3,5,7,9,11,13,15,17,19,..., dimensions={0} | all-to-all | bytes 1310720 | tf_op jit(solution)/shard_map/all_to_all | solution.py:204
  238.2 14.0 %all_to_all.120 = bf16[16,8,2560]{2,1,0:T(8,128)(2,1)S(1)} all-to-all(bf16[16,8,2560]{2,1,0:T(8,128)(2,1)S(1)} %fusion.17), channel_id=1, replica_groups={{0,2,4,6,8,10,12,14,16,18,20,22,24,26,28,30},{1,3,5,7,9,11,13,15,17,19,..., dimensions={0} | all-to-all | bytes 1310720 | tf_op jit(solution)/shard_map/all_to_all | solution.py:204
  261.4 15.2 %all_to_all.121 = bf16[16,8,2560]{2,1,0:T(8,128)(2,1)S(1)} all-to-all(bf16[16,8,2560]{2,1,0:T(8,128)(2,1)S(1)} %fusion.71), channel_id=1, replica_groups={{0,2,4,6,8,10,12,14,16,18,20,22,24,26,28,30},{1,3,5,7,9,11,13,15,17,19,..., dimensions={0} | all-to-all | bytes 1310720 | tf_op jit(solution)/shard_map/all_to_all | solution.py:204
  283.1 14.0 %all_to_all.122 = bf16[16,8,2560]{2,1,0:T(8,128)(2,1)S(1)} all-to-all(bf16[16,8,2560]{2,1,0:T(8,128)(2,1)S(1)} %fusion.16), channel_id=1, replica_groups={{0,2,4,6,8,10,12,14,16,18,20,22,24,26,28,30},{1,3,5,7,9,11,13,15,17,19,..., dimensions={0} | all-to-all | bytes 1310720 | tf_op jit(solution)/shard_map/all_to_all | solution.py:204
  311.1 12.4 %all-to-all-done.12 = bf16[16,8,2560]{2,1,0:T(8,128)(2,1)} async-done(((bf16[16,8,2560]{2,1,0:T(8,128)(2,1)}), bf16[16,8,2560]{2,1,0:T(8,128)(2,1)}, u32[]{:S(2)}, u32[]{:S(2)}) %all-to-all-start.12) | async-done | bytes 655392 | tf_op jit(solution)/shard_map/all_to_all | solution.py:204
  331.2 14.5 %all_to_all.123 = bf16[16,8,2560]{2,1,0:T(8,128)(2,1)S(1)} all-to-all(bf16[16,8,2560]{2,1,0:T(8,128)(2,1)S(1)} %fusion.15), channel_id=1, replica_groups={{0,2,4,6,8,10,12,14,16,18,20,22,24,26,28,30},{1,3,5,7,9,11,13,15,17,19,..., dimensions={0} | all-to-all | bytes 1310720 | tf_op jit(solution)/shard_map/all_to_all | solution.py:204
  355.0 15.4 %all_to_all.124 = bf16[16,8,2560]{2,1,0:T(8,128)(2,1)S(1)} all-to-all(bf16[16,8,2560]{2,1,0:T(8,128)(2,1)S(1)} %fusion.73), channel_id=1, replica_groups={{0,2,4,6,8,10,12,14,16,18,20,22,24,26,28,30},{1,3,5,7,9,11,13,15,17,19,..., dimensions={0} | all-to-all | bytes 1310720 | tf_op jit(solution)/shard_map/all_to_all | solution.py:204
  376.9 13.6 %all_to_all.125 = bf16[16,8,2560]{2,1,0:T(8,128)(2,1)S(1)} all-to-all(bf16[16,8,2560]{2,1,0:T(8,128)(2,1)S(1)} %fusion.14), channel_id=1, replica_groups={{0,2,4,6,8,10,12,14,16,18,20,22,24,26,28,30},{1,3,5,7,9,11,13,15,17,19,..., dimensions={0} | all-to-all | bytes 1310720 | tf_op jit(solution)/shard_map/all_to_all | solution.py:204
  399.3 15.2 %all_to_all.126 = bf16[16,8,2560]{2,1,0:T(8,128)(2,1)S(1)} all-to-all(bf16[16,8,2560]{2,1,0:T(8,128)(2,1)S(1)} %fusion.74), channel_id=1, replica_groups={{0,2,4,6,8,10,12,14,16,18,20,22,24,26,28,30},{1,3,5,7,9,11,13,15,17,19,..., dimensions={0} | all-to-all | bytes 1310720 | tf_op jit(solution)/shard_map/all_to_all | solution.py:204
  421.0 13.8 %all_to_all.127 = bf16[16,8,2560]{2,1,0:T(8,128)(2,1)S(1)} all-to-all(bf16[16,8,2560]{2,1,0:T(8,128)(2,1)S(1)} %fusion.13), channel_id=1, replica_groups={{0,2,4,6,8,10,12,14,16,18,20,22,24,26,28,30},{1,3,5,7,9,11,13,15,17,19,..., dimensions={0} | all-to-all | bytes 1310720 | tf_op jit(solution)/shard_map/all_to_all | solution.py:204
  443.7 15.2 %all_to_all.128 = bf16[16,8,2560]{2,1,0:T(8,128)(2,1)S(1)} all-to-all(bf16[16,8,2560]{2,1,0:T(8,128)(2,1)S(1)} %fusion.75), channel_id=1, replica_groups={{0,2,4,6,8,10,12,14,16,18,20,22,24,26,28,30},{1,3,5,7,9,11,13,15,17,19,..., dimensions={0} | all-to-all | bytes 1310720 | tf_op jit(solution)/shard_map/all_to_all | solution.py:204
  465.4 13.8 %all_to_all.129 = bf16[16,8,2560]{2,1,0:T(8,128)(2,1)S(1)} all-to-all(bf16[16,8,2560]{2,1,0:T(8,128)(2,1)S(1)} %fusion.12), channel_id=1, replica_groups={{0,2,4,6,8,10,12,14,16,18,20,22,24,26,28,30},{1,3,5,7,9,11,13,15,17,19,..., dimensions={0} | all-to-all | bytes 1310720 | tf_op jit(solution)/shard_map/all_to_all | solution.py:204
  488.2 15.2 %all_to_all.130 = bf16[16,8,2560]{2,1,0:T(8,128)(2,1)S(1)} all-to-all(bf16[16,8,2560]{2,1,0:T(8,128)(2,1)S(1)} %fusion.76), channel_id=1, replica_groups={{0,2,4,6,8,10,12,14,16,18,20,22,24,26,28,30},{1,3,5,7,9,11,13,15,17,19,..., dimensions={0} | all-to-all | bytes 1310720 | tf_op jit(solution)/shard_map/all_to_all | solution.py:204
  509.9 14.0 %all_to_all.131 = bf16[16,8,2560]{2,1,0:T(8,128)(2,1)S(1)} all-to-all(bf16[16,8,2560]{2,1,0:T(8,128)(2,1)S(1)} %fusion.11), channel_id=1, replica_groups={{0,2,4,6,8,10,12,14,16,18,20,22,24,26,28,30},{1,3,5,7,9,11,13,15,17,19,..., dimensions={0} | all-to-all | bytes 1310720 | tf_op jit(solution)/shard_map/all_to_all | solution.py:204
  537.5 12.3 %shard_map.102 = (bf16[128,2560]{1,0:T(8,128)(2,1)}, bf16[384,2560]{1,0:T(8,128)(2,1)}, bf16[384,2560]{1,0:T(8,128)(2,1)}, bf16[384,2560]{1,0:T(8,128)(2,1)}) custom-call(s32[1]{0:T(128)} %bitcast.84.first_ref, bf16[128,768]{1,0:T(8,128)(2,1)} %copy-done.32, bf16[128,768]{1,0:T(8,128)(2,1)} %copy-done.33, bf16[128,2560]{1,0:T(8,128)(2,1)} %bitcast.408, ...), custom_call_target="tpu_custom_call" | custom-call | flops 6039797760 | bytes 16384000 | tf_op jit(solution)/shard_map/pallas_call | solution.py:163
  (457 shorter events, 246.0 us)
Async XLA Ops:
  6.1 36.5 %all-to-all-start = ((bf16[16,24,2560]{2,1,0:T(8,128)(2,1)}), bf16[16,24,2560]{2,1,0:T(8,128)(2,1)}, u32[]{:S(2)}, u32[]{:S(2)}) async-start(bf16[16,24,2560]{2,1,0:T(8,128)(2,1)} %bitcast.405), calls=%async_computation | async-start | bytes 3932160 | tf_op jit(solution)/shard_map/all_to_all | solution.py:204
  14.1 8.1 %collective-permute-start = (bf16[128,320]{1,0:T(8,128)(2,1)S(1)}, bf16[128,320]{1,0:T(8,128)(2,1)S(1)}, u32[]{:S(2)}, u32[]{:S(2)}) collective-permute-start(bf16[128,320]{1,0:T(8,128)(2,1)S(1)} %pad_maximum_fusion.3), channel_id=1, source_target_pairs={{0,32},{32,64},{64,96},{96,128},{128,160},{160,192},{192,224},{224... | collective-permute-start | bytes 245768 | tf_op jit(solution)/shard_map/ppermute | solution.py:230
  22.1 7.8 %collective-permute-start.1 = (bf16[128,320]{1,0:T(8,128)(2,1)S(1)}, bf16[128,320]{1,0:T(8,128)(2,1)S(1)}, u32[]{:S(2)}, u32[]{:S(2)}) collective-permute-start(bf16[128,320]{1,0:T(8,128)(2,1)S(1)} %pad_maximum_fusion.4), channel_id=1, source_target_pairs={{0,64},{32,96},{64,128},{96,160},{128,192},{160,224},{192,0},{224,... | collective-permute-start | bytes 245768 | tf_op jit(solution)/shard_map/ppermute | solution.py:230
  29.9 7.5 %collective-permute-start.2 = (bf16[128,320]{1,0:T(8,128)(2,1)S(1)}, bf16[128,320]{1,0:T(8,128)(2,1)S(1)}, u32[]{:S(2)}, u32[]{:S(2)}) collective-permute-start(bf16[128,320]{1,0:T(8,128)(2,1)S(1)} %pad_maximum_fusion.5), channel_id=1, source_target_pairs={{0,128},{32,160},{64,192},{96,224},{128,0},{160,32},{192,64},{224,... | collective-permute-start | bytes 245768 | tf_op jit(solution)/shard_map/ppermute | solution.py:230
  42.6 12.5 %collective-permute-start.3 = (bf16[384,2560]{1,0:T(8,128)(2,1)}, bf16[384,2560]{1,0:T(8,128)(2,1)}, u32[]{:S(2)}, u32[]{:S(2)}) collective-permute-start(bf16[384,2560]{1,0:T(8,128)(2,1)} %bitcast.3), channel_id=1, source_target_pairs={{0,1},{1,0},{2,3},{3,2},{4,5},{5,4},{6,7},{7,6},{8,9},{9,8},{10,11... | collective-permute-start | bytes 5898248 | tf_op jit(solution)/shard_map/ppermute | solution.py:208
  46.5 16.8 %all-to-all-start.1 = ((bf16[16,8,2560]{2,1,0:T(8,128)(2,1)}), bf16[16,8,2560]{2,1,0:T(8,128)(2,1)S(1)}, u32[]{:S(2)}, u32[]{:S(2)}) async-start(bf16[16,8,2560]{2,1,0:T(8,128)(2,1)} %bitcast.430), calls=%async_computation.1 | async-start | bytes 1310720 | tf_op jit(solution)/shard_map/all_to_all | solution.py:204
  72.6 16.8 %all-to-all-start.2 = ((bf16[16,8,2560]{2,1,0:T(8,128)(2,1)}), bf16[16,8,2560]{2,1,0:T(8,128)(2,1)}, u32[]{:S(2)}, u32[]{:S(2)}) async-start(bf16[16,8,2560]{2,1,0:T(8,128)(2,1)} %bitcast.22), calls=%async_computation.2 | async-start | bytes 1310720 | tf_op jit(solution)/shard_map/all_to_all | solution.py:204
  90.8 10.4 %collective-permute-start.6 = (bf16[32,2560]{1,0:T(8,128)(2,1)S(1)}, bf16[32,2560]{1,0:T(8,128)(2,1)S(1)}, u32[]{:S(2)}, u32[]{:S(2)}) collective-permute-start(bf16[32,2560]{1,0:T(8,128)(2,1)S(1)} %fusion.20.refs_48_), channel_id=1, source_target_pairs={{0,224},{32,0},{64,32},{96,64},{128,96},{160,128},{192,160},{224,1... | collective-permute-start | bytes 491528 | tf_op jit(solution)/shard_map/ppermute | solution.py:335
  103.0 15.5 %all-to-all-start.3 = ((bf16[16,8,2560]{2,1,0:T(8,128)(2,1)}), bf16[16,8,2560]{2,1,0:T(8,128)(2,1)}, u32[]{:S(2)}, u32[]{:S(2)}) async-start(bf16[16,8,2560]{2,1,0:T(8,128)(2,1)} %bitcast.431), calls=%async_computation.3 | async-start | bytes 1310720 | tf_op jit(solution)/shard_map/all_to_all | solution.py:204
  163.9 5.1 collective-permute-start.10
  188.2 5.1 collective-permute-start.12
  231.9 5.9 %collective-permute-start.15 = (bf16[32,2560]{1,0:T(8,128)(2,1)S(1)}, bf16[32,2560]{1,0:T(8,128)(2,1)S(1)}, u32[]{:S(2)}, u32[]{:S(2)}) collective-permute-start(bf16[32,2560]{1,0:T(8,128)(2,1)S(1)} %add_convert_fusion.18.refs_51_), channel_id=1, source_target_pairs={{0,224},{32,0},{64,32},{96,64},{128,96},{160,128},{192,160},{224,1... | collective-permute-start | bytes 491528 | tf_op jit(solution)/shard_map/ppermute | solution.py:335
  276.9 5.9 %collective-permute-start.18 = (bf16[32,2560]{1,0:T(8,128)(2,1)S(1)}, bf16[32,2560]{1,0:T(8,128)(2,1)S(1)}, u32[]{:S(2)}, u32[]{:S(2)}) collective-permute-start(bf16[32,2560]{1,0:T(8,128)(2,1)S(1)} %add_convert_fusion.17.refs_52_), channel_id=1, source_target_pairs={{0,224},{32,0},{64,32},{96,64},{128,96},{160,128},{192,160},{224,1... | collective-permute-start | bytes 491528 | tf_op jit(solution)/shard_map/ppermute | solution.py:335
  297.1 5.0 collective-permute-start.19
  306.7 16.7 %all-to-all-start.12 = ((bf16[16,8,2560]{2,1,0:T(8,128)(2,1)}), bf16[16,8,2560]{2,1,0:T(8,128)(2,1)}, u32[]{:S(2)}, u32[]{:S(2)}) async-start(bf16[16,8,2560]{2,1,0:T(8,128)(2,1)} %fusion.72), calls=%async_computation.12 | async-start | bytes 1310720 | tf_op jit(solution)/shard_map/all_to_all | solution.py:204
  324.9 5.9 %collective-permute-start.21 = (bf16[32,2560]{1,0:T(8,128)(2,1)S(1)}, bf16[32,2560]{1,0:T(8,128)(2,1)S(1)}, u32[]{:S(2)}, u32[]{:S(2)}) collective-permute-start(bf16[32,2560]{1,0:T(8,128)(2,1)S(1)} %add_convert_fusion.16.refs_53_), channel_id=1, source_target_pairs={{0,224},{32,0},{64,32},{96,64},{128,96},{160,128},{192,160},{224,1... | collective-permute-start | bytes 491528 | tf_op jit(solution)/shard_map/ppermute | solution.py:335
  370.6 5.9 %collective-permute-start.24 = (bf16[32,2560]{1,0:T(8,128)(2,1)S(1)}, bf16[32,2560]{1,0:T(8,128)(2,1)S(1)}, u32[]{:S(2)}, u32[]{:S(2)}) collective-permute-start(bf16[32,2560]{1,0:T(8,128)(2,1)S(1)} %add_convert_fusion.15.refs_54_), channel_id=1, source_target_pairs={{0,224},{32,0},{64,32},{96,64},{128,96},{160,128},{192,160},{224,1... | collective-permute-start | bytes 491528 | tf_op jit(solution)/shard_map/ppermute | solution.py:335
  414.8 5.9 %collective-permute-start.27 = (bf16[32,2560]{1,0:T(8,128)(2,1)S(1)}, bf16[32,2560]{1,0:T(8,128)(2,1)S(1)}, u32[]{:S(2)}, u32[]{:S(2)}) collective-permute-start(bf16[32,2560]{1,0:T(8,128)(2,1)S(1)} %add_convert_fusion.14.refs_55_), channel_id=1, source_target_pairs={{0,224},{32,0},{64,32},{96,64},{128,96},{160,128},{192,160},{224,1... | collective-permute-start | bytes 491528 | tf_op jit(solution)/shard_map/ppermute | solution.py:335
  434.9 5.0 collective-permute-start.28
  459.1 5.9 %collective-permute-start.30 = (bf16[32,2560]{1,0:T(8,128)(2,1)S(1)}, bf16[32,2560]{1,0:T(8,128)(2,1)S(1)}, u32[]{:S(2)}, u32[]{:S(2)}) collective-permute-start(bf16[32,2560]{1,0:T(8,128)(2,1)S(1)} %add_convert_fusion.13.refs_56_), channel_id=1, source_target_pairs={{0,224},{32,0},{64,32},{96,64},{128,96},{160,128},{192,160},{224,1... | collective-permute-start | bytes 491528 | tf_op jit(solution)/shard_map/ppermute | solution.py:335
  479.2 5.2 collective-permute-start.31
  503.7 5.9 %collective-permute-start.33 = (bf16[32,2560]{1,0:T(8,128)(2,1)S(1)}, bf16[32,2560]{1,0:T(8,128)(2,1)S(1)}, u32[]{:S(2)}, u32[]{:S(2)}) collective-permute-start(bf16[32,2560]{1,0:T(8,128)(2,1)S(1)} %add_convert_fusion.12.refs_57_), channel_id=1, source_target_pairs={{0,224},{32,0},{64,32},{96,64},{128,96},{160,128},{192,160},{224,1... | collective-permute-start | bytes 491528 | tf_op jit(solution)/shard_map/ppermute | solution.py:335
  523.9 5.0 collective-permute-start.34
  533.6 16.2 %all-to-all-start.22 = ((bf16[16,8,2560]{2,1,0:T(8,128)(2,1)}), bf16[16,8,2560]{2,1,0:T(8,128)(2,1)S(1)}, u32[]{:S(2)}, u32[]{:S(2)}) async-start(bf16[16,8,2560]{2,1,0:T(8,128)(2,1)} %bitcast.82), calls=%async_computation.22 | async-start | bytes 1310720 | tf_op jit(solution)/shard_map/all_to_all | solution.py:204
  (123 other events, 988.5 us)
